TPU v7x, 32 devices: a whole 2x2x4 slice. The times are simulated.
32 devices in a mesh: mp: 2 (over core), gx: 4 (over z), gy: 4 (over y, x).
Axes of the slice: x: 2, y: 2, z: 4, core: 2. Of those that a mesh axis runs over, the one named last changes fastest.
Arguments:
- states: float32 [2, 64, 512, 512], P('mp', None, 'gx', 'gy'), may hold values from -6 to 6
- surface: float32 [2, 8, 512, 512], P('mp', None, 'gx', 'gy'), may hold values from -6 to 6
- land_mask: int32 [512, 512], P('gx', 'gy'), may hold values 0 or 1
- tile_weights: bfloat16 [2, 4, 4, 64, 128, 128], P('mp', 'gx', 'gy'), may hold values from -0.5 to 0.5
- tile_source: int32 [2, 4, 4, 64], P('mp', 'gx', 'gy'), may hold values from 0 to 127
- tile_target: int32 [2, 4, 4, 64, 1], P('mp', 'gx', 'gy'), may hold values from 0 to 15; in each aligned block of 64 rows (0 to 63, 64 to 127, ..., all dimensions but the last counted through in order) at most 8 rows name the same one
- tile_row: int32 [2, 4, 4, 64], P('mp', 'gx', 'gy'), may hold values from 0 to 127
Outputs:
- new_states: float32 [2, 64, 512, 512], P('mp', None, 'gx', 'gy')
- remapped: float32 [2, 8, 512, 512], P('mp', None, 'gx', 'gy')
Inputs may be any that keep to these rules, and one draw needn't show every extreme that they name: `tile_target`: among the tiles of one device, no destination device is named by more than 8 tiles, and some device is named by exactly 8.
All inputs are finite; a program needn't handle non-finite values. No bound on the sum of `land_mask` on one device may be relied on, other than what follows from the above.
Results may differ from a plain program's by a relative error of at most 0.0029.
Values sent between devices are 32-bit elements; how exact they have to be, the bound alone decides.
No kernel may reach another device: no remote copies, remote signals or barrier semaphores. Data moves between devices by JAX's collectives and lax.ppermute only.
A program may use at most 192 MiB of HBM per device.

v0:
```python
import jax
import jax.numpy as jnp
from jax import lax
from jax.sharding import PartitionSpec as P

CY = 128
KF = 8
CAP = 8


force_gain = 0.5


def with_halo(shard, sides, width):
    for axis, dim in sides:
        devices, length = (lax.axis_size(axis), shard.shape[dim])
        up = [(i, (i + 1) % devices) for i in range(devices - 1)]
        down = [(j, i) for i, j in up]
        last = lax.slice_in_dim(shard, length - width, length, axis=dim)
        first = lax.slice_in_dim(shard, 0, width, axis=dim)
        before = lax.ppermute(last, axis, up)
        after = lax.ppermute(first, axis, down)
        shard = jnp.concatenate([before, shard, after], axis=dim)
    return shard


def vertical_part(state):
    column = jnp.pad(state, ((1, 1), (0, 0), (0, 0)))
    return column[2:] + column[:-2] - 2.0 * state


def stencil(state, wet, horiz, vert):
    weighted = state * wet
    padded = with_halo(weighted, (("gx", 1), ("gy", 2)), 1)
    lateral = (
        padded[:, 2:, 1:-1]
        + padded[:, :-2, 1:-1]
        + padded[:, 1:-1, 2:]
        + padded[:, 1:-1, :-2]
        - 4.0 * weighted
    )
    return wet * (state + horiz * lateral + vert * vertical_part(state))


def two_steps(state, wet, horiz, vert):
    first = stencil(state, wet, horiz, vert)
    return stencil(first, wet, horiz, vert)


def local(states, surface, land_mask, tile_weights, tile_source, tile_target, tile_row):
    group = lax.axis_index("mp")
    ndev = lax.axis_size("gx") * lax.axis_size("gy")
    state = states[0]
    rows_here = state.shape[1]
    wet = jnp.where(
        group == 0, jnp.ones(land_mask.shape, jnp.float32), land_mask.astype(jnp.float32)
    )
    horiz = jnp.where(group == 0, 0.15, 0.12)
    vert = jnp.where(group == 0, 0.1, 0.15)
    src = (surface[0] * wet).astype(jnp.bfloat16)
    source = tile_source[0, 0, 0]
    target = tile_target[0, 0, 0, :, 0]
    dest_row = tile_row[0, 0, 0]
    picked = jnp.take(src, source, axis=1)
    contrib = jnp.einsum(
        "tji,kti->tkj", tile_weights[0, 0, 0], picked, preferred_element_type=jnp.float32
    )
    onehot = (target[:, None] == jnp.arange(ndev, dtype=jnp.int32)[None, :]).astype(jnp.int32)
    earlier = jnp.cumsum(onehot, axis=0) - onehot
    rank = jnp.sum(earlier * onehot, axis=1)
    slot = target * CAP + rank
    buckets = (
        jnp.zeros((ndev * CAP, KF, CY), jnp.float32)
        .at[slot]
        .set(contrib)
        .reshape(ndev, CAP, KF, CY)
    )
    labels = jnp.zeros((ndev * CAP,), jnp.int32).at[slot].set(dest_row + 1).reshape(ndev, CAP)
    empty = jnp.zeros_like(buckets)
    empty_rows = jnp.zeros_like(labels)
    wide = jnp.where(
        group == 0, jnp.concatenate([empty, buckets], 0), jnp.concatenate([buckets, empty], 0)
    )
    wide_rows = jnp.where(
        group == 0,
        jnp.concatenate([empty_rows, labels], 0),
        jnp.concatenate([labels, empty_rows], 0),
    )
    arrived, arrived_rows = (
        lax.all_to_all(wide, ("mp", "gx", "gy"), split_axis=0, concat_axis=0, tiled=True),
        lax.all_to_all(wide_rows, ("mp", "gx", "gy"), split_axis=0, concat_axis=0, tiled=True),
    )
    start = (1 - group) * ndev
    got = lax.dynamic_slice_in_dim(arrived, start, ndev, 0)
    got_rows = lax.dynamic_slice_in_dim(arrived_rows, start, ndev, 0)
    select = (
        got_rows[:, :, None] == jnp.arange(1, rows_here + 1, dtype=jnp.int32)[None, None, :]
    ).astype(jnp.float32)
    received = jnp.einsum("scr,sckj->krj", select, got, precision=lax.Precision.HIGHEST)
    second = two_steps(state, wet, horiz, vert)
    second = second.at[0].add(force_gain * wet * received[0])
    return (second[None], received[None])


def solution(mesh):
    return jax.shard_map(
        local,
        mesh=mesh,
        in_specs=(
            P("mp", None, "gx", "gy"),
            P("mp", None, "gx", "gy"),
            P("gx", "gy"),
            P("mp", "gx", "gy", None, None, None),
            P("mp", "gx", "gy", None),
            P("mp", "gx", "gy", None, None),
            P("mp", "gx", "gy", None),
        ),
        out_specs=(P("mp", None, "gx", "gy"), P("mp", None, "gx", "gy")),
        check_vma=False,
    )
```

profile of v0, /device:TPU:12, one launch (start us, length us, event | category | flops | bytes accessed | tf_op | source)
XLA Modules:
  0.0 165.4 jit_solution(11554718617153812346)
XLA Ops:
  0.7 1.1 copy.25
  1.7 5.6 %copy.26 = f32[1,64,128,128]{2,3,1,0:T(8,128)} copy(f32[1,64,128,128]{3,2,1,0:T(8,128)} %param.9) | data formatting | bytes 8388608 | tf_op args[0]
  7.3 2.5 %broadcast_multiply_fusion.1 = f32[64,128,128]{1,2,0:T(8,128)S(1)} fusion(f32[128,128]{0,1:T(8,128)S(1)} %convert_select_fusion, f32[1,64,128,128]{2,3,1,0:T(8,128)} %copy.26), kind=kLoop, calls=%fused_computation.38 | loop fusion | flops 1048576 | bytes 8454144 | tf_op jit(solution)/shard_map/mul | solution.py:33
  9.9 4.8 %fusion.42 = (f32[64,1,128]{1,2,0:T(8,128)}, f32[64,1,128]{1,2,0:T(8,128)}) fusion(f32[64,128,128]{1,2,0:T(8,128)S(1)} %broadcast_multiply_fusion.1), kind=kLoop, calls=%fused_computation.85 | loop fusion | bytes 131072 | tf_op jit(solution)/shard_map/slice | solution.py:19
  14.7 2.9 %copy.27 = f32[64,1,128]{2,0,1:T(8,128)S(1)} copy(f32[64,1,128]{1,2,0:T(8,128)} %get-tuple-element.29) | data formatting | bytes 65536 | tf_op jit(solution)/shard_map/slice | solution.py:20
  17.6 2.4 %collective-permute-start = (f32[64,1,128]{2,0,1:T(8,128)S(1)}, f32[64,1,128]{2,0,1:T(8,128)S(1)}, u32[]{:S(2)}, u32[]{:S(2)}) collective-permute-start(f32[64,1,128]{2,0,1:T(8,128)S(1)} %copy.27), channel_id=1, source_target_pairs={{4,0},{8,4},{12,8},{5,1},{9,5},{13,9},{6,2},{10,6},{14,10},{7,3},{... | collective-permute-start | bytes 98312 | tf_op jit(solution)/shard_map/ppermute | solution.py:22
  20.0 2.8 %copy.29 = f32[64,1,128]{2,0,1:T(8,128)S(1)} copy(f32[64,1,128]{1,2,0:T(8,128)} %get-tuple-element.28) | data formatting | bytes 65536 | tf_op jit(solution)/shard_map/slice | solution.py:19
  22.8 3.5 %collective-permute-start.1 = (f32[64,1,128]{2,0,1:T(8,128)S(1)}, f32[64,1,128]{2,0,1:T(8,128)S(1)}, u32[]{:S(2)}, u32[]{:S(2)}) collective-permute-start(f32[64,1,128]{2,0,1:T(8,128)S(1)} %copy.29), channel_id=1, source_target_pairs={{0,4},{4,8},{8,12},{1,5},{5,9},{9,13},{2,6},{6,10},{10,14},{3,7},{... | collective-permute-start | bytes 98312 | tf_op jit(solution)/shard_map/ppermute | solution.py:21
  26.4 0.1 reduce_window_sum.11
  26.5 0.2 select_reduce_fusion
  26.7 0.8 scatter_custom_fusion.1
  27.6 0.6 pad_select_fusion.1
  28.2 5.0 %all-to-all-start.1 = ((s32[32,1,8]{2,1,0:T(1,128)}), s32[32,1,8]{2,1,0:T(1,128)S(1)}, u32[]{:S(2)}, u32[]{:S(2)}) async-start(s32[32,1,8]{2,1,0:T(1,128)} %bitcast.15), calls=%async_computation.1 | async-start | bytes 32768 | tf_op jit(solution)/shard_map/all_to_all | solution.py:91
  33.2 0.1 copy.40
  33.3 0.3 fusion.20
  33.7 0.6 gather_fusion
  34.3 1.2 fusion.16
  35.6 2.4 %scatter_fusion = f32[128,8,128]{2,1,0:T(8,128)S(1)} fusion(f32[128,8,128]{2,1,0:T(8,128)S(1)} %broadcast_in_dim.41, s32[64]{0:T(128)S(1)} %get-tuple-element.30, f32[64,8,128]{2,1,0:T(8,128)S(1)} %fusion.16), kind=kCustom, calls=%fused_computation.1 | custom fusion | bytes 786688 | tf_op jit(solution)/shard_map/scatter | solution.py:75
  38.0 2.6 %copy.28 = f32[64,1,128]{1,2,0:T(8,128)} copy(f32[64,1,128]{2,0,1:T(8,128)S(1)} %collective-permute-done) | data formatting | bytes 65536 | tf_op jit(solution)/shard_map/ppermute | solution.py:22
  40.7 2.6 %copy.30 = f32[64,1,128]{1,2,0:T(8,128)} copy(f32[64,1,128]{2,0,1:T(8,128)S(1)} %collective-permute-done.1) | data formatting | bytes 65536 | tf_op jit(solution)/shard_map/ppermute | solution.py:21
  43.3 1.8 %pad_maximum_fusion.21 = (f32[64,130,1]{1,2,0:T(1,128)S(1)}, f32[64,130,1]{1,2,0:T(1,128)S(1)}) fusion(f32[64,1,128]{1,2,0:T(8,128)} %copy.28, f32[64,128,128]{1,2,0:T(8,128)} %copy-done.2, f32[64,1,128]{1,2,0:T(8,128)} %copy.30), kind=kLoop, calls=%fused_computation.58 | loop fusion | flops 33280 | bytes 4326400 | tf_op jit(solution)/shard_map/slice | solution.py:20
  45.1 3.4 %collective-permute-start.2 = (f32[64,130,1]{1,2,0:T(1,128)S(1)}, f32[64,130,1]{1,2,0:T(1,128)S(1)}, u32[]{:S(2)}, u32[]{:S(2)}) collective-permute-start(f32[64,130,1]{1,2,0:T(1,128)S(1)} %get-tuple-element.24), channel_id=1, source_target_pairs={{1,0},{2,1},{3,2},{5,4},{6,5},{7,6},{9,8},{10,9},{11,10},{13,12},{... | collective-permute-start | bytes 99848 | tf_op jit(solution)/shard_map/ppermute | solution.py:22
  48.5 2.5 %collective-permute-start.3 = (f32[64,130,1]{1,2,0:T(1,128)S(1)}, f32[64,130,1]{1,2,0:T(1,128)S(1)}, u32[]{:S(2)}, u32[]{:S(2)}) collective-permute-start(f32[64,130,1]{1,2,0:T(1,128)S(1)} %get-tuple-element.25), channel_id=1, source_target_pairs={{0,1},{1,2},{2,3},{4,5},{5,6},{6,7},{8,9},{9,10},{10,11},{12,13},{... | collective-permute-start | bytes 99848 | tf_op jit(solution)/shard_map/ppermute | solution.py:21
  51.0 0.1 pad_select_fusion
  51.1 1.2 copy.41
  52.3 3.3 %collective-permute-done.3 = f32[64,130,1]{1,2,0:T(1,128)S(1)} collective-permute-done((f32[64,130,1]{1,2,0:T(1,128)S(1)}, f32[64,130,1]{1,2,0:T(1,128)S(1)}, u32[]{:S(2)}, u32[]{:S(2)}) %collective-permute-start.3) | collective-permute-done | bytes 33312 | tf_op jit(solution)/shard_map/ppermute | solution.py:21
  55.6 25.5 %broadcast_multiply_fusion = (f32[64,128,128]{1,2,0:T(8,128)}, f32[64,128,128]{1,2,0:T(8,128)}) fusion(f32[128,128]{0,1:T(8,128)S(1)} %convert_select_fusion, f32[64,128,128]{1,2,0:T(8,128)} %bitcast.68, f32[]{:T(128)S(6)} %select_n.69, f32[64,128,128]{1,2,0:T(8,128)} %copy-done.2, f32[64,1,128]{1,2,0:T(8,128)} %copy.28, f32[64,1,128]{1,2,0:T(8,128)} %copy.30, ...), kind=kLoop, calls=%fused_computation.37 | loop fusion | flops 23068672 | bytes 16974856 | tf_op jit(solution)/shard_map/mul | solution.py:33
  81.1 4.9 %all-to-all-start = ((f32[32,8,8,128]{3,1,2,0:T(8,128)}), f32[32,8,8,128]{3,1,2,0:T(8,128)S(1)}, u32[]{:S(2)}, u32[]{:S(2)}) async-start(f32[32,8,8,128]{3,1,2,0:T(8,128)} %copy.41), calls=%async_computation | async-start | bytes 2097152 | tf_op jit(solution)/shard_map/all_to_all | solution.py:90
  86.0 8.1 %fusion.41 = (f32[64,1,128]{1,2,0:T(8,128)}, f32[64,1,128]{1,2,0:T(8,128)}) fusion(f32[64,128,128]{1,2,0:T(8,128)} %get-tuple-element.20), kind=kLoop, calls=%fused_computation.84 | loop fusion | bytes 131072 | tf_op jit(solution)/shard_map/slice | solution.py:19
  94.1 2.8 %copy.33 = f32[64,1,128]{2,0,1:T(8,128)S(1)} copy(f32[64,1,128]{1,2,0:T(8,128)} %get-tuple-element.27) | data formatting | bytes 65536 | tf_op jit(solution)/shard_map/slice | solution.py:20
  96.9 2.5 %collective-permute-start.4 = (f32[64,1,128]{2,0,1:T(8,128)S(1)}, f32[64,1,128]{2,0,1:T(8,128)S(1)}, u32[]{:S(2)}, u32[]{:S(2)}) collective-permute-start(f32[64,1,128]{2,0,1:T(8,128)S(1)} %copy.33), channel_id=1, source_target_pairs={{4,0},{8,4},{12,8},{5,1},{9,5},{13,9},{6,2},{10,6},{14,10},{7,3},{... | collective-permute-start | bytes 98312 | tf_op jit(solution)/shard_map/ppermute | solution.py:22
  99.4 2.8 %copy.35 = f32[64,1,128]{2,0,1:T(8,128)S(1)} copy(f32[64,1,128]{1,2,0:T(8,128)} %get-tuple-element.26) | data formatting | bytes 65536 | tf_op jit(solution)/shard_map/slice | solution.py:19
  102.3 3.6 %collective-permute-start.5 = (f32[64,1,128]{2,0,1:T(8,128)S(1)}, f32[64,1,128]{2,0,1:T(8,128)S(1)}, u32[]{:S(2)}, u32[]{:S(2)}) collective-permute-start(f32[64,1,128]{2,0,1:T(8,128)S(1)} %copy.35), channel_id=1, source_target_pairs={{0,4},{4,8},{8,12},{1,5},{5,9},{9,13},{2,6},{6,10},{10,14},{3,7},{... | collective-permute-start | bytes 98312 | tf_op jit(solution)/shard_map/ppermute | solution.py:21
  105.8 5.9 %collective-permute-done.4 = f32[64,1,128]{2,0,1:T(8,128)S(1)} collective-permute-done((f32[64,1,128]{2,0,1:T(8,128)S(1)}, f32[64,1,128]{2,0,1:T(8,128)S(1)}, u32[]{:S(2)}, u32[]{:S(2)}) %collective-permute-start.4) | collective-permute-done | bytes 32800 | tf_op jit(solution)/shard_map/ppermute | solution.py:22
  111.7 2.7 %copy.34 = f32[64,1,128]{1,2,0:T(8,128)} copy(f32[64,1,128]{2,0,1:T(8,128)S(1)} %collective-permute-done.4) | data formatting | bytes 65536 | tf_op jit(solution)/shard_map/ppermute | solution.py:22
  114.4 2.6 %copy.36 = f32[64,1,128]{1,2,0:T(8,128)} copy(f32[64,1,128]{2,0,1:T(8,128)S(1)} %collective-permute-done.5) | data formatting | bytes 65536 | tf_op jit(solution)/shard_map/ppermute | solution.py:21
  117.0 1.8 %pad_maximum_fusion.18 = (f32[64,130,1]{1,2,0:T(1,128)S(1)}, f32[64,130,1]{1,2,0:T(1,128)S(1)}) fusion(f32[64,1,128]{1,2,0:T(8,128)} %copy.34, f32[64,128,128]{1,2,0:T(8,128)} %get-tuple-element.20, f32[64,1,128]{1,2,0:T(8,128)} %copy.36), kind=kLoop, calls=%fused_computation.55 | loop fusion | flops 33280 | bytes 4326400 | tf_op jit(solution)/shard_map/slice | solution.py:20
  118.9 3.4 %collective-permute-start.6 = (f32[64,130,1]{1,2,0:T(1,128)S(1)}, f32[64,130,1]{1,2,0:T(1,128)S(1)}, u32[]{:S(2)}, u32[]{:S(2)}) collective-permute-start(f32[64,130,1]{1,2,0:T(1,128)S(1)} %get-tuple-element.22), channel_id=1, source_target_pairs={{1,0},{2,1},{3,2},{5,4},{6,5},{7,6},{9,8},{10,9},{11,10},{13,12},{... | collective-permute-start | bytes 99848 | tf_op jit(solution)/shard_map/ppermute | solution.py:22
  122.3 2.5 %collective-permute-start.7 = (f32[64,130,1]{1,2,0:T(1,128)S(1)}, f32[64,130,1]{1,2,0:T(1,128)S(1)}, u32[]{:S(2)}, u32[]{:S(2)}) collective-permute-start(f32[64,130,1]{1,2,0:T(1,128)S(1)} %get-tuple-element.23), channel_id=1, source_target_pairs={{0,1},{1,2},{2,3},{4,5},{5,6},{6,7},{8,9},{9,10},{10,11},{12,13},{... | collective-permute-start | bytes 99848 | tf_op jit(solution)/shard_map/ppermute | solution.py:21
  124.8 0.2 collective-permute-done.6
  125.0 4.3 %collective-permute-done.7 = f32[64,130,1]{1,2,0:T(1,128)S(1)} collective-permute-done((f32[64,130,1]{1,2,0:T(1,128)S(1)}, f32[64,130,1]{1,2,0:T(1,128)S(1)}, u32[]{:S(2)}, u32[]{:S(2)}) %collective-permute-start.7) | collective-permute-done | bytes 33312 | tf_op jit(solution)/shard_map/ppermute | solution.py:21
  129.3 23.1 %fusion.5 = f32[64,128,128]{1,2,0:T(8,128)S(1)} fusion(f32[64,128,128]{1,2,0:T(8,128)} %get-tuple-element.21, f32[64,130,1]{1,2,0:T(1,128)S(1)} %collective-permute-done.7, f32[64,1,128]{1,2,0:T(8,128)} %copy.34, f32[64,128,128]{1,2,0:T(8,128)} %get-tuple-element.20, f32[64,1,128]{1,2,0:T(8,128)} %copy.36, f32[64,130,1]{1,2,0:T(1,128)S(1)} %collective-permute-done.6, ...), kind=kLoop, calls=%fused_computation.9 | loop fusion | flops 22020096 | bytes 12780552 | tf_op jit(solution)/shard_map/mul | solution.py:42
  152.4 2.0 %copy-done.3 = f32[64,128,128]{1,2,0:T(8,128)} copy-done((f32[64,128,128]{1,2,0:T(8,128)}, f32[64,128,128]{1,2,0:T(8,128)S(1)}, u32[]{:S(2)}) %copy-start.3) | copy-done | bytes 4194328
  154.4 2.0 %copy.54 = f32[1,64,128,128]{2,3,1,0:T(8,128)} copy(f32[1,64,128,128]{2,3,1,0:T(8,128)S(1)} %bitcast.69) | data formatting | bytes 8388608
  156.4 0.8 fusion.18
  157.2 1.6 fusion.28
  158.8 5.6 %copy.45 = f32[1,64,128,128]{3,2,1,0:T(8,128)} copy(f32[1,64,128,128]{2,3,1,0:T(8,128)} %fusion.28) | data formatting | bytes 8388608
  164.4 1.0 copy.46
  (33 shorter events, 0.4 us)
Async XLA Ops:
  0.6 33.7 %copy-start = (bf16[1,1,1,64,128,128]{5,4,3,2,1,0:T(8,128)(2,1)S(1)}, bf16[1,1,1,64,128,128]{5,4,3,2,1,0:T(8,128)(2,1)}, u32[]{:S(2)}) copy-start(bf16[1,1,1,64,128,128]{5,4,3,2,1,0:T(8,128)(2,1)} %param.12) | copy-start | bytes 6291460
  9.9 4.8 %copy-start.2 = (f32[64,128,128]{1,2,0:T(8,128)}, f32[64,128,128]{1,2,0:T(8,128)S(1)}, u32[]{:S(2)}) copy-start(f32[64,128,128]{1,2,0:T(8,128)S(1)} %broadcast_multiply_fusion.1) | copy-start | bytes 12582916
  14.7 11.6 %copy-start.5 = (s32[1,1,1,64,1]{3,4,2,1,0:T(1,128)S(1)}, s32[1,1,1,64,1]{3,4,2,1,0:T(1,128)}, u32[]{:S(2)}) copy-start(s32[1,1,1,64,1]{3,4,2,1,0:T(1,128)} %param.14) | copy-start | bytes 772
  14.7 12.0 %copy-start.7 = (s32[1,1,1,64]{3,2,1,0:T(1,128)S(1)}, s32[1,1,1,64]{3,2,1,0:T(1,128)}, u32[]{:S(2)}) copy-start(s32[1,1,1,64]{3,2,1,0:T(1,128)} %param.15) | copy-start | bytes 772
  14.7 12.0 %copy-start.6 = (s32[1,1,1,64]{3,2,1,0:T(1,128)S(1)}, s32[1,1,1,64]{3,2,1,0:T(1,128)}, u32[]{:S(2)}) copy-start(s32[1,1,1,64]{3,2,1,0:T(1,128)} %param.13) | copy-start | bytes 772
  14.7 18.6 %copy-start.4 = (f32[1,8,128,128]{3,2,1,0:T(8,128)S(1)}, f32[1,8,128,128]{3,2,1,0:T(8,128)}, u32[]{:S(2)}) copy-start(f32[1,8,128,128]{3,2,1,0:T(8,128)} %param.10) | copy-start | bytes 1572868
  17.6 20.4 %collective-permute-start = (f32[64,1,128]{2,0,1:T(8,128)S(1)}, f32[64,1,128]{2,0,1:T(8,128)S(1)}, u32[]{:S(2)}, u32[]{:S(2)}) collective-permute-start(f32[64,1,128]{2,0,1:T(8,128)S(1)} %copy.27), channel_id=1, source_target_pairs={{4,0},{8,4},{12,8},{5,1},{9,5},{13,9},{6,2},{10,6},{14,10},{7,3},{... | collective-permute-start | bytes 98312 | tf_op jit(solution)/shard_map/ppermute | solution.py:22
  22.8 17.8 %collective-permute-start.1 = (f32[64,1,128]{2,0,1:T(8,128)S(1)}, f32[64,1,128]{2,0,1:T(8,128)S(1)}, u32[]{:S(2)}, u32[]{:S(2)}) collective-permute-start(f32[64,1,128]{2,0,1:T(8,128)S(1)} %copy.29), channel_id=1, source_target_pairs={{0,4},{4,8},{8,12},{1,5},{5,9},{9,13},{2,6},{6,10},{10,14},{3,7},{... | collective-permute-start | bytes 98312 | tf_op jit(solution)/shard_map/ppermute | solution.py:21
  28.2 52.9 %all-to-all-start.1 = ((s32[32,1,8]{2,1,0:T(1,128)}), s32[32,1,8]{2,1,0:T(1,128)S(1)}, u32[]{:S(2)}, u32[]{:S(2)}) async-start(s32[32,1,8]{2,1,0:T(1,128)} %bitcast.15), calls=%async_computation.1 | async-start | bytes 32768 | tf_op jit(solution)/shard_map/all_to_all | solution.py:91
  45.1 7.2 %collective-permute-start.2 = (f32[64,130,1]{1,2,0:T(1,128)S(1)}, f32[64,130,1]{1,2,0:T(1,128)S(1)}, u32[]{:S(2)}, u32[]{:S(2)}) collective-permute-start(f32[64,130,1]{1,2,0:T(1,128)S(1)} %get-tuple-element.24), channel_id=1, source_target_pairs={{1,0},{2,1},{3,2},{5,4},{6,5},{7,6},{9,8},{10,9},{11,10},{13,12},{... | collective-permute-start | bytes 99848 | tf_op jit(solution)/shard_map/ppermute | solution.py:22
  48.5 7.1 %collective-permute-start.3 = (f32[64,130,1]{1,2,0:T(1,128)S(1)}, f32[64,130,1]{1,2,0:T(1,128)S(1)}, u32[]{:S(2)}, u32[]{:S(2)}) collective-permute-start(f32[64,130,1]{1,2,0:T(1,128)S(1)} %get-tuple-element.25), channel_id=1, source_target_pairs={{0,1},{1,2},{2,3},{4,5},{5,6},{6,7},{8,9},{9,10},{10,11},{12,13},{... | collective-permute-start | bytes 99848 | tf_op jit(solution)/shard_map/ppermute | solution.py:21
  81.1 75.3 %all-to-all-start = ((f32[32,8,8,128]{3,1,2,0:T(8,128)}), f32[32,8,8,128]{3,1,2,0:T(8,128)S(1)}, u32[]{:S(2)}, u32[]{:S(2)}) async-start(f32[32,8,8,128]{3,1,2,0:T(8,128)} %copy.41), calls=%async_computation | async-start | bytes 2097152 | tf_op jit(solution)/shard_map/all_to_all | solution.py:90
  96.9 14.8 %collective-permute-start.4 = (f32[64,1,128]{2,0,1:T(8,128)S(1)}, f32[64,1,128]{2,0,1:T(8,128)S(1)}, u32[]{:S(2)}, u32[]{:S(2)}) collective-permute-start(f32[64,1,128]{2,0,1:T(8,128)S(1)} %copy.33), channel_id=1, source_target_pairs={{4,0},{8,4},{12,8},{5,1},{9,5},{13,9},{6,2},{10,6},{14,10},{7,3},{... | collective-permute-start | bytes 98312 | tf_op jit(solution)/shard_map/ppermute | solution.py:22
  102.3 12.2 %collective-permute-start.5 = (f32[64,1,128]{2,0,1:T(8,128)S(1)}, f32[64,1,128]{2,0,1:T(8,128)S(1)}, u32[]{:S(2)}, u32[]{:S(2)}) collective-permute-start(f32[64,1,128]{2,0,1:T(8,128)S(1)} %copy.35), channel_id=1, source_target_pairs={{0,4},{4,8},{8,12},{1,5},{5,9},{9,13},{2,6},{6,10},{10,14},{3,7},{... | collective-permute-start | bytes 98312 | tf_op jit(solution)/shard_map/ppermute | solution.py:21
  118.9 6.2 %collective-permute-start.6 = (f32[64,130,1]{1,2,0:T(1,128)S(1)}, f32[64,130,1]{1,2,0:T(1,128)S(1)}, u32[]{:S(2)}, u32[]{:S(2)}) collective-permute-start(f32[64,130,1]{1,2,0:T(1,128)S(1)} %get-tuple-element.22), channel_id=1, source_target_pairs={{1,0},{2,1},{3,2},{5,4},{6,5},{7,6},{9,8},{10,9},{11,10},{13,12},{... | collective-permute-start | bytes 99848 | tf_op jit(solution)/shard_map/ppermute | solution.py:22
  122.3 7.1 %collective-permute-start.7 = (f32[64,130,1]{1,2,0:T(1,128)S(1)}, f32[64,130,1]{1,2,0:T(1,128)S(1)}, u32[]{:S(2)}, u32[]{:S(2)}) collective-permute-start(f32[64,130,1]{1,2,0:T(1,128)S(1)} %get-tuple-element.23), channel_id=1, source_target_pairs={{0,1},{1,2},{2,3},{4,5},{5,6},{6,7},{8,9},{9,10},{10,11},{12,13},{... | collective-permute-start | bytes 99848 | tf_op jit(solution)/shard_map/ppermute | solution.py:21
  152.4 2.0 %copy-start.3 = (f32[64,128,128]{1,2,0:T(8,128)}, f32[64,128,128]{1,2,0:T(8,128)S(1)}, u32[]{:S(2)}) copy-start(f32[64,128,128]{1,2,0:T(8,128)S(1)} %fusion.5) | copy-start | bytes 12582916
  157.2 8.2 %copy-start.1 = (bf16[1,1,1,64,128,128]{5,4,3,2,1,0:T(8,128)(2,1)S(1)}, bf16[1,1,1,64,128,128]{5,4,3,2,1,0:T(8,128)(2,1)}, u32[]{:S(2)}) copy-start(bf16[1,1,1,64,128,128]{5,4,3,2,1,0:T(8,128)(2,1)} %param.12) | copy-start | bytes 6291460
where the time goes:
time: 166 us; the launch traced here: 165 us
  other arithmetic  57.8 us (35%)
  local copies, waits for them, and re-layouts  57.5 us (35%)
  starting transfers between devices  33.4 us (20%)
  waiting for transfers between devices  13.7 us (8%)
  matrix products  1.99 us (1%)
    mul x2, other arithmetic, stencil(): weighted = state * wet  28 us
    mul x1, other arithmetic, stencil(): return wet * (state + horiz * lateral + vert * vertical_part(state))  23.1 us
    slice x4, local copies, waits for them, and re-layouts, with_halo(): last = lax.slice_in_dim(shard, length - width, length, axis=dim)  18.6 us
    unnamed x22, local copies, waits for them, and re-layouts  17.3 us
    ppermute x4, starting transfers between devices, with_halo(): before = lax.ppermute(last, axis, up)  12 us
    ppermute x4, starting transfers between devices, with_halo(): after = lax.ppermute(first, axis, down)  11.6 us
    ppermute x4, waiting for transfers between devices, with_halo(): before = lax.ppermute(last, axis, up)  7.55 us
    ppermute x4, waiting for transfers between devices, with_halo(): after = lax.ppermute(first, axis, down)  6.13 us
  transfers between devices with their start and end apart: 10, of which 4 were waited for; matrix products, arithmetic and copies ran while one was open for 54% of the time, Pallas kernels for 0%

commit v1 on v0

v1 whole, which is shorter than its diff:
```python
import functools

import jax
import jax.numpy as jnp
from jax import lax
from jax.experimental import pallas as pl
from jax.experimental.pallas import tpu as pltpu
from jax.sharding import PartitionSpec as P

CAP = 8
FORCE = 0.5
HORIZ = (0.15, 0.12)
VERT = (0.1, 0.15)
MIB = 1024 * 1024
ANY = pl.BlockSpec(memory_space=pl.ANY)
VMEM = pl.BlockSpec(memory_space=pltpu.VMEM)
SMEM = pl.BlockSpec(memory_space=pltpu.SMEM)


def params(mib):
    return pltpu.CompilerParams(vmem_limit_bytes=mib * MIB)


def wet_of(mask_ref):
    ocean = lax.axis_index("mp") == 1
    return jnp.where(ocean, mask_ref[...].astype(jnp.float32), 1.0)


def lanes(shape):
    return lax.broadcasted_iota(jnp.int32, shape, len(shape) - 1)


def tiles_kernel(ndev, ngy, chunk, src, tgt, row, mask, surface, weights, out, wet, wbuf, sbuf, count, sems):
    tiles = src.shape[0]
    cx = mask.shape[0]
    pieces = tiles // chunk
    copies = [pltpu.make_async_copy(surface, sbuf, sems.at[pieces])]
    for i in range(pieces):
        part = pl.ds(i * chunk, chunk)
        copies.append(pltpu.make_async_copy(weights.at[part], wbuf.at[part], sems.at[i]))
    for copy in copies:
        copy.start()
    wet[...] = wet_of(mask)
    out[...] = jnp.zeros_like(out)
    for d in range(ndev):
        count[d] = 0
    me = lax.axis_index("gx") * ngy + lax.axis_index("gy")
    place = lax.broadcasted_iota(jnp.int32, (8, 128), 0) * 128 + lanes((8, 128))
    copies[0].wait()

    def one(t, _):
        s, d = src[t], tgt[t, 0]
        rank = count[d]
        count[d] = rank + 1
        picked = sbuf[pl.ds(s, 8, stride=cx), :] * wet[pl.ds(s, 1), :]
        out[d, pl.ds(rank * 8, 8), :] = lax.dot_general(
            picked.astype(jnp.bfloat16),
            wbuf[t],
            (((1,), (1,)), ((), ())),
            preferred_element_type=jnp.float32,
        )
        label = (row[t] + 1).astype(jnp.float32)
        out[d, 64:72, :] = jnp.where(place == me * CAP + rank, label, out[d, 64:72, :])
        return 0

    for i in range(pieces):
        copies[i + 1].wait()
        lax.fori_loop(i * chunk, (i + 1) * chunk, one, 0, unroll=True)


def remap_tiles(src, tgt, row, mask, surface, weights, ndev, ngy):
    tiles = src.shape[0]
    chunk = 16
    return pl.pallas_call(
        functools.partial(tiles_kernel, ndev, ngy, chunk),
        out_shape=jax.ShapeDtypeStruct((ndev, 72, 128), jnp.float32),
        in_specs=[SMEM, SMEM, SMEM, VMEM, ANY, ANY],
        out_specs=VMEM,
        scratch_shapes=[
            pltpu.VMEM(mask.shape, jnp.float32),
            pltpu.VMEM(weights.shape, weights.dtype),
            pltpu.VMEM(surface.shape, jnp.float32),
            pltpu.SMEM((ndev,), jnp.int32),
            pltpu.SemaphoreType.DMA((tiles // chunk + 1,)),
        ],
        compiler_params=params(32),
        cost_estimate=pl.CostEstimate(flops=4 * 10**8, bytes_accessed=4 * 10**6, transcendentals=0),
    )(src, tgt, row, mask, surface, weights)


def pack_kernel(group, mask, state, up, down, left, right, wet, buf, sems):
    lev, cx, cy = state.shape
    copies = []
    for i in range(lev // group):
        part = pl.ds(i * group, group)
        copies.append(pltpu.make_async_copy(state.at[part], buf.at[part], sems.at[i]))
        copies[-1].start()
    wet[...] = wet_of(mask)
    turned = jnp.transpose(wet[...])
    up[2 * lev :, :] = jnp.broadcast_to(wet[0:1, :], (8, cy))
    down[2 * lev :, :] = jnp.broadcast_to(wet[cx - 1 :, :], (8, cy))
    left[cx:, :] = jnp.broadcast_to(turned[0:1, :], (8, cx))
    right[cx:, :] = jnp.broadcast_to(turned[cy - 1 :, :], (8, cx))
    strip = 32
    flat = buf.reshape(lev * cx, cy)
    lane = lanes((strip, cy))
    for i in range(lev // group):
        copies[i].wait()
        part = pl.ds(i * group, group)
        for dst, off, r in ((up, 0, 0), (up, lev, 1), (down, 0, cx - 1), (down, lev, cx - 2)):
            dst[pl.ds(off + i * group, group), :] = (
                flat[pl.ds(i * group * cx + r, group, stride=cx), :] * wet[r : r + 1, :]
            )
        for b in range(cx // strip):
            rows = pl.ds(b * strip, strip)
            if i == 0:
                lo = hi = jnp.zeros((strip, cy), jnp.float32)
            else:
                lo, hi = left[rows, :], right[rows, :]
            for l in range(i * group, (i + 1) * group):
                moved = pltpu.roll(buf[l, rows, :], (2 * l + 2) % cy, 1)
                at = (2 * l + 2) % cy
                lo = jnp.where((lane == at) | (lane == at + 1), moved, lo)
                hi = jnp.where((lane == 2 * l) | (lane == 2 * l + 1), moved, hi)
            if i == lev // group - 1:
                edge = wet[rows, :]
                first, second = edge[:, 0:1], edge[:, 1:2]
                lo = lo * jnp.where(lane % 2 == 0, first, second)
                first, second = edge[:, cy - 2 : cy - 1], edge[:, cy - 1 :]
                hi = hi * jnp.where(lane % 2 == 0, first, second)
            left[rows, :] = lo
            right[rows, :] = hi


def pack_edges(mask, state):
    lev, cx, cy = state.shape
    group = 8
    message = jax.ShapeDtypeStruct((2 * lev + 8, cy), jnp.float32)
    columns = jax.ShapeDtypeStruct((cx + 8, cy), jnp.float32)
    return pl.pallas_call(
        functools.partial(pack_kernel, group),
        out_shape=(message, message, columns, columns),
        in_specs=[VMEM, ANY],
        out_specs=(VMEM,) * 4,
        scratch_shapes=[
            pltpu.VMEM(mask.shape, jnp.float32),
            pltpu.VMEM(state.shape, jnp.float32),
            pltpu.SemaphoreType.DMA((lev // group,)),
        ],
        compiler_params=params(16),
        cost_estimate=pl.CostEstimate(flops=10**7, bytes_accessed=4 * 10**6, transcendentals=0),
    )(mask, state)


def shifted(x, by, axis):
    size = x.shape[axis]
    moved = pltpu.roll(x, by % size, axis)
    index = lax.broadcasted_iota(jnp.int32, x.shape, axis)
    return jnp.where(index == (0 if by == 1 else size - 1), 0.0, moved)


PAD = 8


def stencil_kernel(
    group, ngx, ngy, mask, state, up, down, left, right, top, bottom, west, east, cwest, ceast,
    out, wet, hwet, one, two, cols, cols2, res, sems, osems,
):
    lev, cx, cy = state.shape
    pieces = lev // group
    copies = []
    for i in range(pieces):
        part = pl.ds(i * group, group)
        copies.append(
            pltpu.make_async_copy(
                state.at[part], one.at[pl.ds(i * group + 1, group), pl.ds(PAD, cx), :], sems.at[i]
            )
        )
        copies[-1].start()
    ocean = lax.axis_index("mp") == 1
    horiz = jnp.where(ocean, HORIZ[1], HORIZ[0]).astype(jnp.float32)
    vert = jnp.where(ocean, VERT[1], VERT[0]).astype(jnp.float32)
    centre = 1.0 - 4.0 * horiz - 2.0 * vert
    gx, gy = lax.axis_index("gx"), lax.axis_index("gy")
    has = lambda c: jnp.where(c, 1.0, 0.0).astype(jnp.float32)
    has_top, has_bottom = has(gx > 0), has(gx < ngx - 1)
    has_west, has_east = has(gy > 0), has(gy < ngy - 1)
    wet[...] = wet_of(mask)
    hwet[...] = wet[...] * horiz

    lane = lanes((lev, cy))
    flat_one = one.reshape((lev + 2) * (cx + 2 * PAD), cy)
    flat_two = two.reshape((lev + 2) * (cx + 2 * PAD), cy)
    height = cx + 2 * PAD
    for msg, own, flag, off, at in ((top, up, has_top, 0, PAD - 1), (bottom, down, has_bottom, lev, PAD + cx)):
        near = msg[0:lev, :] * flag
        far = msg[lev : 2 * lev, :] * flag
        w_corner = cwest[off : off + lev, :] * (flag * has_west)
        e_corner = ceast[off : off + lev, :] * (flag * has_east)
        side = pltpu.roll(jnp.where(lane == cy - 1, w_corner, near), 1, 1) + pltpu.roll(
            jnp.where(lane == 0, e_corner, near), cy - 1, 1
        )
        gain = msg[2 * lev : 2 * lev + 1, :] * (horiz * flag)
        ring = (
            centre * near
            + gain * (side + far + own[0:lev, :])
            + vert * (shifted(near, 1, 0) + shifted(near, -1, 0))
        )
        flat_one[pl.ds(height + at, lev, stride=height), :] = near
        flat_two[pl.ds(height + at, lev, stride=height), :] = ring

    lane = lanes((cx, cy))
    odd = lane % 2 == 1
    west_cols = west[0:cx, :] * has_west
    east_cols = east[0:cx, :] * has_east
    w_gain = jnp.transpose(jnp.broadcast_to(west[cx : cx + 1, :], (cx, cx))) * (horiz * has_west)
    e_gain = jnp.transpose(jnp.broadcast_to(east[cx : cx + 1, :], (cx, cx))) * (horiz * has_east)
    merged = jnp.where(odd, west_cols, east_cols)
    cols[...] = merged
    beside = (
        jnp.where(odd, pltpu.roll(west_cols, 1, 1), pltpu.roll(east_cols, cy - 1, 1))
        + jnp.where(odd, pltpu.roll(left[0:cx, :], cy - 1, 1), pltpu.roll(right[0:cx, :], 1, 1))
    )
    eye = lanes((lev, cy)) - 2 * lax.broadcasted_iota(jnp.int32, (lev, cy), 0)
    eye_w = eye == 1
    eye_e = (eye == 2) | (eye == 2 - cy)

    def corner_row(off, flag):
        w = cwest[off : off + lev, cy - 1 : cy] * (flag * has_west)
        e = ceast[off : off + lev, 0:1] * (flag * has_east)
        return jnp.sum(jnp.where(eye_w, w, 0.0) + jnp.where(eye_e, e, 0.0), axis=0, keepdims=True)

    sub = lax.broadcasted_iota(jnp.int32, (cx, cy), 0)
    above = jnp.where(sub == 0, corner_row(0, has_top), pltpu.roll(merged, 1, 0))
    below = jnp.where(sub == cx - 1, corner_row(lev, has_bottom), pltpu.roll(merged, cx - 1, 0))
    less = jnp.where((lane == 1) | (lane == 2), 0.0, pltpu.roll(merged, 2, 1))
    more = jnp.where((lane == cy - 1) | (lane == 0), 0.0, pltpu.roll(merged, cy - 2, 1))
    cols2[...] = (
        centre * merged
        + jnp.where(odd, w_gain, e_gain) * (beside + above + below)
        + vert * (less + more)
    )

    for buf in (one, two):
        buf[0] = jnp.zeros((height, cy), jnp.float32)
        buf[lev + 1] = jnp.zeros((height, cy), jnp.float32)

    strip = 64

    def mask_level(l, _):
        one[l + 1, PAD : PAD + cx, :] = one[l + 1, PAD : PAD + cx, :] * wet[...]
        return 0

    def step(buf, sides, l, b):
        lane = lanes((strip, cy))
        r = PAD + b * strip
        here = buf[l + 1, r : r + strip, :]
        edge = pltpu.roll(sides[b * strip : (b + 1) * strip, :], (2 * cy - 2 * l - 2) % cy, 1)
        around = (
            pltpu.roll(jnp.where(lane == cy - 1, edge, here), 1, 1)
            + pltpu.roll(jnp.where(lane == 0, edge, here), cy - 1, 1)
            + buf[l + 1, r - 1 : r - 1 + strip, :]
            + buf[l + 1, r + 1 : r + 1 + strip, :]
        )
        column = buf[l, r : r + strip, :] + buf[l + 2, r : r + strip, :]
        return centre * here + hwet[b * strip : (b + 1) * strip, :] * around + vert * column

    def first_level(l, _):
        for b in range(cx // strip):
            two[l + 1, PAD + b * strip : PAD + (b + 1) * strip, :] = step(one, cols, l, b)
        return 0

    def second_level(l, _):
        for b in range(cx // strip):
            res[l, b * strip : (b + 1) * strip, :] = step(two, cols2, l, b)
        return 0

    outs = []
    for i in range(pieces + 2):
        if i < pieces:
            copies[i].wait()
            lax.fori_loop(i * group, (i + 1) * group, mask_level, 0, unroll=2)
        a, b = max(0, i * group - 1), min(lev, (i + 1) * group - 1)
        if i >= pieces:
            a, b = max(a, lev - 1), lev
        if i <= pieces and a < b:
            lax.fori_loop(a, b, first_level, 0, unroll=False)
        if i >= 1 and i <= pieces:
            start, stop = (i - 1) * group, i * group
            lax.fori_loop(start, stop, second_level, 0, unroll=False)
            part = pl.ds(start, group)
            outs.append(pltpu.make_async_copy(res.at[part], out.at[part], osems.at[i - 1]))
            outs[-1].start()
    for copy in outs:
        copy.wait()


def two_steps(mask, state, messages, ngx, ngy):
    lev, cx, cy = state.shape
    group = 8
    padded = (lev + 2, cx + 2 * PAD, cy)
    return pl.pallas_call(
        functools.partial(stencil_kernel, group, ngx, ngy),
        out_shape=jax.ShapeDtypeStruct(state.shape, jnp.float32),
        in_specs=[VMEM, ANY] + [VMEM] * len(messages),
        out_specs=ANY,
        scratch_shapes=[
            pltpu.VMEM((cx, cy), jnp.float32),
            pltpu.VMEM((cx, cy), jnp.float32),
            pltpu.VMEM(padded, jnp.float32),
            pltpu.VMEM(padded, jnp.float32),
            pltpu.VMEM((cx, cy), jnp.float32),
            pltpu.VMEM((cx, cy), jnp.float32),
            pltpu.VMEM(state.shape, jnp.float32),
            pltpu.SemaphoreType.DMA((lev // group,)),
            pltpu.SemaphoreType.DMA((lev // group,)),
        ],
        compiler_params=params(40),
        cost_estimate=pl.CostEstimate(flops=2 * 10**7, bytes_accessed=10**7, transcendentals=0),
    )(mask, state, *messages)


def collect_kernel(mask, got, second, out, received, buf, level, onehot, sems):
    ndev = got.shape[0]
    fields, cx, cy = received.shape
    slots = ndev * CAP
    fetch = pltpu.make_async_copy(got, buf, sems.at[0])
    fetch.start()
    surface = pltpu.make_async_copy(second.at[0], level, sems.at[1])
    surface.start()
    fetch.wait()
    flat = buf.reshape(ndev * 72, 128)
    labels = flat[64:72, :]
    for s in range(1, ndev):
        labels = labels + flat[s * 72 + 64 : s * 72 + 72, :]
    labels = labels.astype(jnp.int32)
    want = lax.broadcasted_iota(jnp.int32, (cx, 128), 0) + 1
    wide = jnp.concatenate([labels[q : q + 1, :] == want for q in range(slots // 128)], axis=1)
    hot = jnp.where(wide, 1.0, 0.0).astype(jnp.bfloat16)
    onehot[:, 0:slots] = hot
    onehot[:, slots:] = hot
    surface.wait()
    for k in range(fields):
        x = jnp.concatenate([flat[pl.ds(s * 72 + k, CAP, stride=8), :] for s in range(ndev)], axis=0)
        high = x.astype(jnp.bfloat16)
        low = (x - high.astype(jnp.float32)).astype(jnp.bfloat16)
        total = jnp.dot(
            onehot[...], jnp.concatenate([high, low], axis=0), preferred_element_type=jnp.float32
        )
        received[k] = total
        if k == 0:
            level[...] = level[...] + FORCE * wet_of(mask) * total
            store = pltpu.make_async_copy(level, out.at[0], sems.at[1])
            store.start()
    store.wait()


def collect(mask, got, second, fields):
    ndev = got.shape[0]
    cx, cy = mask.shape
    return pl.pallas_call(
        collect_kernel,
        out_shape=(
            jax.ShapeDtypeStruct(second.shape, jnp.float32),
            jax.ShapeDtypeStruct((fields, cx, cy), jnp.float32),
        ),
        in_specs=[VMEM, ANY, ANY],
        out_specs=(ANY, VMEM),
        scratch_shapes=[
            pltpu.VMEM(got.shape, jnp.float32),
            pltpu.VMEM((cx, cy), jnp.float32),
            pltpu.VMEM((cx, 2 * ndev * CAP), jnp.bfloat16),
            pltpu.SemaphoreType.DMA((2,)),
        ],
        input_output_aliases={2: 0},
        compiler_params=params(16),
        cost_estimate=pl.CostEstimate(flops=10**8, bytes_accessed=2 * 10**6, transcendentals=0),
    )(mask, got, second)


def local(states, surface, land_mask, tile_weights, tile_source, tile_target, tile_row):
    ngx, ngy = lax.axis_size("gx"), lax.axis_size("gy")
    ndev = ngx * ngy
    state, fields = states[0], surface.shape[1]
    cx, cy = land_mask.shape
    buckets = remap_tiles(
        tile_source[0, 0, 0],
        tile_target[0, 0, 0],
        tile_row[0, 0, 0],
        land_mask,
        surface.reshape(fields * cx, cy),
        tile_weights[0, 0, 0],
        ndev,
        ngy,
    )
    buckets = lax.ppermute(buckets, "mp", [(0, 1), (1, 0)])
    got = lax.all_to_all(buckets, ("gx", "gy"), split_axis=0, concat_axis=0, tiled=True)

    ahead = lambda n: [(i, (i + 1) % n) for i in range(n)]
    behind = lambda n: [((i + 1) % n, i) for i in range(n)]
    up, down, left, right = pack_edges(land_mask, state)
    top = lax.ppermute(down, "gx", ahead(ngx))
    bottom = lax.ppermute(up, "gx", behind(ngx))
    west = lax.ppermute(right, "gy", ahead(ngy))
    east = lax.ppermute(left, "gy", behind(ngy))
    lev = state.shape[0]
    rows = jnp.concatenate([top[:lev], bottom[:lev]], axis=0)
    corner_west = lax.ppermute(rows, "gy", ahead(ngy))
    corner_east = lax.ppermute(rows, "gy", behind(ngy))
    messages = (up, down, left, right, top, bottom, west, east, corner_west, corner_east)
    second = two_steps(land_mask, state, messages, ngx, ngy)
    new_state, received = collect(land_mask, got, second, fields)
    return new_state[None], received[None]


def solution(mesh):
    return jax.shard_map(
        local,
        mesh=mesh,
        in_specs=(
            P("mp", None, "gx", "gy"),
            P("mp", None, "gx", "gy"),
            P("gx", "gy"),
            P("mp", "gx", "gy", None, None, None),
            P("mp", "gx", "gy", None),
            P("mp", "gx", "gy", None, None),
            P("mp", "gx", "gy", None),
        ),
        out_specs=(P("mp", None, "gx", "gy"), P("mp", None, "gx", "gy")),
        check_vma=False,
    )
```

time: 166 us -> 72.5 us (0.44)
  the two profiles are of different devices: /device:TPU:12 before, /device:TPU:0 now
where the time goes in v1:
time: 72.5 us; the launch traced here: 72 us
  Pallas kernels  33.1 us (46%)
  starting transfers between devices  17.2 us (24%)
  waiting for transfers between devices  13.3 us (18%)
  local copies, waits for them, and re-layouts  7.72 us (11%)
    pallas_call x1, Pallas kernels, two_steps(): pl.pallas_call(functools.partial(stencil_kernel, group, ngx, ngy), out_sh...  25.3 us
    all_to_all x1, starting transfers between devices, local(): lax.all_to_all(buckets, ('gx', 'gy'), split_axis=0, concat_axis=0, tiled=...  8.23 us
    unnamed x16, local copies, waits for them, and re-layouts  6.97 us
    ppermute x1, waiting for transfers between devices, local(): top = lax.ppermute(down, 'gx', ahead(ngx))  4.52 us
    ppermute x1, starting transfers between devices, local(): bottom = lax.ppermute(up, 'gx', behind(ngx))  3.78 us
    pallas_call x1, Pallas kernels, remap_tiles(): pl.pallas_call(functools.partial(tiles_kernel, ndev, ngy, chunk), out_sha...  2.93 us
    ppermute x1, waiting for transfers between devices, local(): corner_east = lax.ppermute(rows, 'gy', behind(ngy))  2.64 us
    pallas_call x1, Pallas kernels, collect(): pl.pallas_call(collect_kernel, out_shape=(jax.ShapeDtypeStruct(second.sha...  2.6 us
  transfers between devices with their start and end apart: 8, of which 5 were waited for; matrix products, arithmetic and copies ran while one was open for 0% of the time, Pallas kernels for 38%

profile of v1, /device:TPU:0, one launch (start us, length us, event | category | flops | bytes accessed | tf_op | source)
XLA Modules:
  0.0 72.0 jit_solution(16219731860468865752)
XLA Ops:
  0.6 0.7 %copy.10.tgt = s32[64,1]{1,0:T(8,128)S(1)} copy(s32[64,1]{0,1:T(1,128)} %bitcast.15) | data formatting | bytes 512 | tf_op jit(solution)/shard_map/squeeze | solution.py:388
  1.4 0.0 copy-start.2
  1.4 1.6 %copy-done.2 = bf16[1,1,1,64,128,128]{5,4,3,2,1,0:T(8,128)(2,1)S(1)} copy-done((bf16[1,1,1,64,128,128]{5,4,3,2,1,0:T(8,128)(2,1)S(1)}, bf16[1,1,1,64,128,128]{5,4,3,2,1,0:T(8,128)(2,1)}, u32[]{:S(2)}) %copy-start.2) | copy-done | bytes 2097176
  3.0 0.0 copy-start.3
  3.0 0.8 %copy-done.3 = s32[128,128]{1,0:T(8,128)S(1)} copy-done((s32[128,128]{1,0:T(8,128)S(1)}, s32[128,128]{1,0:T(8,128)}, u32[]{:S(2)}) %copy-start.3) | copy-done | bytes 65560
  3.8 0.0 copy-start.5
  3.8 1.0 %copy-done.5 = f32[1,8,128,128]{3,2,1,0:T(8,128)S(1)} copy-done((f32[1,8,128,128]{3,2,1,0:T(8,128)S(1)}, f32[1,8,128,128]{3,2,1,0:T(8,128)}, u32[]{:S(2)}) %copy-start.5) | copy-done | bytes 524312
  4.8 0.0 copy-start.6
  4.9 0.7 copy-done.6
  5.5 0.0 copy-start.7
  5.5 0.7 copy-done.7
  6.2 0.0 copy-start.4
  6.2 2.9 %shard_map.86 = f32[16,72,128]{2,1,0:T(8,128)S(1)} custom-call(s32[64]{0:T(128)S(1)} %bitcast.12, s32[64,1]{1,0:T(8,128)S(1)} %copy.10.tgt, s32[64]{0:T(128)S(1)} %bitcast.13, s32[128,128]{1,0:T(8,128)S(1)} %copy-done.3, f32[1024,128]{1,0:T(8,128)S(1)} %bitcast.11, bf16[64,128,128]{2,1,0:T(8,128)(2,1)S(1)} %bitcast.10), custom_call_target="tpu_custom_call" | custom-call | flops 400000000 | bytes 4000000 | tf_op jit(solution)/shard_map/pallas_call | solution.py:74
  9.1 0.5 collective-permute-start
  9.6 1.8 %collective-permute-done = f32[16,72,128]{2,1,0:T(8,128)} collective-permute-done((f32[16,72,128]{2,1,0:T(8,128)S(1)}, f32[16,72,128]{2,1,0:T(8,128)}, u32[]{:S(2)}, u32[]{:S(2)}) %collective-permute-start) | collective-permute-done | bytes 589856 | tf_op jit(solution)/shard_map/ppermute | solution.py:396
  11.4 8.2 %all-to-all-start = ((f32[16,72,128]{2,1,0:T(8,128)}), f32[16,72,128]{2,1,0:T(8,128)S(1)}, u32[]{:S(2)}, u32[]{:S(2)}) async-start(f32[16,72,128]{2,1,0:T(8,128)} %collective-permute-done), calls=%async_computation | async-start | bytes 1179648 | tf_op jit(solution)/shard_map/all_to_all | solution.py:397
  19.6 0.0 copy-done.4
  19.6 0.0 copy-start
  19.6 2.2 %copy-done = f32[1,64,128,128]{3,2,1,0:T(8,128)S(1)} copy-done((f32[1,64,128,128]{3,2,1,0:T(8,128)S(1)}, f32[1,64,128,128]{3,2,1,0:T(8,128)}, u32[]{:S(2)}) %copy-start) | copy-done | bytes 4194328
  21.8 0.0 copy-start.1
  21.8 2.2 %shard_map.87 = (f32[136,128]{1,0:T(8,128)S(1)}, f32[136,128]{1,0:T(8,128)S(1)}, f32[136,128]{1,0:T(8,128)S(1)}, f32[136,128]{1,0:T(8,128)S(1)}) custom-call(s32[128,128]{1,0:T(8,128)S(1)} %copy-done.4, f32[64,128,128]{2,1,0:T(8,128)S(1)} %bitcast.8), custom_call_target="tpu_custom_call" | custom-call | flops 10000000 | bytes 4000000 | tf_op jit(solution)/shard_map/pallas_call | solution.py:140
  24.1 3.8 %collective-permute-start.2 = (f32[136,128]{1,0:T(8,128)S(1)}, f32[136,128]{1,0:T(8,128)S(1)}, u32[]{:S(2)}, u32[]{:S(2)}) collective-permute-start(f32[136,128]{1,0:T(8,128)S(1)} %get-tuple-element.8.up), channel_id=1, source_target_pairs={{4,0},{8,4},{12,8},{0,12},{5,1},{9,5},{13,9},{1,13},{6,2},{10,6},{... | collective-permute-start | bytes 208904 | tf_op jit(solution)/shard_map/ppermute | solution.py:403
  27.8 0.0 collective-permute-start.1
  27.8 2.4 %collective-permute-start.4 = (f32[136,128]{1,0:T(8,128)S(1)}, f32[136,128]{1,0:T(8,128)S(1)}, u32[]{:S(2)}, u32[]{:S(2)}) collective-permute-start(f32[136,128]{1,0:T(8,128)S(1)} %get-tuple-element.10.left), channel_id=1, source_target_pairs={{1,0},{2,1},{3,2},{0,3},{5,4},{6,5},{7,6},{4,7},{9,8},{10,9},{11,1... | collective-permute-start | bytes 208904 | tf_op jit(solution)/shard_map/ppermute | solution.py:405
  30.2 0.0 collective-permute-start.3
  30.2 1.9 %collective-permute-done.2.bottom = f32[136,128]{1,0:T(8,128)S(1)} collective-permute-done((f32[136,128]{1,0:T(8,128)S(1)}, f32[136,128]{1,0:T(8,128)S(1)}, u32[]{:S(2)}, u32[]{:S(2)}) %collective-permute-start.2) | collective-permute-done | bytes 69664 | tf_op jit(solution)/shard_map/ppermute | solution.py:403
  32.1 4.5 %collective-permute-done.1.top = f32[136,128]{1,0:T(8,128)S(1)} collective-permute-done((f32[136,128]{1,0:T(8,128)S(1)}, f32[136,128]{1,0:T(8,128)S(1)}, u32[]{:S(2)}, u32[]{:S(2)}) %collective-permute-start.1) | collective-permute-done | bytes 69664 | tf_op jit(solution)/shard_map/ppermute | solution.py:402
  36.6 2.3 %collective-permute-start.6 = (f32[128,128]{1,0:T(8,128)S(1)}, f32[128,128]{1,0:T(8,128)S(1)}, u32[]{:S(2)}, u32[]{:S(2)}) collective-permute-start(f32[128,128]{1,0:T(8,128)S(1)} %pad_maximum_fusion), channel_id=1, source_target_pairs={{1,0},{2,1},{3,2},{0,3},{5,4},{6,5},{7,6},{4,7},{9,8},{10,9},{11,1... | collective-permute-start | bytes 196616 | tf_op jit(solution)/shard_map/ppermute | solution.py:409
  38.9 0.0 collective-permute-start.5
  38.9 0.0 collective-permute-done.4.east
  38.9 0.0 collective-permute-done.3.west
  38.9 2.6 %collective-permute-done.6.ceast = f32[128,128]{1,0:T(8,128)S(1)} collective-permute-done((f32[128,128]{1,0:T(8,128)S(1)}, f32[128,128]{1,0:T(8,128)S(1)}, u32[]{:S(2)}, u32[]{:S(2)}) %collective-permute-start.6) | collective-permute-done | bytes 65568 | tf_op jit(solution)/shard_map/ppermute | solution.py:409
  41.6 2.5 %collective-permute-done.5.cwest = f32[128,128]{1,0:T(8,128)S(1)} collective-permute-done((f32[128,128]{1,0:T(8,128)S(1)}, f32[128,128]{1,0:T(8,128)S(1)}, u32[]{:S(2)}, u32[]{:S(2)}) %collective-permute-start.5) | collective-permute-done | bytes 65568 | tf_op jit(solution)/shard_map/ppermute | solution.py:408
  44.1 0.0 copy-done.1
  44.1 25.3 %shard_map.88.second = f32[64,128,128]{2,1,0:T(8,128)} custom-call(s32[128,128]{1,0:T(8,128)S(1)} %copy-done.4, f32[64,128,128]{2,1,0:T(8,128)S(1)} %bitcast.9, f32[136,128]{1,0:T(8,128)S(1)} %get-tuple-element.8.up, f32[136,128]{1,0:T(8,128)S(1)} %get-tuple-element.9.down, f32[136,128]{1,0:T(8,128)S(1)} %get-tuple-element.10.left, ...), custom_call_target="tpu_custom_call" | custom-call | flops 20000000 | bytes 10000000 | tf_op jit(solution)/shard_map/pallas_call | solution.py:302
  69.4 0.0 all-to-all-done.got
  69.4 2.6 %shard_map.89 = (f32[64,128,128]{2,1,0:T(8,128)}, f32[8,128,128]{2,1,0:T(8,128)}) custom-call(s32[128,128]{1,0:T(8,128)S(1)} %copy-done.4, f32[16,72,128]{2,1,0:T(8,128)S(1)} %all-to-all-done.got, f32[64,128,128]{2,1,0:T(8,128)} %shard_map.88.second), custom_call_target="tpu_custom_call", output_to_operand_aliasing={{0}: (2, {})} | custom-call | flops 100000000 | bytes 2000000 | tf_op jit(solution)/shard_map/pallas_call | solution.py:361
  (3 shorter events, 0.0 us)
Async XLA Ops:
  1.4 1.6 %copy-start.2 = (bf16[1,1,1,64,128,128]{5,4,3,2,1,0:T(8,128)(2,1)S(1)}, bf16[1,1,1,64,128,128]{5,4,3,2,1,0:T(8,128)(2,1)}, u32[]{:S(2)}) copy-start(bf16[1,1,1,64,128,128]{5,4,3,2,1,0:T(8,128)(2,1)} %param.10) | copy-start | bytes 6291460
  3.0 0.8 %copy-start.3 = (s32[128,128]{1,0:T(8,128)S(1)}, s32[128,128]{1,0:T(8,128)}, u32[]{:S(2)}) copy-start(s32[128,128]{1,0:T(8,128)} %mask.7) | copy-start | bytes 196612
  3.8 1.0 %copy-start.5 = (f32[1,8,128,128]{3,2,1,0:T(8,128)S(1)}, f32[1,8,128,128]{3,2,1,0:T(8,128)}, u32[]{:S(2)}) copy-start(f32[1,8,128,128]{3,2,1,0:T(8,128)} %param.8) | copy-start | bytes 1572868
  4.8 0.7 copy-start.6
  5.5 0.7 copy-start.7
  6.2 13.5 %copy-start.4 = (s32[128,128]{1,0:T(8,128)S(1)}, s32[128,128]{1,0:T(8,128)}, u32[]{:S(2)}) copy-start(s32[128,128]{1,0:T(8,128)} %mask.7) | copy-start | bytes 196612
  9.1 2.3 %collective-permute-start = (f32[16,72,128]{2,1,0:T(8,128)S(1)}, f32[16,72,128]{2,1,0:T(8,128)}, u32[]{:S(2)}, u32[]{:S(2)}) collective-permute-start(f32[16,72,128]{2,1,0:T(8,128)S(1)} %shard_map.86), channel_id=1, source_target_pairs={{0,16},{16,0},{1,17},{17,1},{2,18},{18,2},{3,19},{19,3},{4,20},{20... | collective-permute-start | bytes 1769480 | tf_op jit(solution)/shard_map/ppermute | solution.py:396
  11.4 58.1 %all-to-all-start = ((f32[16,72,128]{2,1,0:T(8,128)}), f32[16,72,128]{2,1,0:T(8,128)S(1)}, u32[]{:S(2)}, u32[]{:S(2)}) async-start(f32[16,72,128]{2,1,0:T(8,128)} %collective-permute-done), calls=%async_computation | async-start | bytes 1179648 | tf_op jit(solution)/shard_map/all_to_all | solution.py:397
  19.6 2.2 %copy-start = (f32[1,64,128,128]{3,2,1,0:T(8,128)S(1)}, f32[1,64,128,128]{3,2,1,0:T(8,128)}, u32[]{:S(2)}) copy-start(f32[1,64,128,128]{3,2,1,0:T(8,128)} %param.7) | copy-start | bytes 12582916
  21.8 22.3 %copy-start.1 = (f32[1,64,128,128]{3,2,1,0:T(8,128)S(1)}, f32[1,64,128,128]{3,2,1,0:T(8,128)}, u32[]{:S(2)}) copy-start(f32[1,64,128,128]{3,2,1,0:T(8,128)} %param.7) | copy-start | bytes 12582916
  24.1 8.0 %collective-permute-start.2 = (f32[136,128]{1,0:T(8,128)S(1)}, f32[136,128]{1,0:T(8,128)S(1)}, u32[]{:S(2)}, u32[]{:S(2)}) collective-permute-start(f32[136,128]{1,0:T(8,128)S(1)} %get-tuple-element.8.up), channel_id=1, source_target_pairs={{4,0},{8,4},{12,8},{0,12},{5,1},{9,5},{13,9},{1,13},{6,2},{10,6},{... | collective-permute-start | bytes 208904 | tf_op jit(solution)/shard_map/ppermute | solution.py:403
  27.8 8.7 %collective-permute-start.1 = (f32[136,128]{1,0:T(8,128)S(1)}, f32[136,128]{1,0:T(8,128)S(1)}, u32[]{:S(2)}, u32[]{:S(2)}) collective-permute-start(f32[136,128]{1,0:T(8,128)S(1)} %get-tuple-element.9.down), channel_id=1, source_target_pairs={{0,4},{4,8},{8,12},{12,0},{1,5},{5,9},{9,13},{13,1},{2,6},{6,10},{... | collective-permute-start | bytes 208904 | tf_op jit(solution)/shard_map/ppermute | solution.py:402
  27.8 11.1 %collective-permute-start.4 = (f32[136,128]{1,0:T(8,128)S(1)}, f32[136,128]{1,0:T(8,128)S(1)}, u32[]{:S(2)}, u32[]{:S(2)}) collective-permute-start(f32[136,128]{1,0:T(8,128)S(1)} %get-tuple-element.10.left), channel_id=1, source_target_pairs={{1,0},{2,1},{3,2},{0,3},{5,4},{6,5},{7,6},{4,7},{9,8},{10,9},{11,1... | collective-permute-start | bytes 208904 | tf_op jit(solution)/shard_map/ppermute | solution.py:405
  30.2 8.7 %collective-permute-start.3 = (f32[136,128]{1,0:T(8,128)S(1)}, f32[136,128]{1,0:T(8,128)S(1)}, u32[]{:S(2)}, u32[]{:S(2)}) collective-permute-start(f32[136,128]{1,0:T(8,128)S(1)} %get-tuple-element.11.right), channel_id=1, source_target_pairs={{0,1},{1,2},{2,3},{3,0},{4,5},{5,6},{6,7},{7,4},{8,9},{9,10},{10,1... | collective-permute-start | bytes 208904 | tf_op jit(solution)/shard_map/ppermute | solution.py:404
  36.6 5.0 %collective-permute-start.6 = (f32[128,128]{1,0:T(8,128)S(1)}, f32[128,128]{1,0:T(8,128)S(1)}, u32[]{:S(2)}, u32[]{:S(2)}) collective-permute-start(f32[128,128]{1,0:T(8,128)S(1)} %pad_maximum_fusion), channel_id=1, source_target_pairs={{1,0},{2,1},{3,2},{0,3},{5,4},{6,5},{7,6},{4,7},{9,8},{10,9},{11,1... | collective-permute-start | bytes 196616 | tf_op jit(solution)/shard_map/ppermute | solution.py:409
  38.9 5.2 %collective-permute-start.5 = (f32[128,128]{1,0:T(8,128)S(1)}, f32[128,128]{1,0:T(8,128)S(1)}, u32[]{:S(2)}, u32[]{:S(2)}) collective-permute-start(f32[128,128]{1,0:T(8,128)S(1)} %pad_maximum_fusion), channel_id=1, source_target_pairs={{0,1},{1,2},{2,3},{3,0},{4,5},{5,6},{6,7},{7,4},{8,9},{9,10},{10,1... | collective-permute-start | bytes 196616 | tf_op jit(solution)/shard_map/ppermute | solution.py:408

commit v2 on v1

v2 whole, which is shorter than its diff:
```python
import functools

import jax
import jax.numpy as jnp
from jax import lax
from jax.experimental import pallas as pl
from jax.experimental.pallas import tpu as pltpu
from jax.sharding import PartitionSpec as P

CAP = 8
FORCE = 0.5
HORIZ = (0.15, 0.12)
VERT = (0.1, 0.15)
MIB = 1024 * 1024
LIMIT = 60
ANY = pl.BlockSpec(memory_space=pl.ANY)
VMEM = pl.BlockSpec(memory_space=pltpu.VMEM)
SMEM = pl.BlockSpec(memory_space=pltpu.SMEM)


def params(mib):
    return pltpu.CompilerParams(vmem_limit_bytes=mib * MIB)


def wet_of(mask_ref):
    ocean = lax.axis_index("mp") == 1
    return jnp.where(ocean, mask_ref[...].astype(jnp.float32), 1.0)


def lanes(shape):
    return lax.broadcasted_iota(jnp.int32, shape, len(shape) - 1)


def send_kernel(
    ndev, ngy, chunk, group, tile_source, tile_target, tile_row, mask, surface, weights, state,
    out, up, down, left, right, wet,
    src, tgt, row, count, labels, mbuf, sbuf, wbuf, buf, sems, wsems, usems,
):
    lev, cx, cy = state.shape
    tiles = weights.shape[0]
    small = [
        pltpu.make_async_copy(a, b, sems.at[i])
        for i, (a, b) in enumerate(
            ((tile_source, src), (tile_target, tgt), (tile_row, row), (mask, mbuf), (surface, sbuf))
        )
    ]
    for copy in small:
        copy.start()
    wcopies, ucopies = [], []
    for i in range(tiles // chunk):
        part = pl.ds(i * chunk, chunk)
        wcopies.append(pltpu.make_async_copy(weights.at[part], wbuf.at[part], wsems.at[i]))
        wcopies[-1].start()
    for i in range(lev // group):
        part = pl.ds(i * group, group)
        ucopies.append(pltpu.make_async_copy(state.at[part], buf.at[part], usems.at[i]))
        ucopies[-1].start()
    out[...] = jnp.zeros_like(out)
    labels[...] = jnp.zeros_like(labels)
    for d in range(ndev):
        count[d] = 0
    me = lax.axis_index("gx") * ngy + lax.axis_index("gy")
    place = lax.broadcasted_iota(jnp.int32, (8, 128), 0) * 128 + lanes((8, 128))
    for copy in small:
        copy.wait()
    wet[...] = wet_of(mbuf)

    def one(t, _):
        s, d = src[t], tgt[t]
        rank = count[d]
        count[d] = rank + 1
        picked = sbuf[pl.ds(s, 8, stride=cx), :] * wet[pl.ds(s, 1), :]
        out[d, pl.ds(rank * 8, 8), :] = lax.dot_general(
            picked.astype(jnp.bfloat16),
            wbuf[t],
            (((1,), (1,)), ((), ())),
            preferred_element_type=jnp.float32,
        )
        label = (row[t] + 1).astype(jnp.float32)
        labels[d] = jnp.where(place == me * CAP + rank, label, labels[d])
        return 0

    for i in range(tiles // chunk):
        wcopies[i].wait()
        lax.fori_loop(i * chunk, (i + 1) * chunk, one, 0, unroll=True)
    for d in range(ndev):
        out[d, 64:72, :] = labels[d]

    turned = jnp.transpose(wet[...])
    up[2 * lev :, :] = jnp.broadcast_to(wet[0:1, :], (8, cy))
    down[2 * lev :, :] = jnp.broadcast_to(wet[cx - 1 :, :], (8, cy))
    left[cx:, :] = jnp.broadcast_to(turned[0:1, :], (8, cx))
    right[cx:, :] = jnp.broadcast_to(turned[cy - 1 :, :], (8, cx))
    strip = 32
    flat = buf.reshape(lev * cx, cy)
    lane = lanes((strip, cy))
    for i in range(lev // group):
        ucopies[i].wait()
        for dst, off, r in ((up, 0, 0), (up, lev, 1), (down, 0, cx - 1), (down, lev, cx - 2)):
            dst[pl.ds(off + i * group, group), :] = (
                flat[pl.ds(i * group * cx + r, group, stride=cx), :] * wet[r : r + 1, :]
            )
        for b in range(cx // strip):
            rows = pl.ds(b * strip, strip)
            if i == 0:
                lo = hi = jnp.zeros((strip, cy), jnp.float32)
            else:
                lo, hi = left[rows, :], right[rows, :]
            for l in range(i * group, (i + 1) * group):
                moved = pltpu.roll(buf[l, rows, :], (2 * l + 2) % cy, 1)
                at = (2 * l + 2) % cy
                lo = jnp.where((lane == at) | (lane == at + 1), moved, lo)
                hi = jnp.where((lane == 2 * l) | (lane == 2 * l + 1), moved, hi)
            if i == lev // group - 1:
                edge = wet[rows, :]
                first, second = edge[:, 0:1], edge[:, 1:2]
                lo = lo * jnp.where(lane % 2 == 0, first, second)
                first, second = edge[:, cy - 2 : cy - 1], edge[:, cy - 1 :]
                hi = hi * jnp.where(lane % 2 == 0, first, second)
            left[rows, :] = lo
            right[rows, :] = hi


def outgoing(tile_source, tile_target, tile_row, mask, surface, weights, state, ngx, ngy):
    tiles = weights.shape[0]
    lev, cx, cy = state.shape
    ndev, chunk, group = ngx * ngy, 32, 16
    message = jax.ShapeDtypeStruct((2 * lev + 8, cy), jnp.float32)
    columns = jax.ShapeDtypeStruct((cx + 8, cy), jnp.float32)
    return pl.pallas_call(
        functools.partial(send_kernel, ndev, ngy, chunk, group),
        out_shape=(
            jax.ShapeDtypeStruct((ndev, 72, 128), jnp.float32),
            message,
            message,
            columns,
            columns,
            jax.ShapeDtypeStruct(mask.shape, jnp.float32),
        ),
        in_specs=[ANY] * 7,
        out_specs=(VMEM,) * 6,
        scratch_shapes=[
            pltpu.SMEM((tiles,), jnp.int32),
            pltpu.SMEM((tiles,), jnp.int32),
            pltpu.SMEM((tiles,), jnp.int32),
            pltpu.SMEM((ndev,), jnp.int32),
            pltpu.VMEM((ndev, 8, 128), jnp.float32),
            pltpu.VMEM(mask.shape, jnp.int32),
            pltpu.VMEM(surface.shape, jnp.float32),
            pltpu.VMEM(weights.shape, weights.dtype),
            pltpu.VMEM(state.shape, jnp.float32),
            pltpu.SemaphoreType.DMA((5,)),
            pltpu.SemaphoreType.DMA((tiles // chunk,)),
            pltpu.SemaphoreType.DMA((lev // group,)),
        ],
        compiler_params=params(LIMIT),
        cost_estimate=pl.CostEstimate(flops=10**8, bytes_accessed=8 * 10**6, transcendentals=0),
    )(tile_source, tile_target, tile_row, mask, surface, weights, state)


def shifted(x, by, axis):
    size = x.shape[axis]
    moved = pltpu.roll(x, by % size, axis)
    index = lax.broadcasted_iota(jnp.int32, x.shape, axis)
    return jnp.where(index == (0 if by == 1 else size - 1), 0.0, moved)


PAD = 8


def ring_kernel(ngx, ngy, lev, wet, up, down, left, right, east, west, bottom, top, ring, gains, rows):
    cx, cy = wet.shape
    ocean = lax.axis_index("mp") == 1
    horiz = jnp.where(ocean, HORIZ[1], HORIZ[0]).astype(jnp.float32)
    vert = jnp.where(ocean, VERT[1], VERT[0]).astype(jnp.float32)
    centre = 1.0 - 4.0 * horiz - 2.0 * vert
    gx, gy = lax.axis_index("gx"), lax.axis_index("gy")
    has = lambda c: jnp.where(c, 1.0, 0.0).astype(jnp.float32)
    has_top, has_bottom = has(gx > 0), has(gx < ngx - 1)
    has_west, has_east = has(gy > 0), has(gy < ngy - 1)

    lane = lanes((lev, cy))
    edge_lane = lanes((1, cy))
    for msg, own, flag, i in ((top, up, has_top, 0), (bottom, down, has_bottom, 1)):
        rows[i * lev : (i + 1) * lev, :] = msg[0:lev, :]
        near = msg[0:lev, :] * flag
        far = msg[lev : 2 * lev, :] * flag
        side = shifted(near, 1, 1) + shifted(near, -1, 1)
        end = i * (cx - 1)
        beside = jnp.where(
            edge_lane == 0, west[cx : cx + 1, end : end + 1] * has_west, 0.0
        ) + jnp.where(edge_lane == cy - 1, east[cx : cx + 1, end : end + 1] * has_east, 0.0)
        reach = jnp.where(edge_lane == 0, has_west, jnp.where(edge_lane == cy - 1, has_east, 0.0))
        total = (msg[2 * lev : 2 * lev + 1, :] * flag + beside) * (wet[end : end + 1, :] * reach)
        gains[8 * i : 8 * i + 8, :] = jnp.broadcast_to(total * (horiz * horiz * flag), (8, cy))
        gain = msg[2 * lev : 2 * lev + 1, :] * (horiz * flag)
        outer = (
            centre * near
            + gain * (side + far + own[0:lev, :])
            + vert * (shifted(near, 1, 0) + shifted(near, -1, 0))
        )
        ring[2 * i * lev : (2 * i + 1) * lev, :] = near
        ring[(2 * i + 1) * lev : (2 * i + 2) * lev, :] = outer

    lane = lanes((cx, cy))
    odd = lane % 2 == 1
    west_cols = west[0:cx, :] * has_west
    east_cols = east[0:cx, :] * has_east
    w_gain = jnp.transpose(jnp.broadcast_to(west[cx : cx + 1, :], (cx, cx))) * (horiz * has_west)
    e_gain = jnp.transpose(jnp.broadcast_to(east[cx : cx + 1, :], (cx, cx))) * (horiz * has_east)
    merged = jnp.where(odd, west_cols, east_cols)
    ring[4 * lev : 4 * lev + cx, :] = pltpu.roll(jnp.where(odd, merged, pltpu.roll(merged, cy - 2, 1)), cy - 1, 1)
    beside = (
        jnp.where(odd, pltpu.roll(west_cols, 1, 1), pltpu.roll(east_cols, cy - 1, 1))
        + jnp.where(odd, pltpu.roll(left[0:cx, :], cy - 1, 1), pltpu.roll(right[0:cx, :], 1, 1))
    )
    above, below = shifted(merged, 1, 0), shifted(merged, -1, 0)
    less = jnp.where((lane == 1) | (lane == 2), 0.0, pltpu.roll(merged, 2, 1))
    more = jnp.where((lane == cy - 1) | (lane == 0), 0.0, pltpu.roll(merged, cy - 2, 1))
    merged = (
        centre * merged
        + jnp.where(odd, w_gain, e_gain) * (beside + above + below)
        + vert * (less + more)
    )
    ring[4 * lev + cx :, :] = pltpu.roll(jnp.where(odd, merged, pltpu.roll(merged, cy - 2, 1)), cy - 1, 1)


def outer_ring(wet, messages, lev, ngx, ngy):
    cx, cy = wet.shape
    return pl.pallas_call(
        functools.partial(ring_kernel, ngx, ngy, lev),
        out_shape=(
            jax.ShapeDtypeStruct((4 * lev + 2 * cx, cy), jnp.float32),
            jax.ShapeDtypeStruct((16, cy), jnp.float32),
            jax.ShapeDtypeStruct((2 * lev, cy), jnp.float32),
        ),
        in_specs=[VMEM] * 9,
        out_specs=(VMEM, VMEM, VMEM),
        compiler_params=params(LIMIT),
        cost_estimate=pl.CostEstimate(flops=10**11, bytes_accessed=10**8, transcendentals=0),
    )(wet, *messages)


def stencil_kernel(
    group, wet, state, ring, out, hwet, one, two, rbuf, res, sems, osems,
):
    lev, cx, cy = state.shape
    pieces = lev // group
    fetch = pltpu.make_async_copy(ring, rbuf, sems.at[pieces])
    fetch.start()
    copies = []
    for i in range(pieces):
        part = pl.ds(i * group, group)
        copies.append(
            pltpu.make_async_copy(
                state.at[part], one.at[pl.ds(i * group + 1, group), pl.ds(PAD, cx), :], sems.at[i]
            )
        )
        copies[-1].start()
    ocean = lax.axis_index("mp") == 1
    horiz = jnp.where(ocean, HORIZ[1], HORIZ[0]).astype(jnp.float32)
    vert = jnp.where(ocean, VERT[1], VERT[0]).astype(jnp.float32)
    centre = 1.0 - 4.0 * horiz - 2.0 * vert
    hwet[...] = wet[...] * horiz
    lane = lanes((cx, cy))
    height = cx + 2 * PAD
    flat_one = one.reshape((lev + 2) * height, cy)
    flat_two = two.reshape((lev + 2) * height, cy)
    fetch.wait()
    for buf, off, at in (
        (flat_one, 0, PAD - 1),
        (flat_two, lev, PAD - 1),
        (flat_one, 2 * lev, PAD + cx),
        (flat_two, 3 * lev, PAD + cx),
    ):
        buf[pl.ds(height + at, lev, stride=height), :] = rbuf[off : off + lev, :]
    for buf in (one, two):
        buf[0] = jnp.zeros((height, cy), jnp.float32)
        buf[lev + 1] = jnp.zeros((height, cy), jnp.float32)

    def mask_level(l, _):
        one[l + 1, PAD : PAD + cx, :] = one[l + 1, PAD : PAD + cx, :] * wet[...]
        return 0

    ends = (lane == 0) | (lane == cy - 1)
    apart = lax.broadcasted_iota(jnp.int32, (cy, cy), 0) - lanes((cy, cy))
    pairs = jnp.where((apart == 1) | (apart == -1), 1.0, 0.0).astype(jnp.bfloat16)
    pairs = jnp.concatenate([pairs, pairs], axis=0)

    def beside_of(here):
        high = here.astype(jnp.bfloat16)
        low = (here - high.astype(jnp.float32)).astype(jnp.bfloat16)
        both = jnp.concatenate([high, low], axis=1)
        return jnp.dot(both, pairs, preferred_element_type=jnp.float32)

    def step(buf, sides, l, j):
        here = buf[l + 1, PAD : PAD + cx, :]
        edge = pltpu.roll(sides, (cy - 2 * j) % cy, 1)
        around = (
            jnp.where(ends, edge, 0.0)
            + beside_of(here)
            + buf[l + 1, PAD - 1 : PAD - 1 + cx, :]
            + buf[l + 1, PAD + 1 : PAD + 1 + cx, :]
        )
        column = buf[l, PAD : PAD + cx, :] + buf[l + 2, PAD : PAD + cx, :]
        return centre * here + hwet[...] * around + vert * column

    def first_levels(start, count, turn):
        sides = pltpu.roll(rbuf[4 * lev : 4 * lev + cx, :], lax.rem(2 * cy - 2 * start, cy), 1)
        for j in range(count):
            two[start + j + 1, PAD : PAD + cx, :] = step(one, sides, start + j, j)

    def second_levels(start, count):
        sides = pltpu.roll(rbuf[4 * lev + cx :, :], lax.rem(2 * cy - 2 * start, cy), 1)
        for j in range(count):
            res[start + j] = step(two, sides, start + j, j)

    def arrive(i):
        pltpu.make_async_copy(
            state.at[pl.ds(i * group, group)],
            one.at[pl.ds(i * group + 1, group), pl.ds(PAD, cx), :],
            sems.at[i],
        ).wait()
        for j in range(group):
            mask_level(i * group + j, 0)

    def leave(i):
        part = pl.ds(i * group, group)
        return pltpu.make_async_copy(res.at[part], out.at[part], osems.at[i])

    arrive(0)
    first_levels(0, group - 1, 0)

    def middle(i, _):
        arrive(i)
        first_levels(i * group - 1, group, 0)
        second_levels((i - 1) * group, group)
        leave(i - 1).start()
        return 0

    lax.fori_loop(1, pieces, middle, 0)
    first_levels(lev - 1, 1, 0)
    second_levels(lev - group, group)
    leave(pieces - 1).start()
    for i in range(pieces):
        leave(i).wait()


def two_steps(wet, state, ring):
    lev, cx, cy = state.shape
    group = 8
    padded = (lev + 2, cx + 2 * PAD, cy)
    return pl.pallas_call(
        functools.partial(stencil_kernel, group),
        out_shape=jax.ShapeDtypeStruct(state.shape, jnp.float32),
        in_specs=[VMEM, ANY, ANY],
        out_specs=ANY,
        scratch_shapes=[
            pltpu.VMEM((cx, cy), jnp.float32),
            pltpu.VMEM(padded, jnp.float32),
            pltpu.VMEM(padded, jnp.float32),
            pltpu.VMEM(ring.shape, jnp.float32),
            pltpu.VMEM(state.shape, jnp.float32),
            pltpu.SemaphoreType.DMA((lev // group + 1,)),
            pltpu.SemaphoreType.DMA((lev // group,)),
        ],
        compiler_params=params(LIMIT),
        cost_estimate=pl.CostEstimate(flops=10**6, bytes_accessed=10**5, transcendentals=0),
    )(wet, state, ring)


def collect_kernel(
    wet, gains, cwest, ceast, got, second, out, received, level, upper, lower, onehot, sums, sems, rsems
):
    ndev = got.shape[0]
    fields, cx, cy = received.shape
    lev = second.shape[0]
    slots = ndev * CAP

    def move(i, back):
        deep = pl.ds(1, lev - 1)
        here = (level, upper, lower)[i]
        there = (
            lambda r: r.at[0],
            lambda r: r.at[deep, pl.ds(0, 8), :],
            lambda r: r.at[deep, pl.ds(cx - 8, 8), :],
        )[i]
        if back:
            return pltpu.make_async_copy(here, there(out), sems.at[i])
        return pltpu.make_async_copy(there(second), here, sems.at[i])

    def leave(k):
        return pltpu.make_async_copy(sums.at[k], received.at[k], rsems.at[k])

    for i in range(3):
        move(i, False).start()
    flat = got.reshape(ndev * 72, 128)
    labels = flat[64:72, :]
    for s in range(1, ndev):
        labels = labels + flat[s * 72 + 64 : s * 72 + 72, :]
    labels = labels.astype(jnp.int32)
    want = lax.broadcasted_iota(jnp.int32, (cx, 128), 0) + 1
    wide = jnp.concatenate([labels[q : q + 1, :] == want for q in range(slots // 128)], axis=1)
    hot = jnp.where(wide, 1.0, 0.0).astype(jnp.bfloat16)
    onehot[:, 0:slots] = hot
    onehot[:, slots:] = hot
    corners = []
    lane = lanes((lev, cy))
    for i, off in ((0, 0), (1, lev)):
        diagonal = jnp.where(
            lane == 0,
            pltpu.roll(cwest[off : off + lev, :], 1, 1),
            pltpu.roll(ceast[off : off + lev, :], cy - 1, 1),
        )
        corners.append(diagonal * gains[8 * i : 8 * i + 1, :])
    for k in range(fields):
        x = jnp.concatenate([flat[pl.ds(s * 72 + k, CAP, stride=8), :] for s in range(ndev)], axis=0)
        high = x.astype(jnp.bfloat16)
        low = (x - high.astype(jnp.float32)).astype(jnp.bfloat16)
        sums[k] = jnp.dot(
            onehot[...], jnp.concatenate([high, low], axis=0), preferred_element_type=jnp.float32
        )
        leave(k).start()
        if k == 0:
            move(0, False).wait()
            level[...] = level[...] + FORCE * wet[...] * sums[0]
            level[0:1, :] = level[0:1, :] + corners[0][0:1, :]
            level[cx - 1 :, :] = level[cx - 1 :, :] + corners[1][0:1, :]
            move(0, True).start()
            for i, edge, r in ((1, upper, 0), (2, lower, 7)):
                move(i, False).wait()
                rows = edge.reshape((lev - 1) * 8, cy)
                at = pl.ds(r, lev - 1, stride=8)
                rows[at, :] = rows[at, :] + corners[i - 1][1:, :]
                move(i, True).start()
    for i in range(3):
        move(i, True).wait()
    for k in range(fields):
        leave(k).wait()


def collect(wet, gains, corners, got, second, fields):
    ndev = got.shape[0]
    cx, cy = wet.shape
    lev = second.shape[0]
    return pl.pallas_call(
        collect_kernel,
        out_shape=(
            jax.ShapeDtypeStruct(second.shape, jnp.float32),
            jax.ShapeDtypeStruct((fields, cx, cy), jnp.float32),
        ),
        in_specs=[VMEM] * 5 + [ANY],
        out_specs=(ANY, ANY),
        scratch_shapes=[
            pltpu.VMEM((cx, cy), jnp.float32),
            pltpu.VMEM((lev - 1, 8, cy), jnp.float32),
            pltpu.VMEM((lev - 1, 8, cy), jnp.float32),
            pltpu.VMEM((cx, 2 * ndev * CAP), jnp.bfloat16),
            pltpu.VMEM((fields, cx, cy), jnp.float32),
            pltpu.SemaphoreType.DMA((3,)),
            pltpu.SemaphoreType.DMA((fields,)),
        ],
        input_output_aliases={5: 0},
        compiler_params=params(16),
        cost_estimate=pl.CostEstimate(flops=10**8, bytes_accessed=2 * 10**6, transcendentals=0),
    )(wet, gains, *corners, got, second)


def local(states, surface, land_mask, tile_weights, tile_source, tile_target, tile_row):
    ngx, ngy = lax.axis_size("gx"), lax.axis_size("gy")
    ndev = ngx * ngy
    state, fields = states[0], surface.shape[1]
    cx, cy = land_mask.shape
    lev = state.shape[0]
    ahead = lambda n: [(i, (i + 1) % n) for i in range(n)]
    behind = lambda n: [((i + 1) % n, i) for i in range(n)]
    buckets, up, down, left, right, wet = outgoing(
        tile_source[0, 0, 0],
        tile_target[0, 0, 0, :, 0],
        tile_row[0, 0, 0],
        land_mask,
        surface.reshape(fields * cx, cy),
        tile_weights[0, 0, 0],
        state,
        ngx,
        ngy,
    )
    top = lax.ppermute(down, "gx", ahead(ngx))
    bottom = lax.ppermute(up, "gx", behind(ngx))
    west = lax.ppermute(right, "gy", ahead(ngy))
    east = lax.ppermute(left, "gy", behind(ngy))
    buckets = lax.ppermute(buckets, "mp", [(0, 1), (1, 0)])
    got = lax.all_to_all(buckets, ("gx", "gy"), split_axis=0, concat_axis=0, tiled=True)
    messages = (up, down, left, right, east, west, bottom, top)
    ring, gains, rows = outer_ring(wet, messages, lev, ngx, ngy)
    corners = (lax.ppermute(rows, "gy", ahead(ngy)), lax.ppermute(rows, "gy", behind(ngy)))
    second = two_steps(wet, state, ring)
    new_state, received = collect(wet, gains, corners, got, second, fields)
    return new_state[None], received[None]


def solution(mesh):
    return jax.shard_map(
        local,
        mesh=mesh,
        in_specs=(
            P("mp", None, "gx", "gy"),
            P("mp", None, "gx", "gy"),
            P("gx", "gy"),
            P("mp", "gx", "gy", None, None, None),
            P("mp", "gx", "gy", None),
            P("mp", "gx", "gy", None, None),
            P("mp", "gx", "gy", None),
        ),
        out_specs=(P("mp", None, "gx", "gy"), P("mp", None, "gx", "gy")),
        check_vma=False,
    )
```

time: 72.5 us -> 40.2 us (0.55)
  Pallas kernels: 33.1 us -> 19.1 us
  waiting for transfers between devices: 13.3 us -> 1.37 us
  local copies, waits for them, and re-layouts: 7.72 us -> 0.64 us
  starting transfers between devices: 17.2 us -> 18 us
    pallas_call x3, Pallas kernels: 30.5 us -> 16.8 us  [the longest x1 8.52 us: two_steps(): pl.pallas_call(functools.partial(stencil_kernel, group), out_shape=jax.Sh...]
    unnamed x16 -> x12, local copies, waits for them, and re-layouts: 6.97 us -> 0.64 us
    ppermute x2, waiting for transfers between devices: 5.15 us -> 0.01 us  [the longest x1 0.01 us: local(): lax.ppermute(rows, 'gy', ahead(ngy))]
    ppermute x1, waiting for transfers between devices: 4.52 us -> 0.01 us  [local(): top = lax.ppermute(down, 'gx', ahead(ngx))]
    ppermute x1, waiting for transfers between devices: 1.85 us -> 0.01 us  [local(): bottom = lax.ppermute(up, 'gx', behind(ngx))]
    ppermute x1, waiting for transfers between devices: 1.76 us -> 0.01 us  [local(): buckets = lax.ppermute(buckets, 'mp', [(0, 1), (1, 0)])]
    all_to_all x1, waiting for transfers between devices: 0.01 us -> 1.35 us  [local(): lax.all_to_all(buckets, ('gx', 'gy'), split_axis=0, concat_axis=0, tiled=...]
    ppermute x1, starting transfers between devices: 3.78 us -> 4.65 us  [local(): bottom = lax.ppermute(up, 'gx', behind(ngx))]
  transfers between devices with their start and end apart: 8 -> 8, of which waited for: 5 -> 1; matrix products, arithmetic and copies ran while one was open for 0% -> 0% of each run, Pallas kernels for 38% -> 27%
where the time goes in v2:
time: 40.2 us; the launch traced here: 39.9 us
  Pallas kernels  19.1 us (48%)
  starting transfers between devices  18 us (45%)
  waiting for transfers between devices  1.37 us (3%)
  between operations  0.74 us (2%)
  local copies, waits for them, and re-layouts  0.64 us (2%)
    pallas_call x1, Pallas kernels, two_steps(): pl.pallas_call(functools.partial(stencil_kernel, group), out_shape=jax.Sh...  8.52 us
    all_to_all x1, starting transfers between devices, local(): lax.all_to_all(buckets, ('gx', 'gy'), split_axis=0, concat_axis=0, tiled=...  7.56 us
    pallas_call x1, Pallas kernels, outgoing(): pl.pallas_call(functools.partial(send_kernel, ndev, ngy, chunk, group), o...  5.95 us
    ppermute x1, starting transfers between devices, local(): bottom = lax.ppermute(up, 'gx', behind(ngx))  4.65 us
    ppermute x1, starting transfers between devices, local(): lax.ppermute(rows, 'gy', behind(ngy))  2.82 us
    ppermute x1, starting transfers between devices, local(): east = lax.ppermute(left, 'gy', behind(ngy))  2.45 us
    pallas_call x1, Pallas kernels, outer_ring(): pl.pallas_call(functools.partial(ring_kernel, ngx, ngy, lev), out_shape=(...  2.33 us
    pallas_call x1, Pallas kernels, collect(): pl.pallas_call(collect_kernel, out_shape=(jax.ShapeDtypeStruct(second.sha...  2.32 us
  transfers between devices with their start and end apart: 8, of which 1 were waited for; matrix products, arithmetic and copies ran while one was open for 0% of the time, Pallas kernels for 27%

profile of v2, /device:TPU:0, one launch (start us, length us, event | category | flops | bytes accessed | tf_op | source)
XLA Modules:
  0.0 39.9 jit_solution(17479905464560906655)
XLA Ops:
  0.6 5.9 %shard_map.86 = (f32[16,72,128]{2,1,0:T(8,128)}, f32[136,128]{1,0:T(8,128)}, f32[136,128]{1,0:T(8,128)}, f32[136,128]{1,0:T(8,128)}, f32[136,128]{1,0:T(8,128)}, /*index=5*/f32[128,128]{1,0:T(8,128)}) custom-call(s32[64]{0:T(128)} %bitcast.13, s32[64]{0:T(128)} %bitcast.14, s32[64]{0:T(128)} %bitcast.15, s32[128,128]{1,0:T(8,128)} %mask.1, ...), custom_call_target="tpu_custom_call" | custom-call | flops 100000000 | bytes 8000000 | tf_op jit(solution)/shard_map/pallas_call | solution.py:130
  6.6 0.5 %collective-permute-start.6 = (f32[16,72,128]{2,1,0:T(8,128)}, f32[16,72,128]{2,1,0:T(8,128)}, u32[]{:S(2)}, u32[]{:S(2)}) collective-permute-start(f32[16,72,128]{2,1,0:T(8,128)} %get-tuple-element.20), channel_id=1, source_target_pairs={{0,16},{16,0},{1,17},{17,1},{2,18},{18,2},{3,19},{19,3},{4,20},{20... | collective-permute-start | bytes 1769480 | tf_op jit(solution)/shard_map/ppermute | solution.py:492
  7.1 4.7 %collective-permute-start.2 = (f32[136,128]{1,0:T(8,128)}, f32[136,128]{1,0:T(8,128)S(1)}, u32[]{:S(2)}, u32[]{:S(2)}) collective-permute-start(f32[136,128]{1,0:T(8,128)} %get-tuple-element.14.up), channel_id=1, source_target_pairs={{4,0},{8,4},{12,8},{0,12},{5,1},{9,5},{13,9},{1,13},{6,2},{10,6},{... | collective-permute-start | bytes 208904 | tf_op jit(solution)/shard_map/ppermute | solution.py:489
  11.8 0.0 collective-permute-start.3
  11.8 2.5 %collective-permute-start = (f32[136,128]{1,0:T(8,128)}, f32[136,128]{1,0:T(8,128)S(1)}, u32[]{:S(2)}, u32[]{:S(2)}) collective-permute-start(f32[136,128]{1,0:T(8,128)} %get-tuple-element.16.left), channel_id=1, source_target_pairs={{1,0},{2,1},{3,2},{0,3},{5,4},{6,5},{7,6},{4,7},{9,8},{10,9},{11,1... | collective-permute-start | bytes 208904 | tf_op jit(solution)/shard_map/ppermute | solution.py:491
  14.2 0.0 collective-permute-start.1
  14.2 0.0 collective-permute-done.6
  14.2 7.6 %all-to-all-start = ((f32[16,72,128]{2,1,0:T(8,128)}), f32[16,72,128]{2,1,0:T(8,128)S(1)}, u32[]{:S(2)}, u32[]{:S(2)}) async-start(f32[16,72,128]{2,1,0:T(8,128)} %collective-permute-done.6), calls=%async_computation | async-start | bytes 1179648 | tf_op jit(solution)/shard_map/all_to_all | solution.py:493
  21.8 0.0 collective-permute-done.2.bottom
  21.8 0.0 copy-start.2
  21.8 0.0 collective-permute-done.3.top
  21.8 0.0 copy-start.3
  21.8 0.0 collective-permute-done.east
  21.9 0.0 copy-start.4
  21.9 0.0 collective-permute-done.1.west
  21.9 0.0 copy-start.5
  21.9 0.5 %copy-done.2 = f32[136,128]{1,0:T(8,128)} copy-done((f32[136,128]{1,0:T(8,128)}, f32[136,128]{1,0:T(8,128)S(1)}, u32[]{:S(2)}) %copy-start.2) | copy-done | bytes 69656
  22.4 0.0 copy-done.3
  22.5 0.0 copy-done.4
  22.5 0.0 copy-done.5
  22.5 2.3 %shard_map.87 = (f32[512,128]{1,0:T(8,128)}, f32[16,128]{1,0:T(8,128)}, f32[128,128]{1,0:T(8,128)}) custom-call(f32[128,128]{1,0:T(8,128)} %get-tuple-element.13.wet, f32[136,128]{1,0:T(8,128)} %get-tuple-element.14.up, f32[136,128]{1,0:T(8,128)} %get-tuple-element.15.down, f32[136,128]{1,0:T(8,128)} %get-tuple-element.16.left, ...), custom_call_target="tpu_custom_call" | custom-call | flops 99999997952 | bytes 100000000 | tf_op jit(solution)/shard_map/pallas_call | solution.py:230
  24.8 2.8 %collective-permute-start.5 = (f32[128,128]{1,0:T(8,128)}, f32[128,128]{1,0:T(8,128)S(1)}, u32[]{:S(2)}, u32[]{:S(2)}) collective-permute-start(f32[128,128]{1,0:T(8,128)} %get-tuple-element.19), channel_id=1, source_target_pairs={{1,0},{2,1},{3,2},{0,3},{5,4},{6,5},{7,6},{4,7},{9,8},{10,9},{11,1... | collective-permute-start | bytes 196616 | tf_op jit(solution)/shard_map/ppermute | solution.py:496
  27.7 0.0 collective-permute-start.4
  27.7 0.0 copy-start
  27.7 0.0 copy-start.1
  27.7 8.5 %shard_map.88.second = f32[64,128,128]{2,1,0:T(8,128)} custom-call(f32[128,128]{1,0:T(8,128)} %get-tuple-element.13.wet, f32[64,128,128]{2,1,0:T(8,128)} %bitcast.9, f32[512,128]{1,0:T(8,128)} %get-tuple-element.21.ring), custom_call_target="tpu_custom_call" | custom-call | flops 1000000 | bytes 100000 | tf_op jit(solution)/shard_map/pallas_call | solution.py:353
  36.2 0.0 collective-permute-done.5.ceast
  36.2 0.0 collective-permute-done.4.cwest
  36.2 1.4 %all-to-all-done.got = f32[16,72,128]{2,1,0:T(8,128)S(1)} async-done(((f32[16,72,128]{2,1,0:T(8,128)}), f32[16,72,128]{2,1,0:T(8,128)S(1)}, u32[]{:S(2)}, u32[]{:S(2)}) %all-to-all-start) | async-done | bytes 589856 | tf_op jit(solution)/shard_map/all_to_all | solution.py:493
  37.6 0.0 copy-done
  37.6 0.0 copy-done.1
  37.6 2.3 %shard_map.89 = (f32[64,128,128]{2,1,0:T(8,128)}, f32[8,128,128]{2,1,0:T(8,128)}) custom-call(f32[128,128]{1,0:T(8,128)S(1)} %copy-done, f32[16,128]{1,0:T(8,128)S(1)} %copy-done.1, f32[128,128]{1,0:T(8,128)S(1)} %collective-permute-done.4.cwest, f32[128,128]{1,0:T(8,128)S(1)} %collective-permute-done.5.ceast, ...), custom_call_target="tpu_custom_call", output_to_operand_aliasing={{0}: (5, {})} | custom-call | flops 100000000 | bytes 2000000 | tf_op jit(solution)/shard_map/pallas_call | solution.py:446
Async XLA Ops:
  6.6 7.6 %collective-permute-start.6 = (f32[16,72,128]{2,1,0:T(8,128)}, f32[16,72,128]{2,1,0:T(8,128)}, u32[]{:S(2)}, u32[]{:S(2)}) collective-permute-start(f32[16,72,128]{2,1,0:T(8,128)} %get-tuple-element.20), channel_id=1, source_target_pairs={{0,16},{16,0},{1,17},{17,1},{2,18},{18,2},{3,19},{19,3},{4,20},{20... | collective-permute-start | bytes 1769480 | tf_op jit(solution)/shard_map/ppermute | solution.py:492
  7.1 14.7 %collective-permute-start.2 = (f32[136,128]{1,0:T(8,128)}, f32[136,128]{1,0:T(8,128)S(1)}, u32[]{:S(2)}, u32[]{:S(2)}) collective-permute-start(f32[136,128]{1,0:T(8,128)} %get-tuple-element.14.up), channel_id=1, source_target_pairs={{4,0},{8,4},{12,8},{0,12},{5,1},{9,5},{13,9},{1,13},{6,2},{10,6},{... | collective-permute-start | bytes 208904 | tf_op jit(solution)/shard_map/ppermute | solution.py:489
  11.8 10.1 %collective-permute-start.3 = (f32[136,128]{1,0:T(8,128)}, f32[136,128]{1,0:T(8,128)S(1)}, u32[]{:S(2)}, u32[]{:S(2)}) collective-permute-start(f32[136,128]{1,0:T(8,128)} %get-tuple-element.15.down), channel_id=1, source_target_pairs={{0,4},{4,8},{8,12},{12,0},{1,5},{5,9},{9,13},{13,1},{2,6},{6,10},{... | collective-permute-start | bytes 208904 | tf_op jit(solution)/shard_map/ppermute | solution.py:488
  11.8 10.1 %collective-permute-start = (f32[136,128]{1,0:T(8,128)}, f32[136,128]{1,0:T(8,128)S(1)}, u32[]{:S(2)}, u32[]{:S(2)}) collective-permute-start(f32[136,128]{1,0:T(8,128)} %get-tuple-element.16.left), channel_id=1, source_target_pairs={{1,0},{2,1},{3,2},{0,3},{5,4},{6,5},{7,6},{4,7},{9,8},{10,9},{11,1... | collective-permute-start | bytes 208904 | tf_op jit(solution)/shard_map/ppermute | solution.py:491
  14.2 7.6 %collective-permute-start.1 = (f32[136,128]{1,0:T(8,128)}, f32[136,128]{1,0:T(8,128)S(1)}, u32[]{:S(2)}, u32[]{:S(2)}) collective-permute-start(f32[136,128]{1,0:T(8,128)} %get-tuple-element.17.right), channel_id=1, source_target_pairs={{0,1},{1,2},{2,3},{3,0},{4,5},{5,6},{6,7},{7,4},{8,9},{9,10},{10,1... | collective-permute-start | bytes 208904 | tf_op jit(solution)/shard_map/ppermute | solution.py:490
  14.2 23.3 %all-to-all-start = ((f32[16,72,128]{2,1,0:T(8,128)}), f32[16,72,128]{2,1,0:T(8,128)S(1)}, u32[]{:S(2)}, u32[]{:S(2)}) async-start(f32[16,72,128]{2,1,0:T(8,128)} %collective-permute-done.6), calls=%async_computation | async-start | bytes 1179648 | tf_op jit(solution)/shard_map/all_to_all | solution.py:493
  21.8 0.6 %copy-start.2 = (f32[136,128]{1,0:T(8,128)}, f32[136,128]{1,0:T(8,128)S(1)}, u32[]{:S(2)}) copy-start(f32[136,128]{1,0:T(8,128)S(1)} %collective-permute-done.2.bottom) | copy-start | bytes 208900
  21.8 0.6 %copy-start.3 = (f32[136,128]{1,0:T(8,128)}, f32[136,128]{1,0:T(8,128)S(1)}, u32[]{:S(2)}) copy-start(f32[136,128]{1,0:T(8,128)S(1)} %collective-permute-done.3.top) | copy-start | bytes 208900
  21.9 0.6 %copy-start.4 = (f32[136,128]{1,0:T(8,128)}, f32[136,128]{1,0:T(8,128)S(1)}, u32[]{:S(2)}) copy-start(f32[136,128]{1,0:T(8,128)S(1)} %collective-permute-done.east) | copy-start | bytes 208900
  21.9 0.6 %copy-start.5 = (f32[136,128]{1,0:T(8,128)}, f32[136,128]{1,0:T(8,128)S(1)}, u32[]{:S(2)}) copy-start(f32[136,128]{1,0:T(8,128)S(1)} %collective-permute-done.1.west) | copy-start | bytes 208900
  24.8 11.4 %collective-permute-start.5 = (f32[128,128]{1,0:T(8,128)}, f32[128,128]{1,0:T(8,128)S(1)}, u32[]{:S(2)}, u32[]{:S(2)}) collective-permute-start(f32[128,128]{1,0:T(8,128)} %get-tuple-element.19), channel_id=1, source_target_pairs={{1,0},{2,1},{3,2},{0,3},{5,4},{6,5},{7,6},{4,7},{9,8},{10,9},{11,1... | collective-permute-start | bytes 196616 | tf_op jit(solution)/shard_map/ppermute | solution.py:496
  27.7 8.6 %collective-permute-start.4 = (f32[128,128]{1,0:T(8,128)}, f32[128,128]{1,0:T(8,128)S(1)}, u32[]{:S(2)}, u32[]{:S(2)}) collective-permute-start(f32[128,128]{1,0:T(8,128)} %get-tuple-element.19), channel_id=1, source_target_pairs={{0,1},{1,2},{2,3},{3,0},{4,5},{5,6},{6,7},{7,4},{8,9},{9,10},{10,1... | collective-permute-start | bytes 196616 | tf_op jit(solution)/shard_map/ppermute | solution.py:496
  27.7 9.9 %copy-start = (f32[128,128]{1,0:T(8,128)S(1)}, f32[128,128]{1,0:T(8,128)}, u32[]{:S(2)}) copy-start(f32[128,128]{1,0:T(8,128)} %get-tuple-element.13.wet) | copy-start | bytes 196612
  27.7 9.9 %copy-start.1 = (f32[16,128]{1,0:T(8,128)S(1)}, f32[16,128]{1,0:T(8,128)}, u32[]{:S(2)}) copy-start(f32[16,128]{1,0:T(8,128)} %get-tuple-element.18.gains) | copy-start | bytes 24580

commit v3 on v2

--- a/solution.py
+++ b/solution.py
@@ -31,13 +31,22 @@
     return lax.broadcasted_iota(jnp.int32, shape, len(shape) - 1)
 
 
+def parts(lev, cx):
+    sizes, start, out = (cx, lev, lev, cx + 8, cx + 8), 0, []
+    for size in sizes:
+        out.append(pl.ds(start, size))
+        start += size
+    return out
+
+
 def send_kernel(
     ndev, ngy, chunk, group, tile_source, tile_target, tile_row, mask, surface, weights, state,
-    out, up, down, left, right, wet,
+    out, up, down, own,
     src, tgt, row, count, labels, mbuf, sbuf, wbuf, buf, sems, wsems, usems,
 ):
     lev, cx, cy = state.shape
     tiles = weights.shape[0]
+    wet, up_near, down_near, left, right = (own.at[part] for part in parts(lev, cx))
     small = [
         pltpu.make_async_copy(a, b, sems.at[i])
         for i, (a, b) in enumerate(
@@ -119,26 +128,25 @@
                 hi = hi * jnp.where(lane % 2 == 0, first, second)
             left[rows, :] = lo
             right[rows, :] = hi
+    up_near[...] = up[0:lev, :]
+    down_near[...] = down[0:lev, :]
 
 
 def outgoing(tile_source, tile_target, tile_row, mask, surface, weights, state, ngx, ngy):
     tiles = weights.shape[0]
     lev, cx, cy = state.shape
-    ndev, chunk, group = ngx * ngy, 32, 16
+    ndev, chunk, group = ngx * ngy, 32, lev
     message = jax.ShapeDtypeStruct((2 * lev + 8, cy), jnp.float32)
-    columns = jax.ShapeDtypeStruct((cx + 8, cy), jnp.float32)
     return pl.pallas_call(
         functools.partial(send_kernel, ndev, ngy, chunk, group),
         out_shape=(
             jax.ShapeDtypeStruct((ndev, 72, 128), jnp.float32),
             message,
             message,
-            columns,
-            columns,
-            jax.ShapeDtypeStruct(mask.shape, jnp.float32),
+            jax.ShapeDtypeStruct((parts(lev, cx)[-1].start + cx + 8, cy), jnp.float32),
         ),
         in_specs=[ANY] * 7,
-        out_specs=(VMEM,) * 6,
+        out_specs=(VMEM,) * 4,
         scratch_shapes=[
             pltpu.SMEM((tiles,), jnp.int32),
             pltpu.SMEM((tiles,), jnp.int32),
@@ -168,8 +176,36 @@
 PAD = 8
 
 
-def ring_kernel(ngx, ngy, lev, wet, up, down, left, right, east, west, bottom, top, ring, gains, rows):
-    cx, cy = wet.shape
+def relay_kernel(own, top, bottom, to_west, to_east):
+    cx = to_west.shape[0] - 8
+    cy = to_west.shape[1]
+    lev = top.shape[0] // 2 - 4
+    eye = lanes((lev, cy)) == lax.broadcasted_iota(jnp.int32, (lev, cy), 0)
+    for out, part, c in ((to_west, parts(lev, cx)[3], 0), (to_east, parts(lev, cx)[4], cy - 1)):
+        out[...] = own[part, :]
+        for i, msg in enumerate((top, bottom)):
+            column = msg[0:lev, c : c + 1]
+            row = jnp.sum(jnp.where(eye, column, 0.0), axis=0, keepdims=True)
+            out[cx + 1 + i : cx + 2 + i, :] = row
+
+
+def relay(own, top, bottom, cx):
+    cy = own.shape[1]
+    columns = jax.ShapeDtypeStruct((cx + 8, cy), jnp.float32)
+    return pl.pallas_call(
+        relay_kernel,
+        out_shape=(columns, columns),
+        in_specs=[VMEM] * 3,
+        out_specs=(VMEM, VMEM),
+        compiler_params=params(8),
+        cost_estimate=pl.CostEstimate(flops=10**11, bytes_accessed=10**8, transcendentals=0),
+    )(own, top, bottom)
+
+
+def ring_kernel(ngx, ngy, own, top, bottom, west, east, ring):
+    cx, cy = west.shape[0] - 8, west.shape[1]
+    lev = top.shape[0] // 2 - 4
+    _, up, down, left, right = (own.at[part] for part in parts(lev, cx))
     ocean = lax.axis_index("mp") == 1
     horiz = jnp.where(ocean, HORIZ[1], HORIZ[0]).astype(jnp.float32)
     vert = jnp.where(ocean, VERT[1], VERT[0]).astype(jnp.float32)
@@ -180,23 +216,27 @@
     has_west, has_east = has(gy > 0), has(gy < ngy - 1)
 
     lane = lanes((lev, cy))
-    edge_lane = lanes((1, cy))
-    for msg, own, flag, i in ((top, up, has_top, 0), (bottom, down, has_bottom, 1)):
-        rows[i * lev : (i + 1) * lev, :] = msg[0:lev, :]
+    eye = lane == lax.broadcasted_iota(jnp.int32, (lev, cy), 0)
+
+    def corner(msg, i, flag):
+        row = msg[cx + 1 + i : cx + 2 + i, :]
+        return flag * jnp.sum(jnp.where(eye, row, 0.0), axis=1, keepdims=True)
+
+    corners = [
+        (corner(west, i, flag * has_west), corner(east, i, flag * has_east))
+        for i, flag in enumerate((has_top, has_bottom))
+    ]
+    for msg, mine, flag, i in ((top, up, has_top, 0), (bottom, down, has_bottom, 1)):
         near = msg[0:lev, :] * flag
         far = msg[lev : 2 * lev, :] * flag
-        side = shifted(near, 1, 1) + shifted(near, -1, 1)
-        end = i * (cx - 1)
-        beside = jnp.where(
-            edge_lane == 0, west[cx : cx + 1, end : end + 1] * has_west, 0.0
-        ) + jnp.where(edge_lane == cy - 1, east[cx : cx + 1, end : end + 1] * has_east, 0.0)
-        reach = jnp.where(edge_lane == 0, has_west, jnp.where(edge_lane == cy - 1, has_east, 0.0))
-        total = (msg[2 * lev : 2 * lev + 1, :] * flag + beside) * (wet[end : end + 1, :] * reach)
-        gains[8 * i : 8 * i + 8, :] = jnp.broadcast_to(total * (horiz * horiz * flag), (8, cy))
+        w_corner, e_corner = corners[i]
+        side = pltpu.roll(jnp.where(lane == cy - 1, w_corner, near), 1, 1) + pltpu.roll(
+            jnp.where(lane == 0, e_corner, near), cy - 1, 1
+        )
         gain = msg[2 * lev : 2 * lev + 1, :] * (horiz * flag)
         outer = (
             centre * near
-            + gain * (side + far + own[0:lev, :])
+            + gain * (side + far + mine[...])
             + vert * (shifted(near, 1, 0) + shifted(near, -1, 0))
         )
         ring[2 * i * lev : (2 * i + 1) * lev, :] = near
@@ -214,7 +254,15 @@
         jnp.where(odd, pltpu.roll(west_cols, 1, 1), pltpu.roll(east_cols, cy - 1, 1))
         + jnp.where(odd, pltpu.roll(left[0:cx, :], cy - 1, 1), pltpu.roll(right[0:cx, :], 1, 1))
     )
-    above, below = shifted(merged, 1, 0), shifted(merged, -1, 0)
+    offset = lane[0:lev, :] - 2 * lax.broadcasted_iota(jnp.int32, (lev, cy), 0)
+    at_west, at_east = offset == 1, (offset == 2) | (offset == 2 - cy)
+    beyond = [
+        jnp.sum(jnp.where(at_west, w, 0.0) + jnp.where(at_east, e, 0.0), axis=0, keepdims=True)
+        for w, e in corners
+    ]
+    sub = lax.broadcasted_iota(jnp.int32, (cx, cy), 0)
+    above = jnp.where(sub == 0, beyond[0], pltpu.roll(merged, 1, 0))
+    below = jnp.where(sub == cx - 1, beyond[1], pltpu.roll(merged, cx - 1, 0))
     less = jnp.where((lane == 1) | (lane == 2), 0.0, pltpu.roll(merged, 2, 1))
     more = jnp.where((lane == cy - 1) | (lane == 0), 0.0, pltpu.roll(merged, cy - 2, 1))
     merged = (
@@ -225,26 +273,24 @@
     ring[4 * lev + cx :, :] = pltpu.roll(jnp.where(odd, merged, pltpu.roll(merged, cy - 2, 1)), cy - 1, 1)
 
 
-def outer_ring(wet, messages, lev, ngx, ngy):
-    cx, cy = wet.shape
+def outer_ring(own, top, bottom, west, east, ngx, ngy):
+    cx, cy = west.shape[0] - 8, west.shape[1]
+    lev = top.shape[0] // 2 - 4
     return pl.pallas_call(
-        functools.partial(ring_kernel, ngx, ngy, lev),
-        out_shape=(
-            jax.ShapeDtypeStruct((4 * lev + 2 * cx, cy), jnp.float32),
-            jax.ShapeDtypeStruct((16, cy), jnp.float32),
-            jax.ShapeDtypeStruct((2 * lev, cy), jnp.float32),
-        ),
-        in_specs=[VMEM] * 9,
-        out_specs=(VMEM, VMEM, VMEM),
-        compiler_params=params(LIMIT),
-        cost_estimate=pl.CostEstimate(flops=10**11, bytes_accessed=10**8, transcendentals=0),
-    )(wet, *messages)
+        functools.partial(ring_kernel, ngx, ngy),
+        out_shape=jax.ShapeDtypeStruct((4 * lev + 2 * cx, cy), jnp.float32),
+        in_specs=[VMEM] * 5,
+        out_specs=VMEM,
+        compiler_params=params(8),
+        cost_estimate=pl.CostEstimate(flops=10**6, bytes_accessed=10**5, transcendentals=0),
+    )(own, top, bottom, west, east)
 
 
 def stencil_kernel(
-    group, wet, state, ring, out, hwet, one, two, rbuf, res, sems, osems,
+    group, own, state, ring, out, hwet, one, two, rbuf, res, sems, osems,
 ):
     lev, cx, cy = state.shape
+    wet = own.at[pl.ds(0, cx)]
     pieces = lev // group
     fetch = pltpu.make_async_copy(ring, rbuf, sems.at[pieces])
     fetch.start()
@@ -346,7 +392,7 @@
         leave(i).wait()
 
 
-def two_steps(wet, state, ring):
+def two_steps(own, state, ring):
     lev, cx, cy = state.shape
     group = 8
     padded = (lev + 2, cx + 2 * PAD, cy)
@@ -364,36 +410,22 @@
             pltpu.SemaphoreType.DMA((lev // group + 1,)),
             pltpu.SemaphoreType.DMA((lev // group,)),
         ],
-        compiler_params=params(LIMIT),
+        compiler_params=params(24),
         cost_estimate=pl.CostEstimate(flops=10**6, bytes_accessed=10**5, transcendentals=0),
-    )(wet, state, ring)
-
-
-def collect_kernel(
-    wet, gains, cwest, ceast, got, second, out, received, level, upper, lower, onehot, sums, sems, rsems
-):
+    )(own, state, ring)
+
+
+def collect_kernel(own, got, second, out, received, level, onehot, sums, sems, rsems):
     ndev = got.shape[0]
     fields, cx, cy = received.shape
-    lev = second.shape[0]
     slots = ndev * CAP
-
-    def move(i, back):
-        deep = pl.ds(1, lev - 1)
-        here = (level, upper, lower)[i]
-        there = (
-            lambda r: r.at[0],
-            lambda r: r.at[deep, pl.ds(0, 8), :],
-            lambda r: r.at[deep, pl.ds(cx - 8, 8), :],
-        )[i]
-        if back:
-            return pltpu.make_async_copy(here, there(out), sems.at[i])
-        return pltpu.make_async_copy(there(second), here, sems.at[i])
+    fetch = pltpu.make_async_copy(second.at[0], level, sems.at[0])
+    fetch.start()
+    store = pltpu.make_async_copy(level, out.at[0], sems.at[1])
 
     def leave(k):
         return pltpu.make_async_copy(sums.at[k], received.at[k], rsems.at[k])
 
-    for i in range(3):
-        move(i, False).start()
     flat = got.reshape(ndev * 72, 128)
     labels = flat[64:72, :]
     for s in range(1, ndev):
@@ -404,15 +436,6 @@
     hot = jnp.where(wide, 1.0, 0.0).astype(jnp.bfloat16)
     onehot[:, 0:slots] = hot
     onehot[:, slots:] = hot
-    corners = []
-    lane = lanes((lev, cy))
-    for i, off in ((0, 0), (1, lev)):
-        diagonal = jnp.where(
-            lane == 0,
-            pltpu.roll(cwest[off : off + lev, :], 1, 1),
-            pltpu.roll(ceast[off : off + lev, :], cy - 1, 1),
-        )
-        corners.append(diagonal * gains[8 * i : 8 * i + 1, :])
     for k in range(fields):
         x = jnp.concatenate([flat[pl.ds(s * 72 + k, CAP, stride=8), :] for s in range(ndev)], axis=0)
         high = x.astype(jnp.bfloat16)
@@ -422,48 +445,36 @@
         )
         leave(k).start()
         if k == 0:
-            move(0, False).wait()
-            level[...] = level[...] + FORCE * wet[...] * sums[0]
-            level[0:1, :] = level[0:1, :] + corners[0][0:1, :]
-            level[cx - 1 :, :] = level[cx - 1 :, :] + corners[1][0:1, :]
-            move(0, True).start()
-            for i, edge, r in ((1, upper, 0), (2, lower, 7)):
-                move(i, False).wait()
-                rows = edge.reshape((lev - 1) * 8, cy)
-                at = pl.ds(r, lev - 1, stride=8)
-                rows[at, :] = rows[at, :] + corners[i - 1][1:, :]
-                move(i, True).start()
-    for i in range(3):
-        move(i, True).wait()
+            fetch.wait()
+            level[...] = level[...] + FORCE * own[0:cx, :] * sums[0]
+            store.start()
+    store.wait()
     for k in range(fields):
         leave(k).wait()
 
 
-def collect(wet, gains, corners, got, second, fields):
+def collect(own, got, second, fields):
     ndev = got.shape[0]
-    cx, cy = wet.shape
-    lev = second.shape[0]
+    _, cx, cy = second.shape
     return pl.pallas_call(
         collect_kernel,
         out_shape=(
             jax.ShapeDtypeStruct(second.shape, jnp.float32),
             jax.ShapeDtypeStruct((fields, cx, cy), jnp.float32),
         ),
-        in_specs=[VMEM] * 5 + [ANY],
+        in_specs=[VMEM, VMEM, ANY],
         out_specs=(ANY, ANY),
         scratch_shapes=[
             pltpu.VMEM((cx, cy), jnp.float32),
-            pltpu.VMEM((lev - 1, 8, cy), jnp.float32),
-            pltpu.VMEM((lev - 1, 8, cy), jnp.float32),
             pltpu.VMEM((cx, 2 * ndev * CAP), jnp.bfloat16),
             pltpu.VMEM((fields, cx, cy), jnp.float32),
-            pltpu.SemaphoreType.DMA((3,)),
+            pltpu.SemaphoreType.DMA((2,)),
             pltpu.SemaphoreType.DMA((fields,)),
         ],
-        input_output_aliases={5: 0},
+        input_output_aliases={2: 0},
         compiler_params=params(16),
         cost_estimate=pl.CostEstimate(flops=10**8, bytes_accessed=2 * 10**6, transcendentals=0),
-    )(wet, gains, *corners, got, second)
+    )(own, got, second)
 
 
 def local(states, surface, land_mask, tile_weights, tile_source, tile_target, tile_row):
@@ -471,10 +482,9 @@
     ndev = ngx * ngy
     state, fields = states[0], surface.shape[1]
     cx, cy = land_mask.shape
-    lev = state.shape[0]
     ahead = lambda n: [(i, (i + 1) % n) for i in range(n)]
     behind = lambda n: [((i + 1) % n, i) for i in range(n)]
-    buckets, up, down, left, right, wet = outgoing(
+    buckets, up, down, own = outgoing(
         tile_source[0, 0, 0],
         tile_target[0, 0, 0, :, 0],
         tile_row[0, 0, 0],
@@ -487,15 +497,14 @@
     )
     top = lax.ppermute(down, "gx", ahead(ngx))
     bottom = lax.ppermute(up, "gx", behind(ngx))
-    west = lax.ppermute(right, "gy", ahead(ngy))
-    east = lax.ppermute(left, "gy", behind(ngy))
     buckets = lax.ppermute(buckets, "mp", [(0, 1), (1, 0)])
     got = lax.all_to_all(buckets, ("gx", "gy"), split_axis=0, concat_axis=0, tiled=True)
-    messages = (up, down, left, right, east, west, bottom, top)
-    ring, gains, rows = outer_ring(wet, messages, lev, ngx, ngy)
-    corners = (lax.ppermute(rows, "gy", ahead(ngy)), lax.ppermute(rows, "gy", behind(ngy)))
-    second = two_steps(wet, state, ring)
-    new_state, received = collect(wet, gains, corners, got, second, fields)
+    to_west, to_east = relay(own, top, bottom, cx)
+    west = lax.ppermute(to_east, "gy", ahead(ngy))
+    east = lax.ppermute(to_west, "gy", behind(ngy))
+    ring = outer_ring(own, top, bottom, west, east, ngx, ngy)
+    second = two_steps(own, state, ring)
+    new_state, received = collect(own, got, second, fields)
     return new_state[None], received[None]
 
 

time: 40.2 us -> 35.3 us (0.88)
  Pallas kernels: 19.1 us -> 14.7 us
  starting transfers between devices: 18 us -> 13.7 us
  waiting for transfers between devices: 1.37 us -> 4.98 us
    ppermute x4 -> x2, waiting for transfers between devices: 0.01 us -> 4.37 us  [the longest x1 4.36 us: local(): west = lax.ppermute(to_east, 'gy', ahead(ngy))]
    ppermute x1, starting transfers between devices: 0.01 us -> 2.64 us  [local(): top = lax.ppermute(down, 'gx', ahead(ngx))]
    ppermute x1, starting transfers between devices: 4.65 us -> 2.11 us  [local(): bottom = lax.ppermute(up, 'gx', behind(ngx))]
    ppermute x4 -> x2, starting transfers between devices: 5.28 us -> 2.98 us  [the longest x1 1.97 us: local(): west = lax.ppermute(to_east, 'gy', ahead(ngy))]
    all_to_all x1, starting transfers between devices: 7.56 us -> 5.46 us  [local(): lax.all_to_all(buckets, ('gx', 'gy'), split_axis=0, concat_axis=0, tiled=...]
    pallas_call x1 -> x2, Pallas kernels: 2.33 us -> 0.66 us  [the longest x1 0.55 us: outer_ring(): pl.pallas_call(functools.partial(ring_kernel, ngx, ngy), out_shape=jax.Sh...]
    pallas_call x1, Pallas kernels: 8.52 us -> 6.91 us  [two_steps(): pl.pallas_call(functools.partial(stencil_kernel, group), out_shape=jax.Sh...]
    all_to_all x1, waiting for transfers between devices: 1.35 us -> 0.6 us  [local(): lax.all_to_all(buckets, ('gx', 'gy'), split_axis=0, concat_axis=0, tiled=...]
  transfers between devices with their start and end apart: 8 -> 6, of which waited for: 1 -> 2; matrix products, arithmetic and copies ran while one was open for 0% -> 0% of each run, Pallas kernels for 27% -> 22%
where the time goes in v3:
time: 35.3 us; the launch traced here: 35 us
  Pallas kernels  14.7 us (42%)
  starting transfers between devices  13.7 us (39%)
  waiting for transfers between devices  4.98 us (14%)
  local copies, waits for them, and re-layouts  0.96 us (3%)
  between operations  0.71 us (2%)
    pallas_call x1, Pallas kernels, two_steps(): pl.pallas_call(functools.partial(stencil_kernel, group), out_shape=jax.Sh...  6.91 us
    all_to_all x1, starting transfers between devices, local(): lax.all_to_all(buckets, ('gx', 'gy'), split_axis=0, concat_axis=0, tiled=...  5.46 us
    pallas_call x1, Pallas kernels, outgoing(): pl.pallas_call(functools.partial(send_kernel, ndev, ngy, chunk, group), o...  5.2 us
    ppermute x1, waiting for transfers between devices, local(): west = lax.ppermute(to_east, 'gy', ahead(ngy))  4.36 us
    ppermute x1, starting transfers between devices, local(): top = lax.ppermute(down, 'gx', ahead(ngx))  2.64 us
    ppermute x1, starting transfers between devices, local(): bottom = lax.ppermute(up, 'gx', behind(ngx))  2.11 us
    ppermute x1, starting transfers between devices, local(): west = lax.ppermute(to_east, 'gy', ahead(ngy))  1.97 us
    pallas_call x1, Pallas kernels, collect(): pl.pallas_call(collect_kernel, out_shape=(jax.ShapeDtypeStruct(second.sha...  1.9 us
  transfers between devices with their start and end apart: 6, of which 2 were waited for; matrix products, arithmetic and copies ran while one was open for 0% of the time, Pallas kernels for 22%

profile of v3, /device:TPU:0, one launch (start us, length us, event | category | flops | bytes accessed | tf_op | source)
XLA Modules:
  0.0 35.0 jit_solution(18365340537403065680)
XLA Ops:
  0.6 5.2 %shard_map.86 = (f32[16,72,128]{2,1,0:T(8,128)}, f32[136,128]{1,0:T(8,128)}, f32[136,128]{1,0:T(8,128)}, f32[528,128]{1,0:T(8,128)}) custom-call(s32[64]{0:T(128)} %bitcast.13, s32[64]{0:T(128)} %bitcast.14, s32[64]{0:T(128)} %bitcast.15, s32[128,128]{1,0:T(8,128)} %mask.1, f32[1024,128]{1,0:T(8,128)} %bitcast.12, bf16[64,128,128]{2,1,0:T(8,128)(2,1)} %bitcast.11, ...), custom_call_target="tpu_custom_call" | custom-call | flops 100000000 | bytes 8000000 | tf_op jit(solution)/shard_map/pallas_call | solution.py:140
  5.8 0.5 %collective-permute-start = (f32[16,72,128]{2,1,0:T(8,128)}, f32[16,72,128]{2,1,0:T(8,128)}, u32[]{:S(2)}, u32[]{:S(2)}) collective-permute-start(f32[16,72,128]{2,1,0:T(8,128)} %get-tuple-element.11), channel_id=1, source_target_pairs={{0,16},{16,0},{1,17},{17,1},{2,18},{18,2},{3,19},{19,3},{4,20},{20... | collective-permute-start | bytes 1769480 | tf_op jit(solution)/shard_map/ppermute | solution.py:500
  6.4 2.6 %collective-permute-start.1 = (f32[136,128]{1,0:T(8,128)}, f32[136,128]{1,0:T(8,128)S(1)}, u32[]{:S(2)}, u32[]{:S(2)}) collective-permute-start(f32[136,128]{1,0:T(8,128)} %get-tuple-element.12), channel_id=1, source_target_pairs={{0,4},{4,8},{8,12},{12,0},{1,5},{5,9},{9,13},{13,1},{2,6},{6,10},{... | collective-permute-start | bytes 208904 | tf_op jit(solution)/shard_map/ppermute | solution.py:498
  9.0 2.1 %collective-permute-start.2 = (f32[136,128]{1,0:T(8,128)}, f32[136,128]{1,0:T(8,128)S(1)}, u32[]{:S(2)}, u32[]{:S(2)}) collective-permute-start(f32[136,128]{1,0:T(8,128)} %get-tuple-element.13), channel_id=1, source_target_pairs={{4,0},{8,4},{12,8},{0,12},{5,1},{9,5},{13,9},{1,13},{6,2},{10,6},{... | collective-permute-start | bytes 208904 | tf_op jit(solution)/shard_map/ppermute | solution.py:499
  11.1 0.0 collective-permute-done
  11.1 5.5 %all-to-all-start = ((f32[16,72,128]{2,1,0:T(8,128)}), f32[16,72,128]{2,1,0:T(8,128)S(1)}, u32[]{:S(2)}, u32[]{:S(2)}) async-start(f32[16,72,128]{2,1,0:T(8,128)} %collective-permute-done), calls=%async_computation | async-start | bytes 1179648 | tf_op jit(solution)/shard_map/all_to_all | solution.py:501
  16.6 0.0 collective-permute-done.1.top
  16.6 0.0 collective-permute-done.2.bottom
  16.6 0.0 copy-start.1
  16.6 0.9 %copy-done.1 = f32[528,128]{1,0:T(8,128)S(1)} copy-done((f32[528,128]{1,0:T(8,128)S(1)}, f32[528,128]{1,0:T(8,128)}, u32[]{:S(2)}) %copy-start.1) | copy-done | bytes 270360
  17.5 0.0 copy-start
  17.6 0.0 copy-start.2
  17.6 0.1 shard_map.87
  17.7 2.0 %collective-permute-start.3 = (f32[136,128]{1,0:T(8,128)S(1)}, f32[136,128]{1,0:T(8,128)S(1)}, u32[]{:S(2)}, u32[]{:S(2)}) collective-permute-start(f32[136,128]{1,0:T(8,128)S(1)} %get-tuple-element.14), channel_id=1, source_target_pairs={{0,1},{1,2},{2,3},{3,0},{4,5},{5,6},{6,7},{7,4},{8,9},{9,10},{10,1... | collective-permute-start | bytes 208904 | tf_op jit(solution)/shard_map/ppermute | solution.py:503
  19.6 1.0 %collective-permute-start.4 = (f32[136,128]{1,0:T(8,128)S(1)}, f32[136,128]{1,0:T(8,128)S(1)}, u32[]{:S(2)}, u32[]{:S(2)}) collective-permute-start(f32[136,128]{1,0:T(8,128)S(1)} %get-tuple-element.15), channel_id=1, source_target_pairs={{1,0},{2,1},{3,2},{0,3},{5,4},{6,5},{7,6},{4,7},{9,8},{10,9},{11,1... | collective-permute-start | bytes 208904 | tf_op jit(solution)/shard_map/ppermute | solution.py:504
  20.6 4.4 %collective-permute-done.3.west = f32[136,128]{1,0:T(8,128)S(1)} collective-permute-done((f32[136,128]{1,0:T(8,128)S(1)}, f32[136,128]{1,0:T(8,128)S(1)}, u32[]{:S(2)}, u32[]{:S(2)}) %collective-permute-start.3) | collective-permute-done | bytes 69664 | tf_op jit(solution)/shard_map/ppermute | solution.py:503
  25.0 0.0 collective-permute-done.4.east
  25.0 0.5 %shard_map.88.ring = f32[512,128]{1,0:T(8,128)S(1)} custom-call(f32[528,128]{1,0:T(8,128)S(1)} %copy-done.1, f32[136,128]{1,0:T(8,128)S(1)} %collective-permute-done.1.top, f32[136,128]{1,0:T(8,128)S(1)} %collective-permute-done.2.bottom, f32[136,128]{1,0:T(8,128)S(1)} %collective-permute-done.3.west, f32[136,128]{1,0:T(8,128)S(1)} %collective-permute-done.4.east), custom_call_target="tpu_custom_call" | custom-call | flops 1000000 | bytes 100000 | tf_op jit(solution)/shard_map/pallas_call | solution.py:279
  25.6 0.0 copy-done
  25.6 0.0 copy-done.2
  25.6 6.9 %shard_map.89.second = f32[64,128,128]{2,1,0:T(8,128)} custom-call(f32[528,128]{1,0:T(8,128)S(1)} %copy-done.2, f32[64,128,128]{2,1,0:T(8,128)S(1)} %bitcast.9, f32[512,128]{1,0:T(8,128)S(1)} %shard_map.88.ring), custom_call_target="tpu_custom_call" | custom-call | flops 1000000 | bytes 100000 | tf_op jit(solution)/shard_map/pallas_call | solution.py:399
  32.5 0.6 %all-to-all-done.got = f32[16,72,128]{2,1,0:T(8,128)S(1)} async-done(((f32[16,72,128]{2,1,0:T(8,128)}), f32[16,72,128]{2,1,0:T(8,128)S(1)}, u32[]{:S(2)}, u32[]{:S(2)}) %all-to-all-start) | async-done | bytes 589856 | tf_op jit(solution)/shard_map/all_to_all | solution.py:501
  33.1 1.9 %shard_map.90 = (f32[64,128,128]{2,1,0:T(8,128)}, f32[8,128,128]{2,1,0:T(8,128)}) custom-call(f32[528,128]{1,0:T(8,128)S(1)} %copy-done.2, f32[16,72,128]{2,1,0:T(8,128)S(1)} %all-to-all-done.got, f32[64,128,128]{2,1,0:T(8,128)} %shard_map.89.second), custom_call_target="tpu_custom_call", output_to_operand_aliasing={{0}: (2, {})} | custom-call | flops 100000000 | bytes 2000000 | tf_op jit(solution)/shard_map/pallas_call | solution.py:459
Async XLA Ops:
  5.8 5.3 %collective-permute-start = (f32[16,72,128]{2,1,0:T(8,128)}, f32[16,72,128]{2,1,0:T(8,128)}, u32[]{:S(2)}, u32[]{:S(2)}) collective-permute-start(f32[16,72,128]{2,1,0:T(8,128)} %get-tuple-element.11), channel_id=1, source_target_pairs={{0,16},{16,0},{1,17},{17,1},{2,18},{18,2},{3,19},{19,3},{4,20},{20... | collective-permute-start | bytes 1769480 | tf_op jit(solution)/shard_map/ppermute | solution.py:500
  6.4 10.2 %collective-permute-start.1 = (f32[136,128]{1,0:T(8,128)}, f32[136,128]{1,0:T(8,128)S(1)}, u32[]{:S(2)}, u32[]{:S(2)}) collective-permute-start(f32[136,128]{1,0:T(8,128)} %get-tuple-element.12), channel_id=1, source_target_pairs={{0,4},{4,8},{8,12},{12,0},{1,5},{5,9},{9,13},{13,1},{2,6},{6,10},{... | collective-permute-start | bytes 208904 | tf_op jit(solution)/shard_map/ppermute | solution.py:498
  9.0 7.6 %collective-permute-start.2 = (f32[136,128]{1,0:T(8,128)}, f32[136,128]{1,0:T(8,128)S(1)}, u32[]{:S(2)}, u32[]{:S(2)}) collective-permute-start(f32[136,128]{1,0:T(8,128)} %get-tuple-element.13), channel_id=1, source_target_pairs={{4,0},{8,4},{12,8},{0,12},{5,1},{9,5},{13,9},{1,13},{6,2},{10,6},{... | collective-permute-start | bytes 208904 | tf_op jit(solution)/shard_map/ppermute | solution.py:499
  11.1 22.0 %all-to-all-start = ((f32[16,72,128]{2,1,0:T(8,128)}), f32[16,72,128]{2,1,0:T(8,128)S(1)}, u32[]{:S(2)}, u32[]{:S(2)}) async-start(f32[16,72,128]{2,1,0:T(8,128)} %collective-permute-done), calls=%async_computation | async-start | bytes 1179648 | tf_op jit(solution)/shard_map/all_to_all | solution.py:501
  16.6 1.0 %copy-start.1 = (f32[528,128]{1,0:T(8,128)S(1)}, f32[528,128]{1,0:T(8,128)}, u32[]{:S(2)}) copy-start(f32[528,128]{1,0:T(8,128)} %get-tuple-element.10.own) | copy-start | bytes 811012
  17.5 8.0 %copy-start = (f32[1,64,128,128]{3,2,1,0:T(8,128)S(1)}, f32[1,64,128,128]{3,2,1,0:T(8,128)}, u32[]{:S(2)}) copy-start(f32[1,64,128,128]{3,2,1,0:T(8,128)} %param.7) | copy-start | bytes 12582916
  17.6 8.0 %copy-start.2 = (f32[528,128]{1,0:T(8,128)S(1)}, f32[528,128]{1,0:T(8,128)}, u32[]{:S(2)}) copy-start(f32[528,128]{1,0:T(8,128)} %get-tuple-element.10.own) | copy-start | bytes 811012
  17.7 7.3 %collective-permute-start.3 = (f32[136,128]{1,0:T(8,128)S(1)}, f32[136,128]{1,0:T(8,128)S(1)}, u32[]{:S(2)}, u32[]{:S(2)}) collective-permute-start(f32[136,128]{1,0:T(8,128)S(1)} %get-tuple-element.14), channel_id=1, source_target_pairs={{0,1},{1,2},{2,3},{3,0},{4,5},{5,6},{6,7},{7,4},{8,9},{9,10},{10,1... | collective-permute-start | bytes 208904 | tf_op jit(solution)/shard_map/ppermute | solution.py:503
  19.6 5.4 %collective-permute-start.4 = (f32[136,128]{1,0:T(8,128)S(1)}, f32[136,128]{1,0:T(8,128)S(1)}, u32[]{:S(2)}, u32[]{:S(2)}) collective-permute-start(f32[136,128]{1,0:T(8,128)S(1)} %get-tuple-element.15), channel_id=1, source_target_pairs={{1,0},{2,1},{3,2},{0,3},{5,4},{6,5},{7,6},{4,7},{9,8},{10,9},{11,1... | collective-permute-start | bytes 208904 | tf_op jit(solution)/shard_map/ppermute | solution.py:504

commit v4 on v3

--- a/solution.py
+++ b/solution.py
@@ -13,6 +13,7 @@
 VERT = (0.1, 0.15)
 MIB = 1024 * 1024
 LIMIT = 60
+FIRST_COST = 5 * 10**9
 ANY = pl.BlockSpec(memory_space=pl.ANY)
 VMEM = pl.BlockSpec(memory_space=pltpu.VMEM)
 SMEM = pl.BlockSpec(memory_space=pltpu.SMEM)
@@ -64,6 +65,8 @@
         part = pl.ds(i * group, group)
         ucopies.append(pltpu.make_async_copy(state.at[part], buf.at[part], usems.at[i]))
         ucopies[-1].start()
+    block = out.shape[0] // ndev
+    extra = block - 8 * CAP
     out[...] = jnp.zeros_like(out)
     labels[...] = jnp.zeros_like(labels)
     for d in range(ndev):
@@ -79,7 +82,7 @@
         rank = count[d]
         count[d] = rank + 1
         picked = sbuf[pl.ds(s, 8, stride=cx), :] * wet[pl.ds(s, 1), :]
-        out[d, pl.ds(rank * 8, 8), :] = lax.dot_general(
+        out[pl.ds(d * block + rank * 8, 8), :] = lax.dot_general(
             picked.astype(jnp.bfloat16),
             wbuf[t],
             (((1,), (1,)), ((), ())),
@@ -93,7 +96,7 @@
         wcopies[i].wait()
         lax.fori_loop(i * chunk, (i + 1) * chunk, one, 0, unroll=True)
     for d in range(ndev):
-        out[d, 64:72, :] = labels[d]
+        out[(d + 1) * block - extra : (d + 1) * block, :] = labels[d, 0:extra, :]
 
     turned = jnp.transpose(wet[...])
     up[2 * lev :, :] = jnp.broadcast_to(wet[0:1, :], (8, cy))
@@ -136,11 +139,12 @@
     tiles = weights.shape[0]
     lev, cx, cy = state.shape
     ndev, chunk, group = ngx * ngy, 32, lev
+    block = 8 * CAP + ndev * CAP // 128
     message = jax.ShapeDtypeStruct((2 * lev + 8, cy), jnp.float32)
     return pl.pallas_call(
         functools.partial(send_kernel, ndev, ngy, chunk, group),
         out_shape=(
-            jax.ShapeDtypeStruct((ndev, 72, 128), jnp.float32),
+            jax.ShapeDtypeStruct((ndev * block, 128), jnp.float32),
             message,
             message,
             jax.ShapeDtypeStruct((parts(lev, cx)[-1].start + cx + 8, cy), jnp.float32),
@@ -205,7 +209,7 @@
 def ring_kernel(ngx, ngy, own, top, bottom, west, east, ring):
     cx, cy = west.shape[0] - 8, west.shape[1]
     lev = top.shape[0] // 2 - 4
-    _, up, down, left, right = (own.at[part] for part in parts(lev, cx))
+    wet, up, down, left, right = (own.at[part] for part in parts(lev, cx))
     ocean = lax.axis_index("mp") == 1
     horiz = jnp.where(ocean, HORIZ[1], HORIZ[0]).astype(jnp.float32)
     vert = jnp.where(ocean, VERT[1], VERT[0]).astype(jnp.float32)
@@ -239,8 +243,7 @@
             + gain * (side + far + mine[...])
             + vert * (shifted(near, 1, 0) + shifted(near, -1, 0))
         )
-        ring[2 * i * lev : (2 * i + 1) * lev, :] = near
-        ring[(2 * i + 1) * lev : (2 * i + 2) * lev, :] = outer
+        ring[i * lev : (i + 1) * lev, :] = outer
 
     lane = lanes((cx, cy))
     odd = lane % 2 == 1
@@ -249,7 +252,10 @@
     w_gain = jnp.transpose(jnp.broadcast_to(west[cx : cx + 1, :], (cx, cx))) * (horiz * has_west)
     e_gain = jnp.transpose(jnp.broadcast_to(east[cx : cx + 1, :], (cx, cx))) * (horiz * has_east)
     merged = jnp.where(odd, west_cols, east_cols)
-    ring[4 * lev : 4 * lev + cx, :] = pltpu.roll(jnp.where(odd, merged, pltpu.roll(merged, cy - 2, 1)), cy - 1, 1)
+    given = merged * (horiz * jnp.where(odd, wet[:, 0:1], wet[:, cy - 1 : cy]))
+    ring[2 * lev : 2 * lev + cx, :] = pltpu.roll(
+        jnp.where(odd, given, pltpu.roll(given, cy - 2, 1)), cy - 1, 1
+    )
     beside = (
         jnp.where(odd, pltpu.roll(west_cols, 1, 1), pltpu.roll(east_cols, cy - 1, 1))
         + jnp.where(odd, pltpu.roll(left[0:cx, :], cy - 1, 1), pltpu.roll(right[0:cx, :], 1, 1))
@@ -270,7 +276,7 @@
         + jnp.where(odd, w_gain, e_gain) * (beside + above + below)
         + vert * (less + more)
     )
-    ring[4 * lev + cx :, :] = pltpu.roll(jnp.where(odd, merged, pltpu.roll(merged, cy - 2, 1)), cy - 1, 1)
+    ring[2 * lev + cx :, :] = pltpu.roll(jnp.where(odd, merged, pltpu.roll(merged, cy - 2, 1)), cy - 1, 1)
 
 
 def outer_ring(own, top, bottom, west, east, ngx, ngy):
@@ -278,7 +284,7 @@
     lev = top.shape[0] // 2 - 4
     return pl.pallas_call(
         functools.partial(ring_kernel, ngx, ngy),
-        out_shape=jax.ShapeDtypeStruct((4 * lev + 2 * cx, cy), jnp.float32),
+        out_shape=jax.ShapeDtypeStruct((2 * lev + 2 * cx, cy), jnp.float32),
         in_specs=[VMEM] * 5,
         out_specs=VMEM,
         compiler_params=params(8),
@@ -286,49 +292,48 @@
     )(own, top, bottom, west, east)
 
 
-def stencil_kernel(
-    group, own, state, ring, out, hwet, one, two, rbuf, res, sems, osems,
-):
-    lev, cx, cy = state.shape
-    wet = own.at[pl.ds(0, cx)]
+def step_kernel(ngx, group, second, own, x, *refs):
+    if second:
+        ring, out, hwet, buf, res, sems, osems = refs
+    else:
+        top, bottom, out, hwet, buf, res, sems, osems = refs
+    lev, cx, cy = x.shape
     pieces = lev // group
-    fetch = pltpu.make_async_copy(ring, rbuf, sems.at[pieces])
-    fetch.start()
-    copies = []
+
+    def arrive(i):
+        return pltpu.make_async_copy(
+            x.at[pl.ds(i * group, group)],
+            buf.at[pl.ds(i * group + 1, group), pl.ds(PAD, cx), :],
+            sems.at[i],
+        )
+
+    def leave(i):
+        part = pl.ds(i * group, group)
+        return pltpu.make_async_copy(res.at[part], out.at[part], osems.at[i])
+
     for i in range(pieces):
-        part = pl.ds(i * group, group)
-        copies.append(
-            pltpu.make_async_copy(
-                state.at[part], one.at[pl.ds(i * group + 1, group), pl.ds(PAD, cx), :], sems.at[i]
-            )
-        )
-        copies[-1].start()
+        arrive(i).start()
     ocean = lax.axis_index("mp") == 1
     horiz = jnp.where(ocean, HORIZ[1], HORIZ[0]).astype(jnp.float32)
     vert = jnp.where(ocean, VERT[1], VERT[0]).astype(jnp.float32)
     centre = 1.0 - 4.0 * horiz - 2.0 * vert
+    wet = own.at[pl.ds(0, cx)]
     hwet[...] = wet[...] * horiz
     lane = lanes((cx, cy))
+    ends = (lane == 0) | (lane == cy - 1)
     height = cx + 2 * PAD
-    flat_one = one.reshape((lev + 2) * height, cy)
-    flat_two = two.reshape((lev + 2) * height, cy)
-    fetch.wait()
-    for buf, off, at in (
-        (flat_one, 0, PAD - 1),
-        (flat_two, lev, PAD - 1),
-        (flat_one, 2 * lev, PAD + cx),
-        (flat_two, 3 * lev, PAD + cx),
-    ):
-        buf[pl.ds(height + at, lev, stride=height), :] = rbuf[off : off + lev, :]
-    for buf in (one, two):
-        buf[0] = jnp.zeros((height, cy), jnp.float32)
-        buf[lev + 1] = jnp.zeros((height, cy), jnp.float32)
-
-    def mask_level(l, _):
-        one[l + 1, PAD : PAD + cx, :] = one[l + 1, PAD : PAD + cx, :] * wet[...]
-        return 0
-
-    ends = (lane == 0) | (lane == cy - 1)
+    flat = buf.reshape((lev + 2) * height, cy)
+    above, below = pl.ds(height + PAD - 1, lev, stride=height), pl.ds(height + PAD + cx, lev, stride=height)
+    if second:
+        flat[above, :] = ring[0:lev, :]
+        flat[below, :] = ring[lev : 2 * lev, :]
+    else:
+        gx = lax.axis_index("gx")
+        flat[above, :] = top[0:lev, :] * jnp.where(gx > 0, 1.0, 0.0).astype(jnp.float32)
+        flat[below, :] = bottom[0:lev, :] * jnp.where(gx < ngx - 1, 1.0, 0.0).astype(jnp.float32)
+    buf[0] = jnp.zeros((height, cy), jnp.float32)
+    buf[lev + 1] = jnp.zeros((height, cy), jnp.float32)
+
     apart = lax.broadcasted_iota(jnp.int32, (cy, cy), 0) - lanes((cy, cy))
     pairs = jnp.where((apart == 1) | (apart == -1), 1.0, 0.0).astype(jnp.bfloat16)
     pairs = jnp.concatenate([pairs, pairs], axis=0)
@@ -339,84 +344,79 @@
         both = jnp.concatenate([high, low], axis=1)
         return jnp.dot(both, pairs, preferred_element_type=jnp.float32)
 
-    def step(buf, sides, l, j):
-        here = buf[l + 1, PAD : PAD + cx, :]
-        edge = pltpu.roll(sides, (cy - 2 * j) % cy, 1)
-        around = (
-            jnp.where(ends, edge, 0.0)
-            + beside_of(here)
-            + buf[l + 1, PAD - 1 : PAD - 1 + cx, :]
-            + buf[l + 1, PAD + 1 : PAD + 1 + cx, :]
-        )
-        column = buf[l, PAD : PAD + cx, :] + buf[l + 2, PAD : PAD + cx, :]
-        return centre * here + hwet[...] * around + vert * column
-
-    def first_levels(start, count, turn):
-        sides = pltpu.roll(rbuf[4 * lev : 4 * lev + cx, :], lax.rem(2 * cy - 2 * start, cy), 1)
+    def columns(part, start):
+        off = 2 * lev + part * cx
+        return pltpu.roll(ring[off : off + cx, :], lax.rem(2 * cy - 2 * start, cy), 1)
+
+    def at_ends(sides, j):
+        return jnp.where(ends, pltpu.roll(sides, (cy - 2 * j) % cy, 1), 0.0)
+
+    def accept(i):
+        arrive(i).wait()
+        sides = columns(0, i * group) if second else None
+        for j in range(group):
+            here = (i * group + j + 1, slice(PAD, PAD + cx), slice(None))
+            if second:
+                buf[here] = buf[here] + at_ends(sides, j)
+            else:
+                buf[here] = buf[here] * wet[...]
+
+    def levels(start, count):
+        sides = columns(1, start) if second else None
         for j in range(count):
-            two[start + j + 1, PAD : PAD + cx, :] = step(one, sides, start + j, j)
-
-    def second_levels(start, count):
-        sides = pltpu.roll(rbuf[4 * lev + cx :, :], lax.rem(2 * cy - 2 * start, cy), 1)
-        for j in range(count):
-            res[start + j] = step(two, sides, start + j, j)
-
-    def arrive(i):
-        pltpu.make_async_copy(
-            state.at[pl.ds(i * group, group)],
-            one.at[pl.ds(i * group + 1, group), pl.ds(PAD, cx), :],
-            sems.at[i],
-        ).wait()
-        for j in range(group):
-            mask_level(i * group + j, 0)
-
-    def leave(i):
-        part = pl.ds(i * group, group)
-        return pltpu.make_async_copy(res.at[part], out.at[part], osems.at[i])
-
-    arrive(0)
-    first_levels(0, group - 1, 0)
+            l = start + j
+            here = buf[l + 1, PAD : PAD + cx, :]
+            around = (
+                beside_of(here)
+                + buf[l + 1, PAD - 1 : PAD - 1 + cx, :]
+                + buf[l + 1, PAD + 1 : PAD + 1 + cx, :]
+            )
+            if second:
+                around = around + at_ends(sides, j)
+            column = buf[l, PAD : PAD + cx, :] + buf[l + 2, PAD : PAD + cx, :]
+            res[l] = centre * here + hwet[...] * around + vert * column
+
+    accept(0)
+    levels(0, group - 1)
 
     def middle(i, _):
-        arrive(i)
-        first_levels(i * group - 1, group, 0)
-        second_levels((i - 1) * group, group)
+        accept(i)
+        levels(i * group - 1, group)
         leave(i - 1).start()
         return 0
 
     lax.fori_loop(1, pieces, middle, 0)
-    first_levels(lev - 1, 1, 0)
-    second_levels(lev - group, group)
+    levels(lev - 1, 1)
     leave(pieces - 1).start()
     for i in range(pieces):
         leave(i).wait()
 
 
-def two_steps(own, state, ring):
-    lev, cx, cy = state.shape
+def one_step(own, x, outside, ngx, second):
+    lev, cx, cy = x.shape
     group = 8
-    padded = (lev + 2, cx + 2 * PAD, cy)
     return pl.pallas_call(
-        functools.partial(stencil_kernel, group),
-        out_shape=jax.ShapeDtypeStruct(state.shape, jnp.float32),
-        in_specs=[VMEM, ANY, ANY],
+        functools.partial(step_kernel, ngx, group, second),
+        out_shape=jax.ShapeDtypeStruct(x.shape, jnp.float32),
+        in_specs=[VMEM, ANY] + [VMEM] * len(outside),
         out_specs=ANY,
         scratch_shapes=[
             pltpu.VMEM((cx, cy), jnp.float32),
-            pltpu.VMEM(padded, jnp.float32),
-            pltpu.VMEM(padded, jnp.float32),
-            pltpu.VMEM(ring.shape, jnp.float32),
-            pltpu.VMEM(state.shape, jnp.float32),
-            pltpu.SemaphoreType.DMA((lev // group + 1,)),
+            pltpu.VMEM((lev + 2, cx + 2 * PAD, cy), jnp.float32),
+            pltpu.VMEM(x.shape, jnp.float32),
+            pltpu.SemaphoreType.DMA((lev // group,)),
             pltpu.SemaphoreType.DMA((lev // group,)),
         ],
-        compiler_params=params(24),
-        cost_estimate=pl.CostEstimate(flops=10**6, bytes_accessed=10**5, transcendentals=0),
-    )(own, state, ring)
-
-
-def collect_kernel(own, got, second, out, received, level, onehot, sums, sems, rsems):
-    ndev = got.shape[0]
+        compiler_params=params(16),
+        cost_estimate=pl.CostEstimate(
+            flops=10**6 if second else FIRST_COST, bytes_accessed=10**5, transcendentals=0
+        ),
+    )(own, x, *outside)
+
+
+def collect_kernel(ndev, own, got, second, out, received, level, onehot, sums, sems, rsems):
+    block = got.shape[0] // ndev
+    extra = block - 8 * CAP
     fields, cx, cy = received.shape
     slots = ndev * CAP
     fetch = pltpu.make_async_copy(second.at[0], level, sems.at[0])
@@ -426,10 +426,9 @@
     def leave(k):
         return pltpu.make_async_copy(sums.at[k], received.at[k], rsems.at[k])
 
-    flat = got.reshape(ndev * 72, 128)
-    labels = flat[64:72, :]
+    labels = got[block - extra : block, :]
     for s in range(1, ndev):
-        labels = labels + flat[s * 72 + 64 : s * 72 + 72, :]
+        labels = labels + got[(s + 1) * block - extra : (s + 1) * block, :]
     labels = labels.astype(jnp.int32)
     want = lax.broadcasted_iota(jnp.int32, (cx, 128), 0) + 1
     wide = jnp.concatenate([labels[q : q + 1, :] == want for q in range(slots // 128)], axis=1)
@@ -437,7 +436,7 @@
     onehot[:, 0:slots] = hot
     onehot[:, slots:] = hot
     for k in range(fields):
-        x = jnp.concatenate([flat[pl.ds(s * 72 + k, CAP, stride=8), :] for s in range(ndev)], axis=0)
+        x = jnp.concatenate([got[pl.ds(s * block + k, CAP, stride=8), :] for s in range(ndev)], axis=0)
         high = x.astype(jnp.bfloat16)
         low = (x - high.astype(jnp.float32)).astype(jnp.bfloat16)
         sums[k] = jnp.dot(
@@ -453,11 +452,10 @@
         leave(k).wait()
 
 
-def collect(own, got, second, fields):
-    ndev = got.shape[0]
+def collect(own, got, second, fields, ndev):
     _, cx, cy = second.shape
     return pl.pallas_call(
-        collect_kernel,
+        functools.partial(collect_kernel, ndev),
         out_shape=(
             jax.ShapeDtypeStruct(second.shape, jnp.float32),
             jax.ShapeDtypeStruct((fields, cx, cy), jnp.float32),
@@ -498,13 +496,17 @@
     top = lax.ppermute(down, "gx", ahead(ngx))
     bottom = lax.ppermute(up, "gx", behind(ngx))
     buckets = lax.ppermute(buckets, "mp", [(0, 1), (1, 0)])
+    whole = buckets.shape
+    buckets = buckets.reshape(ndev, whole[0] // ndev, 1, whole[1])
     got = lax.all_to_all(buckets, ("gx", "gy"), split_axis=0, concat_axis=0, tiled=True)
+    got = got.reshape(whole)
     to_west, to_east = relay(own, top, bottom, cx)
     west = lax.ppermute(to_east, "gy", ahead(ngy))
     east = lax.ppermute(to_west, "gy", behind(ngy))
+    first = one_step(own, state, (top, bottom), ngx, False)
     ring = outer_ring(own, top, bottom, west, east, ngx, ngy)
-    second = two_steps(own, state, ring)
-    new_state, received = collect(own, got, second, fields)
+    second = one_step(own, first, (ring,), ngx, True)
+    new_state, received = collect(own, got, second, fields, ndev)
     return new_state[None], received[None]
 
 

time: 35.3 us -> 34.3 us (0.972)
  waiting for transfers between devices: 4.98 us -> 1.69 us
  Pallas kernels: 14.7 us -> 17 us
    ppermute x1, waiting for transfers between devices: 4.36 us -> 1.61 us  [local(): west = lax.ppermute(to_east, 'gy', ahead(ngy))]
    pallas_call x2 -> x3, Pallas kernels: 8.81 us -> 11 us  [the longest x2 9.07 us: one_step(): pl.pallas_call(functools.partial(step_kernel, ngx, group, second), out_sh...]
    all_to_all x1, waiting for transfers between devices: 0.6 us -> 0.07 us  [local(): lax.all_to_all(buckets, ('gx', 'gy'), split_axis=0, concat_axis=0, tiled=...]
  transfers between devices with their start and end apart: 6 -> 6, of which waited for: 2 -> 2; matrix products, arithmetic and copies ran while one was open for 0% -> 0% of each run, Pallas kernels for 22% -> 29%
where the time goes in v4:
time: 34.3 us; the launch traced here: 34 us
  Pallas kernels  17 us (50%)
  starting transfers between devices  13.6 us (40%)
  waiting for transfers between devices  1.69 us (5%)
  local copies, waits for them, and re-layouts  0.96 us (3%)
  between operations  0.7 us (2%)
    pallas_call x2, Pallas kernels, one_step(): pl.pallas_call(functools.partial(step_kernel, ngx, group, second), out_sh...  9.07 us
    all_to_all x1, starting transfers between devices, local(): lax.all_to_all(buckets, ('gx', 'gy'), split_axis=0, concat_axis=0, tiled=...  5.37 us
    pallas_call x1, Pallas kernels, outgoing(): pl.pallas_call(functools.partial(send_kernel, ndev, ngy, chunk, group), o...  5.23 us
    ppermute x1, starting transfers between devices, local(): top = lax.ppermute(down, 'gx', ahead(ngx))  2.64 us
    ppermute x1, starting transfers between devices, local(): bottom = lax.ppermute(up, 'gx', behind(ngx))  2.11 us
    ppermute x1, starting transfers between devices, local(): west = lax.ppermute(to_east, 'gy', ahead(ngy))  1.97 us
    pallas_call x1, Pallas kernels, collect(): pl.pallas_call(functools.partial(collect_kernel, ndev), out_shape=(jax.Sh...  1.91 us
    ppermute x1, waiting for transfers between devices, local(): west = lax.ppermute(to_east, 'gy', ahead(ngy))  1.61 us
  transfers between devices with their start and end apart: 6, of which 2 were waited for; matrix products, arithmetic and copies ran while one was open for 0% of the time, Pallas kernels for 29%

profile of v4, /device:TPU:0, one launch (start us, length us, event | category | flops | bytes accessed | tf_op | source)
XLA Modules:
  0.0 34.0 jit_solution(7879632281086423682)
XLA Ops:
  0.6 5.2 %shard_map.86 = (f32[1040,128]{1,0:T(8,128)}, f32[136,128]{1,0:T(8,128)}, f32[136,128]{1,0:T(8,128)}, f32[528,128]{1,0:T(8,128)}) custom-call(s32[64]{0:T(128)} %bitcast.16, s32[64]{0:T(128)} %bitcast.17, s32[64]{0:T(128)} %bitcast.18, s32[128,128]{1,0:T(8,128)} %mask.1, f32[1024,128]{1,0:T(8,128)} %bitcast.15, bf16[64,128,128]{2,1,0:T(8,128)(2,1)} %bitcast.14, ...), custom_call_target="tpu_custom_call" | custom-call | flops 100000000 | bytes 8000000 | tf_op jit(solution)/shard_map/pallas_call | solution.py:144
  5.9 0.5 %collective-permute-start = (f32[1040,128]{1,0:T(8,128)}, f32[1040,128]{1,0:T(8,128)}, u32[]{:S(2)}, u32[]{:S(2)}) collective-permute-start(f32[1040,128]{1,0:T(8,128)} %get-tuple-element.11), channel_id=1, source_target_pairs={{0,16},{16,0},{1,17},{17,1},{2,18},{18,2},{3,19},{19,3},{4,20},{20... | collective-permute-start | bytes 1597448 | tf_op jit(solution)/shard_map/ppermute | solution.py:498
  6.4 2.6 %collective-permute-start.1 = (f32[136,128]{1,0:T(8,128)}, f32[136,128]{1,0:T(8,128)S(1)}, u32[]{:S(2)}, u32[]{:S(2)}) collective-permute-start(f32[136,128]{1,0:T(8,128)} %get-tuple-element.12), channel_id=1, source_target_pairs={{0,4},{4,8},{8,12},{12,0},{1,5},{5,9},{9,13},{13,1},{2,6},{6,10},{... | collective-permute-start | bytes 208904 | tf_op jit(solution)/shard_map/ppermute | solution.py:496
  9.0 2.1 %collective-permute-start.2 = (f32[136,128]{1,0:T(8,128)}, f32[136,128]{1,0:T(8,128)S(1)}, u32[]{:S(2)}, u32[]{:S(2)}) collective-permute-start(f32[136,128]{1,0:T(8,128)} %get-tuple-element.13), channel_id=1, source_target_pairs={{4,0},{8,4},{12,8},{0,12},{5,1},{9,5},{13,9},{1,13},{6,2},{10,6},{... | collective-permute-start | bytes 208904 | tf_op jit(solution)/shard_map/ppermute | solution.py:497
  11.1 0.0 collective-permute-done
  11.1 5.4 %all-to-all-start = ((f32[16,65,1,128]{3,2,1,0:T(1,128)}), f32[16,65,1,128]{3,2,1,0:T(1,128)S(1)}, u32[]{:S(2)}, u32[]{:S(2)}) async-start(f32[16,65,1,128]{3,2,1,0:T(1,128)} %bitcast.6), calls=%async_computation | async-start | bytes 1064960 | tf_op jit(solution)/shard_map/all_to_all | solution.py:501
  16.5 0.0 collective-permute-done.1.refs_0_.top
  16.5 0.0 collective-permute-done.2.refs_1_.bottom
  16.5 0.0 copy-start.1
  16.6 0.9 %copy-done.1 = f32[528,128]{1,0:T(8,128)S(1)} copy-done((f32[528,128]{1,0:T(8,128)S(1)}, f32[528,128]{1,0:T(8,128)}, u32[]{:S(2)}) %copy-start.1) | copy-done | bytes 270360
  17.5 0.0 copy-start
  17.5 0.0 copy-start.2
  17.5 0.1 shard_map.88
  17.6 2.0 %collective-permute-start.3 = (f32[136,128]{1,0:T(8,128)S(1)}, f32[136,128]{1,0:T(8,128)S(1)}, u32[]{:S(2)}, u32[]{:S(2)}) collective-permute-start(f32[136,128]{1,0:T(8,128)S(1)} %get-tuple-element.14), channel_id=1, source_target_pairs={{0,1},{1,2},{2,3},{3,0},{4,5},{5,6},{6,7},{7,4},{8,9},{9,10},{10,1... | collective-permute-start | bytes 208904 | tf_op jit(solution)/shard_map/ppermute | solution.py:504
  19.6 1.0 %collective-permute-start.4 = (f32[136,128]{1,0:T(8,128)S(1)}, f32[136,128]{1,0:T(8,128)S(1)}, u32[]{:S(2)}, u32[]{:S(2)}) collective-permute-start(f32[136,128]{1,0:T(8,128)S(1)} %get-tuple-element.15), channel_id=1, source_target_pairs={{1,0},{2,1},{3,2},{0,3},{5,4},{6,5},{7,6},{4,7},{9,8},{10,9},{11,1... | collective-permute-start | bytes 208904 | tf_op jit(solution)/shard_map/ppermute | solution.py:505
  20.6 0.0 copy-done
  20.6 0.0 copy-done.2
  20.6 3.6 %shard_map.87.x = f32[64,128,128]{2,1,0:T(8,128)S(1)} custom-call(f32[528,128]{1,0:T(8,128)S(1)} %copy-done.2, f32[64,128,128]{2,1,0:T(8,128)S(1)} %bitcast.11, f32[136,128]{1,0:T(8,128)S(1)} %collective-permute-done.1.refs_0_.top, f32[136,128]{1,0:T(8,128)S(1)} %collective-permute-done.2.refs_1_.bottom), custom_call_target="tpu_custom_call" | custom-call | flops 5000000000 | bytes 100000 | tf_op jit(solution)/shard_map/pallas_call | solution.py:398
  24.2 1.6 %collective-permute-done.3.west = f32[136,128]{1,0:T(8,128)S(1)} collective-permute-done((f32[136,128]{1,0:T(8,128)S(1)}, f32[136,128]{1,0:T(8,128)S(1)}, u32[]{:S(2)}, u32[]{:S(2)}) %collective-permute-start.3) | collective-permute-done | bytes 69664 | tf_op jit(solution)/shard_map/ppermute | solution.py:504
  25.8 0.0 collective-permute-done.4.east
  25.8 0.7 %shard_map.89.refs_0_ = f32[384,128]{1,0:T(8,128)S(1)} custom-call(f32[528,128]{1,0:T(8,128)S(1)} %copy-done.2, f32[136,128]{1,0:T(8,128)S(1)} %collective-permute-done.1.refs_0_.top, f32[136,128]{1,0:T(8,128)S(1)} %collective-permute-done.2.refs_1_.bottom, f32[136,128]{1,0:T(8,128)S(1)} %collective-permute-done.3.west, ...), custom_call_target="tpu_custom_call" | custom-call | flops 1000000 | bytes 100000 | tf_op jit(solution)/shard_map/pallas_call | solution.py:285
  26.5 5.5 %shard_map.90.second = f32[64,128,128]{2,1,0:T(8,128)} custom-call(f32[528,128]{1,0:T(8,128)S(1)} %copy-done.2, f32[64,128,128]{2,1,0:T(8,128)S(1)} %shard_map.87.x, f32[384,128]{1,0:T(8,128)S(1)} %shard_map.89.refs_0_), custom_call_target="tpu_custom_call" | custom-call | flops 1000000 | bytes 100000 | tf_op jit(solution)/shard_map/pallas_call | solution.py:398
  32.0 0.1 all-to-all-done
  32.1 1.9 %shard_map.91 = (f32[64,128,128]{2,1,0:T(8,128)}, f32[8,128,128]{2,1,0:T(8,128)}) custom-call(f32[528,128]{1,0:T(8,128)S(1)} %copy-done.2, f32[1040,128]{1,0:T(8,128)S(1)} %bitcast.12, f32[64,128,128]{2,1,0:T(8,128)} %shard_map.90.second), custom_call_target="tpu_custom_call", output_to_operand_aliasing={{0}: (2, {})} | custom-call | flops 100000000 | bytes 2000000 | tf_op jit(solution)/shard_map/pallas_call | solution.py:457
Async XLA Ops:
  5.9 5.3 %collective-permute-start = (f32[1040,128]{1,0:T(8,128)}, f32[1040,128]{1,0:T(8,128)}, u32[]{:S(2)}, u32[]{:S(2)}) collective-permute-start(f32[1040,128]{1,0:T(8,128)} %get-tuple-element.11), channel_id=1, source_target_pairs={{0,16},{16,0},{1,17},{17,1},{2,18},{18,2},{3,19},{19,3},{4,20},{20... | collective-permute-start | bytes 1597448 | tf_op jit(solution)/shard_map/ppermute | solution.py:498
  6.4 10.1 %collective-permute-start.1 = (f32[136,128]{1,0:T(8,128)}, f32[136,128]{1,0:T(8,128)S(1)}, u32[]{:S(2)}, u32[]{:S(2)}) collective-permute-start(f32[136,128]{1,0:T(8,128)} %get-tuple-element.12), channel_id=1, source_target_pairs={{0,4},{4,8},{8,12},{12,0},{1,5},{5,9},{9,13},{13,1},{2,6},{6,10},{... | collective-permute-start | bytes 208904 | tf_op jit(solution)/shard_map/ppermute | solution.py:496
  9.0 7.5 %collective-permute-start.2 = (f32[136,128]{1,0:T(8,128)}, f32[136,128]{1,0:T(8,128)S(1)}, u32[]{:S(2)}, u32[]{:S(2)}) collective-permute-start(f32[136,128]{1,0:T(8,128)} %get-tuple-element.13), channel_id=1, source_target_pairs={{4,0},{8,4},{12,8},{0,12},{5,1},{9,5},{13,9},{1,13},{6,2},{10,6},{... | collective-permute-start | bytes 208904 | tf_op jit(solution)/shard_map/ppermute | solution.py:497
  11.1 20.9 %all-to-all-start = ((f32[16,65,1,128]{3,2,1,0:T(1,128)}), f32[16,65,1,128]{3,2,1,0:T(1,128)S(1)}, u32[]{:S(2)}, u32[]{:S(2)}) async-start(f32[16,65,1,128]{3,2,1,0:T(1,128)} %bitcast.6), calls=%async_computation | async-start | bytes 1064960 | tf_op jit(solution)/shard_map/all_to_all | solution.py:501
  16.5 1.0 %copy-start.1 = (f32[528,128]{1,0:T(8,128)S(1)}, f32[528,128]{1,0:T(8,128)}, u32[]{:S(2)}) copy-start(f32[528,128]{1,0:T(8,128)} %get-tuple-element.10.own) | copy-start | bytes 811012
  17.5 3.1 %copy-start = (f32[1,64,128,128]{3,2,1,0:T(8,128)S(1)}, f32[1,64,128,128]{3,2,1,0:T(8,128)}, u32[]{:S(2)}) copy-start(f32[1,64,128,128]{3,2,1,0:T(8,128)} %param.7) | copy-start | bytes 12582916
  17.5 3.1 %copy-start.2 = (f32[528,128]{1,0:T(8,128)S(1)}, f32[528,128]{1,0:T(8,128)}, u32[]{:S(2)}) copy-start(f32[528,128]{1,0:T(8,128)} %get-tuple-element.10.own) | copy-start | bytes 811012
  17.6 8.2 %collective-permute-start.3 = (f32[136,128]{1,0:T(8,128)S(1)}, f32[136,128]{1,0:T(8,128)S(1)}, u32[]{:S(2)}, u32[]{:S(2)}) collective-permute-start(f32[136,128]{1,0:T(8,128)S(1)} %get-tuple-element.14), channel_id=1, source_target_pairs={{0,1},{1,2},{2,3},{3,0},{4,5},{5,6},{6,7},{7,4},{8,9},{9,10},{10,1... | collective-permute-start | bytes 208904 | tf_op jit(solution)/shard_map/ppermute | solution.py:504
  19.6 6.2 %collective-permute-start.4 = (f32[136,128]{1,0:T(8,128)S(1)}, f32[136,128]{1,0:T(8,128)S(1)}, u32[]{:S(2)}, u32[]{:S(2)}) collective-permute-start(f32[136,128]{1,0:T(8,128)S(1)} %get-tuple-element.15), channel_id=1, source_target_pairs={{1,0},{2,1},{3,2},{0,3},{5,4},{6,5},{7,6},{4,7},{9,8},{10,9},{11,1... | collective-permute-start | bytes 208904 | tf_op jit(solution)/shard_map/ppermute | solution.py:505

commit v5 on v4

--- a/solution.py
+++ b/solution.py
@@ -165,9 +165,14 @@
             pltpu.SemaphoreType.DMA((tiles // chunk,)),
             pltpu.SemaphoreType.DMA((lev // group,)),
         ],
-        compiler_params=params(LIMIT),
+        compiler_params=params(16),
         cost_estimate=pl.CostEstimate(flops=10**8, bytes_accessed=8 * 10**6, transcendentals=0),
-    )(tile_source, tile_target, tile_row, mask, surface, weights, state)
+    )(
+        *[
+            pltpu.with_memory_space_constraint(x, pltpu.HBM)
+            for x in (tile_source, tile_target, tile_row, mask, surface, weights, state)
+        ]
+    )
 
 
 def shifted(x, by, axis):
@@ -294,25 +299,16 @@
 
 def step_kernel(ngx, group, second, own, x, *refs):
     if second:
-        ring, out, hwet, buf, res, sems, osems = refs
+        ring, out, surface, hwet, buf, res, osems = refs
     else:
-        top, bottom, out, hwet, buf, res, sems, osems = refs
+        top, bottom, res, hwet, buf = refs
     lev, cx, cy = x.shape
     pieces = lev // group
-
-    def arrive(i):
-        return pltpu.make_async_copy(
-            x.at[pl.ds(i * group, group)],
-            buf.at[pl.ds(i * group + 1, group), pl.ds(PAD, cx), :],
-            sems.at[i],
-        )
 
     def leave(i):
         part = pl.ds(i * group, group)
         return pltpu.make_async_copy(res.at[part], out.at[part], osems.at[i])
 
-    for i in range(pieces):
-        arrive(i).start()
     ocean = lax.axis_index("mp") == 1
     horiz = jnp.where(ocean, HORIZ[1], HORIZ[0]).astype(jnp.float32)
     vert = jnp.where(ocean, VERT[1], VERT[0]).astype(jnp.float32)
@@ -352,14 +348,11 @@
         return jnp.where(ends, pltpu.roll(sides, (cy - 2 * j) % cy, 1), 0.0)
 
     def accept(i):
-        arrive(i).wait()
         sides = columns(0, i * group) if second else None
         for j in range(group):
-            here = (i * group + j + 1, slice(PAD, PAD + cx), slice(None))
-            if second:
-                buf[here] = buf[here] + at_ends(sides, j)
-            else:
-                buf[here] = buf[here] * wet[...]
+            here = x[i * group + j]
+            here = here + at_ends(sides, j) if second else here * wet[...]
+            buf[i * group + j + 1, PAD : PAD + cx, :] = here
 
     def levels(start, count):
         sides = columns(1, start) if second else None
@@ -378,35 +371,38 @@
 
     accept(0)
     levels(0, group - 1)
+    if second:
+        surface[...] = res[0]
 
     def middle(i, _):
         accept(i)
         levels(i * group - 1, group)
-        leave(i - 1).start()
+        if second:
+            leave(i - 1).start()
         return 0
 
     lax.fori_loop(1, pieces, middle, 0)
     levels(lev - 1, 1)
-    leave(pieces - 1).start()
-    for i in range(pieces):
-        leave(i).wait()
+    if second:
+        leave(pieces - 1).start()
+        for i in range(pieces):
+            leave(i).wait()
 
 
 def one_step(own, x, outside, ngx, second):
     lev, cx, cy = x.shape
     group = 8
+    whole = jax.ShapeDtypeStruct(x.shape, jnp.float32)
     return pl.pallas_call(
         functools.partial(step_kernel, ngx, group, second),
-        out_shape=jax.ShapeDtypeStruct(x.shape, jnp.float32),
-        in_specs=[VMEM, ANY] + [VMEM] * len(outside),
-        out_specs=ANY,
+        out_shape=(whole, jax.ShapeDtypeStruct((cx, cy), jnp.float32)) if second else whole,
+        in_specs=[VMEM] * (2 + len(outside)),
+        out_specs=(ANY, VMEM) if second else VMEM,
         scratch_shapes=[
             pltpu.VMEM((cx, cy), jnp.float32),
             pltpu.VMEM((lev + 2, cx + 2 * PAD, cy), jnp.float32),
-            pltpu.VMEM(x.shape, jnp.float32),
-            pltpu.SemaphoreType.DMA((lev // group,)),
-            pltpu.SemaphoreType.DMA((lev // group,)),
-        ],
+        ]
+        + [pltpu.VMEM(x.shape, jnp.float32), pltpu.SemaphoreType.DMA((lev // group,))] * second,
         compiler_params=params(16),
         cost_estimate=pl.CostEstimate(
             flops=10**6 if second else FIRST_COST, bytes_accessed=10**5, transcendentals=0
@@ -414,17 +410,16 @@
     )(own, x, *outside)
 
 
-def collect_kernel(ndev, own, got, second, out, received, level, onehot, sums, sems, rsems):
+def collect_kernel(ndev, own, got, surface, second, out, received, level, onehot, sums, sems, rsems):
     block = got.shape[0] // ndev
     extra = block - 8 * CAP
     fields, cx, cy = received.shape
     slots = ndev * CAP
-    fetch = pltpu.make_async_copy(second.at[0], level, sems.at[0])
-    fetch.start()
-    store = pltpu.make_async_copy(level, out.at[0], sems.at[1])
-
-    def leave(k):
-        return pltpu.make_async_copy(sums.at[k], received.at[k], rsems.at[k])
+    store = pltpu.make_async_copy(level, out.at[0], sems.at[0])
+
+    def leave(i):
+        part = pl.ds(i * fields // 2, fields // 2)
+        return pltpu.make_async_copy(sums.at[part], received.at[part], rsems.at[i])
 
     labels = got[block - extra : block, :]
     for s in range(1, ndev):
@@ -442,17 +437,18 @@
         sums[k] = jnp.dot(
             onehot[...], jnp.concatenate([high, low], axis=0), preferred_element_type=jnp.float32
         )
-        leave(k).start()
+        if k == fields // 2 - 1:
+            leave(0).start()
         if k == 0:
-            fetch.wait()
-            level[...] = level[...] + FORCE * own[0:cx, :] * sums[0]
+            level[...] = surface[...] + FORCE * own[0:cx, :] * sums[0]
             store.start()
+    leave(1).start()
     store.wait()
-    for k in range(fields):
-        leave(k).wait()
-
-
-def collect(own, got, second, fields, ndev):
+    leave(0).wait()
+    leave(1).wait()
+
+
+def collect(own, got, surface, second, fields, ndev):
     _, cx, cy = second.shape
     return pl.pallas_call(
         functools.partial(collect_kernel, ndev),
@@ -460,19 +456,19 @@
             jax.ShapeDtypeStruct(second.shape, jnp.float32),
             jax.ShapeDtypeStruct((fields, cx, cy), jnp.float32),
         ),
-        in_specs=[VMEM, VMEM, ANY],
+        in_specs=[VMEM, VMEM, VMEM, ANY],
         out_specs=(ANY, ANY),
         scratch_shapes=[
             pltpu.VMEM((cx, cy), jnp.float32),
             pltpu.VMEM((cx, 2 * ndev * CAP), jnp.bfloat16),
             pltpu.VMEM((fields, cx, cy), jnp.float32),
+            pltpu.SemaphoreType.DMA((1,)),
             pltpu.SemaphoreType.DMA((2,)),
-            pltpu.SemaphoreType.DMA((fields,)),
         ],
-        input_output_aliases={2: 0},
+        input_output_aliases={3: 0},
         compiler_params=params(16),
         cost_estimate=pl.CostEstimate(flops=10**8, bytes_accessed=2 * 10**6, transcendentals=0),
-    )(own, got, second)
+    )(own, got, surface, second)
 
 
 def local(states, surface, land_mask, tile_weights, tile_source, tile_target, tile_row):
@@ -505,8 +501,8 @@
     east = lax.ppermute(to_west, "gy", behind(ngy))
     first = one_step(own, state, (top, bottom), ngx, False)
     ring = outer_ring(own, top, bottom, west, east, ngx, ngy)
-    second = one_step(own, first, (ring,), ngx, True)
-    new_state, received = collect(own, got, second, fields, ndev)
+    second, level = one_step(own, first, (ring,), ngx, True)
+    new_state, received = collect(own, got, level, second, fields, ndev)
     return new_state[None], received[None]
 
 

time: 34.3 us -> 32.5 us (0.948)
  Pallas kernels: 17 us -> 14.3 us
  waiting for transfers between devices: 1.69 us -> 3.83 us
  local copies, waits for them, and re-layouts: 0.96 us -> 0.01 us
    pallas_call x2, Pallas kernels: 9.07 us -> 7.86 us  [one_step(): pl.pallas_call(functools.partial(step_kernel, ngx, group, second), out_sh...]
    ppermute x1, waiting for transfers between devices: 0.01 us -> 1.17 us  [local(): east = lax.ppermute(to_west, 'gy', behind(ngy))]
    unnamed x6 -> x2, local copies, waits for them, and re-layouts: 0.96 us -> 0.01 us
    pallas_call x1, Pallas kernels: 1.91 us -> 1.07 us  [collect(): pl.pallas_call(functools.partial(collect_kernel, ndev), out_shape=(jax.Sh...]
    pallas_call x1, Pallas kernels: 5.23 us -> 4.54 us  [outgoing(): pl.pallas_call(functools.partial(send_kernel, ndev, ngy, chunk, group), o...]
    all_to_all x1, waiting for transfers between devices: 0.07 us -> 0.55 us  [local(): lax.all_to_all(buckets, ('gx', 'gy'), split_axis=0, concat_axis=0, tiled=...]
    ppermute x1, waiting for transfers between devices: 1.61 us -> 2.1 us  [local(): west = lax.ppermute(to_east, 'gy', ahead(ngy))]
  transfers between devices with their start and end apart: 6 -> 6, of which waited for: 2 -> 3; matrix products, arithmetic and copies ran while one was open for 0% -> 0% of each run, Pallas kernels for 29% -> 27%
where the time goes in v5:
time: 32.5 us; the launch traced here: 32.2 us
  Pallas kernels  14.3 us (44%)
  starting transfers between devices  13.4 us (41%)
  waiting for transfers between devices  3.83 us (12%)
  between operations  0.7 us (2%)
    pallas_call x2, Pallas kernels, one_step(): pl.pallas_call(functools.partial(step_kernel, ngx, group, second), out_sh...  7.86 us
    all_to_all x1, starting transfers between devices, local(): lax.all_to_all(buckets, ('gx', 'gy'), split_axis=0, concat_axis=0, tiled=...  5.21 us
    pallas_call x1, Pallas kernels, outgoing(): pl.pallas_call(functools.partial(send_kernel, ndev, ngy, chunk, group), o...  4.54 us
    ppermute x1, starting transfers between devices, local(): top = lax.ppermute(down, 'gx', ahead(ngx))  2.64 us
    ppermute x1, starting transfers between devices, local(): bottom = lax.ppermute(up, 'gx', behind(ngx))  2.11 us
    ppermute x1, waiting for transfers between devices, local(): west = lax.ppermute(to_east, 'gy', ahead(ngy))  2.1 us
    ppermute x1, starting transfers between devices, local(): west = lax.ppermute(to_east, 'gy', ahead(ngy))  1.97 us
    ppermute x1, waiting for transfers between devices, local(): east = lax.ppermute(to_west, 'gy', behind(ngy))  1.17 us
  transfers between devices with their start and end apart: 6, of which 3 were waited for; matrix products, arithmetic and copies ran while one was open for 0% of the time, Pallas kernels for 27%

profile of v5, /device:TPU:0, one launch (start us, length us, event | category | flops | bytes accessed | tf_op | source)
XLA Modules:
  0.0 32.2 jit_solution(11474950622837986982)
XLA Ops:
  0.6 4.5 %shard_map.86 = (f32[1040,128]{1,0:T(8,128)S(1)}, f32[136,128]{1,0:T(8,128)S(1)}, f32[136,128]{1,0:T(8,128)S(1)}, f32[528,128]{1,0:T(8,128)S(1)}) custom-call(s32[64]{0:T(128)} %bitcast.16, s32[64]{0:T(128)} %bitcast.17, s32[64]{0:T(128)} %bitcast.18, s32[128,128]{1,0:T(8,128)} %mask.1, f32[1024,128]{1,0:T(8,128)} %bitcast.15, ...), custom_call_target="tpu_custom_call" | custom-call | flops 100000000 | bytes 8000000 | tf_op jit(solution)/shard_map/pallas_call | solution.py:144
  5.2 0.5 %collective-permute-start = (f32[1040,128]{1,0:T(8,128)S(1)}, f32[1040,128]{1,0:T(8,128)}, u32[]{:S(2)}, u32[]{:S(2)}) collective-permute-start(f32[1040,128]{1,0:T(8,128)S(1)} %get-tuple-element.13), channel_id=1, source_target_pairs={{0,16},{16,0},{1,17},{17,1},{2,18},{18,2},{3,19},{19,3},{4,20},{20... | collective-permute-start | bytes 1597448 | tf_op jit(solution)/shard_map/ppermute | solution.py:494
  5.7 2.6 %collective-permute-start.1 = (f32[136,128]{1,0:T(8,128)S(1)}, f32[136,128]{1,0:T(8,128)S(1)}, u32[]{:S(2)}, u32[]{:S(2)}) collective-permute-start(f32[136,128]{1,0:T(8,128)S(1)} %get-tuple-element.14), channel_id=1, source_target_pairs={{0,4},{4,8},{8,12},{12,0},{1,5},{5,9},{9,13},{13,1},{2,6},{6,10},{... | collective-permute-start | bytes 208904 | tf_op jit(solution)/shard_map/ppermute | solution.py:492
  8.3 2.1 %collective-permute-start.2 = (f32[136,128]{1,0:T(8,128)S(1)}, f32[136,128]{1,0:T(8,128)S(1)}, u32[]{:S(2)}, u32[]{:S(2)}) collective-permute-start(f32[136,128]{1,0:T(8,128)S(1)} %get-tuple-element.15), channel_id=1, source_target_pairs={{4,0},{8,4},{12,8},{0,12},{5,1},{9,5},{13,9},{1,13},{6,2},{10,6},{... | collective-permute-start | bytes 208904 | tf_op jit(solution)/shard_map/ppermute | solution.py:493
  10.4 0.0 collective-permute-done
  10.4 5.2 %all-to-all-start = ((f32[16,65,1,128]{3,2,1,0:T(1,128)}), f32[16,65,1,128]{3,2,1,0:T(1,128)S(1)}, u32[]{:S(2)}, u32[]{:S(2)}) async-start(f32[16,65,1,128]{3,2,1,0:T(1,128)} %bitcast.6), calls=%async_computation | async-start | bytes 1064960 | tf_op jit(solution)/shard_map/all_to_all | solution.py:497
  15.7 0.0 collective-permute-done.1.refs_0_.top
  15.7 0.0 collective-permute-done.2.refs_1_.bottom
  15.7 0.0 copy-start
  15.7 0.1 shard_map.88
  15.8 2.0 %collective-permute-start.3 = (f32[136,128]{1,0:T(8,128)S(1)}, f32[136,128]{1,0:T(8,128)S(1)}, u32[]{:S(2)}, u32[]{:S(2)}) collective-permute-start(f32[136,128]{1,0:T(8,128)S(1)} %get-tuple-element.16), channel_id=1, source_target_pairs={{0,1},{1,2},{2,3},{3,0},{4,5},{5,6},{6,7},{7,4},{8,9},{9,10},{10,1... | collective-permute-start | bytes 208904 | tf_op jit(solution)/shard_map/ppermute | solution.py:500
  17.8 1.0 %collective-permute-start.4 = (f32[136,128]{1,0:T(8,128)S(1)}, f32[136,128]{1,0:T(8,128)S(1)}, u32[]{:S(2)}, u32[]{:S(2)}) collective-permute-start(f32[136,128]{1,0:T(8,128)S(1)} %get-tuple-element.17), channel_id=1, source_target_pairs={{1,0},{2,1},{3,2},{0,3},{5,4},{6,5},{7,6},{4,7},{9,8},{10,9},{11,1... | collective-permute-start | bytes 208904 | tf_op jit(solution)/shard_map/ppermute | solution.py:501
  18.8 0.0 copy-done
  18.8 2.8 %shard_map.87.x = f32[64,128,128]{2,1,0:T(8,128)S(1)} custom-call(f32[528,128]{1,0:T(8,128)S(1)} %get-tuple-element.12.own, f32[64,128,128]{2,1,0:T(8,128)S(1)} %bitcast.11, f32[136,128]{1,0:T(8,128)S(1)} %collective-permute-done.1.refs_0_.top, f32[136,128]{1,0:T(8,128)S(1)} %collective-permute-done.2.refs_1_.bottom), custom_call_target="tpu_custom_call" | custom-call | flops 5000000000 | bytes 100000 | tf_op jit(solution)/shard_map/pallas_call | solution.py:396
  21.6 2.1 %collective-permute-done.3.west = f32[136,128]{1,0:T(8,128)S(1)} collective-permute-done((f32[136,128]{1,0:T(8,128)S(1)}, f32[136,128]{1,0:T(8,128)S(1)}, u32[]{:S(2)}, u32[]{:S(2)}) %collective-permute-start.3) | collective-permute-done | bytes 69664 | tf_op jit(solution)/shard_map/ppermute | solution.py:500
  23.7 1.2 %collective-permute-done.4.east = f32[136,128]{1,0:T(8,128)S(1)} collective-permute-done((f32[136,128]{1,0:T(8,128)S(1)}, f32[136,128]{1,0:T(8,128)S(1)}, u32[]{:S(2)}, u32[]{:S(2)}) %collective-permute-start.4) | collective-permute-done | bytes 69664 | tf_op jit(solution)/shard_map/ppermute | solution.py:501
  24.8 0.7 %shard_map.89.refs_0_ = f32[384,128]{1,0:T(8,128)S(1)} custom-call(f32[528,128]{1,0:T(8,128)S(1)} %get-tuple-element.12.own, f32[136,128]{1,0:T(8,128)S(1)} %collective-permute-done.1.refs_0_.top, f32[136,128]{1,0:T(8,128)S(1)} %collective-permute-done.2.refs_1_.bottom, f32[136,128]{1,0:T(8,128)S(1)} %collective-permute-done.3.west, ...), custom_call_target="tpu_custom_call" | custom-call | flops 1000000 | bytes 100000 | tf_op jit(solution)/shard_map/pallas_call | solution.py:290
  25.5 5.1 %shard_map.90 = (f32[64,128,128]{2,1,0:T(8,128)}, f32[128,128]{1,0:T(8,128)S(1)}) custom-call(f32[528,128]{1,0:T(8,128)S(1)} %get-tuple-element.12.own, f32[64,128,128]{2,1,0:T(8,128)S(1)} %shard_map.87.x, f32[384,128]{1,0:T(8,128)S(1)} %shard_map.89.refs_0_), custom_call_target="tpu_custom_call" | custom-call | flops 1000000 | bytes 100000 | tf_op jit(solution)/shard_map/pallas_call | solution.py:396
  30.6 0.6 %all-to-all-done = f32[16,65,1,128]{3,2,1,0:T(1,128)S(1)} async-done(((f32[16,65,1,128]{3,2,1,0:T(1,128)}), f32[16,65,1,128]{3,2,1,0:T(1,128)S(1)}, u32[]{:S(2)}, u32[]{:S(2)}) %all-to-all-start) | async-done | bytes 532512 | tf_op jit(solution)/shard_map/all_to_all | solution.py:497
  31.2 1.1 %shard_map.91 = (f32[64,128,128]{2,1,0:T(8,128)}, f32[8,128,128]{2,1,0:T(8,128)}) custom-call(f32[528,128]{1,0:T(8,128)S(1)} %get-tuple-element.12.own, f32[1040,128]{1,0:T(8,128)S(1)} %bitcast.12, f32[128,128]{1,0:T(8,128)S(1)} %get-tuple-element.18.surface, f32[64,128,128]{2,1,0:T(8,128)} %get-tuple-element.19.second), custom_call_target="tpu_custom_call", output_to_operand_aliasing={{0}: (3, {})} | custom-call | flops 100000000 | bytes 2000000 | tf_op jit(solution)/shard_map/pallas_call | solution.py:453
Async XLA Ops:
  5.2 5.3 %collective-permute-start = (f32[1040,128]{1,0:T(8,128)S(1)}, f32[1040,128]{1,0:T(8,128)}, u32[]{:S(2)}, u32[]{:S(2)}) collective-permute-start(f32[1040,128]{1,0:T(8,128)S(1)} %get-tuple-element.13), channel_id=1, source_target_pairs={{0,16},{16,0},{1,17},{17,1},{2,18},{18,2},{3,19},{19,3},{4,20},{20... | collective-permute-start | bytes 1597448 | tf_op jit(solution)/shard_map/ppermute | solution.py:494
  5.7 10.0 %collective-permute-start.1 = (f32[136,128]{1,0:T(8,128)S(1)}, f32[136,128]{1,0:T(8,128)S(1)}, u32[]{:S(2)}, u32[]{:S(2)}) collective-permute-start(f32[136,128]{1,0:T(8,128)S(1)} %get-tuple-element.14), channel_id=1, source_target_pairs={{0,4},{4,8},{8,12},{12,0},{1,5},{5,9},{9,13},{13,1},{2,6},{6,10},{... | collective-permute-start | bytes 208904 | tf_op jit(solution)/shard_map/ppermute | solution.py:492
  8.3 7.3 %collective-permute-start.2 = (f32[136,128]{1,0:T(8,128)S(1)}, f32[136,128]{1,0:T(8,128)S(1)}, u32[]{:S(2)}, u32[]{:S(2)}) collective-permute-start(f32[136,128]{1,0:T(8,128)S(1)} %get-tuple-element.15), channel_id=1, source_target_pairs={{4,0},{8,4},{12,8},{0,12},{5,1},{9,5},{13,9},{1,13},{6,2},{10,6},{... | collective-permute-start | bytes 208904 | tf_op jit(solution)/shard_map/ppermute | solution.py:493
  10.4 20.7 %all-to-all-start = ((f32[16,65,1,128]{3,2,1,0:T(1,128)}), f32[16,65,1,128]{3,2,1,0:T(1,128)S(1)}, u32[]{:S(2)}, u32[]{:S(2)}) async-start(f32[16,65,1,128]{3,2,1,0:T(1,128)} %bitcast.6), calls=%async_computation | async-start | bytes 1064960 | tf_op jit(solution)/shard_map/all_to_all | solution.py:497
  15.7 3.1 %copy-start = (f32[1,64,128,128]{3,2,1,0:T(8,128)S(1)}, f32[1,64,128,128]{3,2,1,0:T(8,128)}, u32[]{:S(2)}) copy-start(f32[1,64,128,128]{3,2,1,0:T(8,128)} %param.7) | copy-start | bytes 12582916
  15.8 7.8 %collective-permute-start.3 = (f32[136,128]{1,0:T(8,128)S(1)}, f32[136,128]{1,0:T(8,128)S(1)}, u32[]{:S(2)}, u32[]{:S(2)}) collective-permute-start(f32[136,128]{1,0:T(8,128)S(1)} %get-tuple-element.16), channel_id=1, source_target_pairs={{0,1},{1,2},{2,3},{3,0},{4,5},{5,6},{6,7},{7,4},{8,9},{9,10},{10,1... | collective-permute-start | bytes 208904 | tf_op jit(solution)/shard_map/ppermute | solution.py:500
  17.8 7.0 %collective-permute-start.4 = (f32[136,128]{1,0:T(8,128)S(1)}, f32[136,128]{1,0:T(8,128)S(1)}, u32[]{:S(2)}, u32[]{:S(2)}) collective-permute-start(f32[136,128]{1,0:T(8,128)S(1)} %get-tuple-element.17), channel_id=1, source_target_pairs={{1,0},{2,1},{3,2},{0,3},{5,4},{6,5},{7,6},{4,7},{9,8},{10,9},{11,1... | collective-permute-start | bytes 208904 | tf_op jit(solution)/shard_map/ppermute | solution.py:501

commit v6 on v5

--- a/solution.py
+++ b/solution.py
@@ -46,12 +46,13 @@
     src, tgt, row, count, labels, mbuf, sbuf, wbuf, buf, sems, wsems, usems,
 ):
     lev, cx, cy = state.shape
-    tiles = weights.shape[0]
+    tiles, band = weights.shape[0], 64
     wet, up_near, down_near, left, right = (own.at[part] for part in parts(lev, cx))
+    held = sbuf.at[pl.ds(0, surface.shape[0])]
     small = [
         pltpu.make_async_copy(a, b, sems.at[i])
         for i, (a, b) in enumerate(
-            ((tile_source, src), (tile_target, tgt), (tile_row, row), (mask, mbuf), (surface, sbuf))
+            ((tile_source, src), (tile_target, tgt), (tile_row, row), (mask, mbuf), (surface, held))
         )
     ]
     for copy in small:
@@ -61,8 +62,8 @@
         part = pl.ds(i * chunk, chunk)
         wcopies.append(pltpu.make_async_copy(weights.at[part], wbuf.at[part], wsems.at[i]))
         wcopies[-1].start()
-    for i in range(lev // group):
-        part = pl.ds(i * group, group)
+    for i in range(cx // band):
+        part = (slice(None), pl.ds(i * band, band), slice(None))
         ucopies.append(pltpu.make_async_copy(state.at[part], buf.at[part], usems.at[i]))
         ucopies[-1].start()
     block = out.shape[0] // ndev
@@ -77,24 +78,36 @@
         copy.wait()
     wet[...] = wet_of(mbuf)
 
-    def one(t, _):
-        s, d = src[t], tgt[t]
-        rank = count[d]
-        count[d] = rank + 1
-        picked = sbuf[pl.ds(s, 8, stride=cx), :] * wet[pl.ds(s, 1), :]
-        out[pl.ds(d * block + rank * 8, 8), :] = lax.dot_general(
-            picked.astype(jnp.bfloat16),
-            wbuf[t],
-            (((1,), (1,)), ((), ())),
+    per = 128 // 8
+    own_lanes = lanes((cy, 128)) // 8
+
+    def some(start):
+        picked = []
+        for t in range(start, start + per):
+            s = src[t]
+            picked.append(sbuf[pl.ds(s, 8, stride=cx), :] * wet[pl.ds(s, 1), :])
+        rounded = jnp.concatenate(picked, axis=0).astype(jnp.bfloat16).astype(jnp.float32)
+        turned = jnp.transpose(rounded)
+        apart = [jnp.where(own_lanes == i, turned, 0.0).astype(jnp.bfloat16) for i in range(per)]
+        total = jnp.dot(
+            jnp.concatenate([wbuf[start + i] for i in range(per)], axis=1),
+            jnp.concatenate(apart, axis=0),
             preferred_element_type=jnp.float32,
         )
-        label = (row[t] + 1).astype(jnp.float32)
-        labels[d] = jnp.where(place == me * CAP + rank, label, labels[d])
-        return 0
+        total = jnp.transpose(total)
+        for i in range(per):
+            t = start + i
+            d = tgt[t]
+            rank = count[d]
+            count[d] = rank + 1
+            out[pl.ds(d * block + rank * 8, 8), :] = total[i * 8 : (i + 1) * 8, :]
+            label = (row[t] + 1).astype(jnp.float32)
+            labels[d] = jnp.where(place == me * CAP + rank, label, labels[d])
 
     for i in range(tiles // chunk):
         wcopies[i].wait()
-        lax.fori_loop(i * chunk, (i + 1) * chunk, one, 0, unroll=True)
+        for start in range(i * chunk, (i + 1) * chunk, per):
+            some(start)
     for d in range(ndev):
         out[(d + 1) * block - extra : (d + 1) * block, :] = labels[d, 0:extra, :]
 
@@ -106,31 +119,23 @@
     strip = 32
     flat = buf.reshape(lev * cx, cy)
     lane = lanes((strip, cy))
-    for i in range(lev // group):
+    even, low_half = lane % 2 == 0, lane % 4 < 2
+    fours = lane // 4, lax.rem(lane + cy - 2, cy) // 4
+    for i in range(cx // band):
         ucopies[i].wait()
-        for dst, off, r in ((up, 0, 0), (up, lev, 1), (down, 0, cx - 1), (down, lev, cx - 2)):
-            dst[pl.ds(off + i * group, group), :] = (
-                flat[pl.ds(i * group * cx + r, group, stride=cx), :] * wet[r : r + 1, :]
-            )
-        for b in range(cx // strip):
+        for b in range(i * band // strip, (i + 1) * band // strip):
             rows = pl.ds(b * strip, strip)
-            if i == 0:
-                lo = hi = jnp.zeros((strip, cy), jnp.float32)
-            else:
-                lo, hi = left[rows, :], right[rows, :]
-            for l in range(i * group, (i + 1) * group):
+            gathered = [jnp.zeros((strip, cy), jnp.float32)] * 2
+            for l in range(lev):
                 moved = pltpu.roll(buf[l, rows, :], (2 * l + 2) % cy, 1)
-                at = (2 * l + 2) % cy
-                lo = jnp.where((lane == at) | (lane == at + 1), moved, lo)
-                hi = jnp.where((lane == 2 * l) | (lane == 2 * l + 1), moved, hi)
-            if i == lev // group - 1:
-                edge = wet[rows, :]
-                first, second = edge[:, 0:1], edge[:, 1:2]
-                lo = lo * jnp.where(lane % 2 == 0, first, second)
-                first, second = edge[:, cy - 2 : cy - 1], edge[:, cy - 1 :]
-                hi = hi * jnp.where(lane % 2 == 0, first, second)
-            left[rows, :] = lo
-            right[rows, :] = hi
+                gathered[l % 2] = jnp.where(fours[l % 2] == l // 2, moved, gathered[l % 2])
+            edge = wet[rows, :]
+            lo = jnp.where(low_half, gathered[1], gathered[0])
+            hi = jnp.where(low_half, gathered[0], gathered[1])
+            left[rows, :] = lo * jnp.where(even, edge[:, 0:1], edge[:, 1:2])
+            right[rows, :] = hi * jnp.where(even, edge[:, cy - 2 : cy - 1], edge[:, cy - 1 :])
+    for dst, off, r in ((up, 0, 0), (up, lev, 1), (down, 0, cx - 1), (down, lev, cx - 2)):
+        dst[off : off + lev, :] = flat[pl.ds(r, lev, stride=cx), :] * wet[r : r + 1, :]
     up_near[...] = up[0:lev, :]
     down_near[...] = down[0:lev, :]
 
@@ -158,12 +163,12 @@
             pltpu.SMEM((ndev,), jnp.int32),
             pltpu.VMEM((ndev, 8, 128), jnp.float32),
             pltpu.VMEM(mask.shape, jnp.int32),
-            pltpu.VMEM(surface.shape, jnp.float32),
+            pltpu.VMEM((surface.shape[0] + cx, cy), jnp.float32),
             pltpu.VMEM(weights.shape, weights.dtype),
             pltpu.VMEM(state.shape, jnp.float32),
             pltpu.SemaphoreType.DMA((5,)),
             pltpu.SemaphoreType.DMA((tiles // chunk,)),
-            pltpu.SemaphoreType.DMA((lev // group,)),
+            pltpu.SemaphoreType.DMA((4,)),
         ],
         compiler_params=params(16),
         cost_estimate=pl.CostEstimate(flops=10**8, bytes_accessed=8 * 10**6, transcendentals=0),

time: 32.5 us -> 32.2 us (level)
  no operation moved by 1% of the time
where the time goes in v6:
time: 32.2 us; the launch traced here: 32 us
  Pallas kernels  14 us (43%)
  starting transfers between devices  13.4 us (42%)
  waiting for transfers between devices  3.83 us (12%)
  between operations  0.69 us (2%)
    pallas_call x2, Pallas kernels, one_step(): pl.pallas_call(functools.partial(step_kernel, ngx, group, second), out_sh...  7.86 us
    all_to_all x1, starting transfers between devices, local(): lax.all_to_all(buckets, ('gx', 'gy'), split_axis=0, concat_axis=0, tiled=...  5.22 us
    pallas_call x1, Pallas kernels, outgoing(): pl.pallas_call(functools.partial(send_kernel, ndev, ngy, chunk, group), o...  4.31 us
    ppermute x1, starting transfers between devices, local(): top = lax.ppermute(down, 'gx', ahead(ngx))  2.64 us
    ppermute x1, waiting for transfers between devices, local(): west = lax.ppermute(to_east, 'gy', ahead(ngy))  2.1 us
    ppermute x1, starting transfers between devices, local(): bottom = lax.ppermute(up, 'gx', behind(ngx))  2.1 us
    ppermute x1, starting transfers between devices, local(): west = lax.ppermute(to_east, 'gy', ahead(ngy))  1.97 us
    ppermute x1, waiting for transfers between devices, local(): east = lax.ppermute(to_west, 'gy', behind(ngy))  1.17 us
  transfers between devices with their start and end apart: 6, of which 3 were waited for; matrix products, arithmetic and copies ran while one was open for 0% of the time, Pallas kernels for 27%

profile of v6, /device:TPU:0, one launch (start us, length us, event | category | flops | bytes accessed | tf_op | source)
XLA Modules:
  0.0 32.0 jit_solution(12486360972235429112)
XLA Ops:
  0.6 4.3 %shard_map.86 = (f32[1040,128]{1,0:T(8,128)S(1)}, f32[136,128]{1,0:T(8,128)S(1)}, f32[136,128]{1,0:T(8,128)S(1)}, f32[528,128]{1,0:T(8,128)S(1)}) custom-call(s32[64]{0:T(128)} %bitcast.16, s32[64]{0:T(128)} %bitcast.17, s32[64]{0:T(128)} %bitcast.18, s32[128,128]{1,0:T(8,128)} %mask.1, f32[1024,128]{1,0:T(8,128)} %bitcast.15, ...), custom_call_target="tpu_custom_call" | custom-call | flops 100000000 | bytes 8000000 | tf_op jit(solution)/shard_map/pallas_call | solution.py:149
  4.9 0.5 %collective-permute-start = (f32[1040,128]{1,0:T(8,128)S(1)}, f32[1040,128]{1,0:T(8,128)}, u32[]{:S(2)}, u32[]{:S(2)}) collective-permute-start(f32[1040,128]{1,0:T(8,128)S(1)} %get-tuple-element.13), channel_id=1, source_target_pairs={{0,16},{16,0},{1,17},{17,1},{2,18},{18,2},{3,19},{19,3},{4,20},{20... | collective-permute-start | bytes 1597448 | tf_op jit(solution)/shard_map/ppermute | solution.py:499
  5.5 2.6 %collective-permute-start.1 = (f32[136,128]{1,0:T(8,128)S(1)}, f32[136,128]{1,0:T(8,128)S(1)}, u32[]{:S(2)}, u32[]{:S(2)}) collective-permute-start(f32[136,128]{1,0:T(8,128)S(1)} %get-tuple-element.14), channel_id=1, source_target_pairs={{0,4},{4,8},{8,12},{12,0},{1,5},{5,9},{9,13},{13,1},{2,6},{6,10},{... | collective-permute-start | bytes 208904 | tf_op jit(solution)/shard_map/ppermute | solution.py:497
  8.1 2.1 %collective-permute-start.2 = (f32[136,128]{1,0:T(8,128)S(1)}, f32[136,128]{1,0:T(8,128)S(1)}, u32[]{:S(2)}, u32[]{:S(2)}) collective-permute-start(f32[136,128]{1,0:T(8,128)S(1)} %get-tuple-element.15), channel_id=1, source_target_pairs={{4,0},{8,4},{12,8},{0,12},{5,1},{9,5},{13,9},{1,13},{6,2},{10,6},{... | collective-permute-start | bytes 208904 | tf_op jit(solution)/shard_map/ppermute | solution.py:498
  10.2 0.0 collective-permute-done
  10.2 5.2 %all-to-all-start = ((f32[16,65,1,128]{3,2,1,0:T(1,128)}), f32[16,65,1,128]{3,2,1,0:T(1,128)S(1)}, u32[]{:S(2)}, u32[]{:S(2)}) async-start(f32[16,65,1,128]{3,2,1,0:T(1,128)} %bitcast.6), calls=%async_computation | async-start | bytes 1064960 | tf_op jit(solution)/shard_map/all_to_all | solution.py:502
  15.4 0.0 collective-permute-done.1.refs_0_.top
  15.4 0.0 collective-permute-done.2.refs_1_.bottom
  15.5 0.0 copy-start
  15.5 0.1 shard_map.88
  15.6 2.0 %collective-permute-start.3 = (f32[136,128]{1,0:T(8,128)S(1)}, f32[136,128]{1,0:T(8,128)S(1)}, u32[]{:S(2)}, u32[]{:S(2)}) collective-permute-start(f32[136,128]{1,0:T(8,128)S(1)} %get-tuple-element.16), channel_id=1, source_target_pairs={{0,1},{1,2},{2,3},{3,0},{4,5},{5,6},{6,7},{7,4},{8,9},{9,10},{10,1... | collective-permute-start | bytes 208904 | tf_op jit(solution)/shard_map/ppermute | solution.py:505
  17.6 1.0 %collective-permute-start.4 = (f32[136,128]{1,0:T(8,128)S(1)}, f32[136,128]{1,0:T(8,128)S(1)}, u32[]{:S(2)}, u32[]{:S(2)}) collective-permute-start(f32[136,128]{1,0:T(8,128)S(1)} %get-tuple-element.17), channel_id=1, source_target_pairs={{1,0},{2,1},{3,2},{0,3},{5,4},{6,5},{7,6},{4,7},{9,8},{10,9},{11,1... | collective-permute-start | bytes 208904 | tf_op jit(solution)/shard_map/ppermute | solution.py:506
  18.6 0.0 copy-done
  18.6 2.8 %shard_map.87.x = f32[64,128,128]{2,1,0:T(8,128)S(1)} custom-call(f32[528,128]{1,0:T(8,128)S(1)} %get-tuple-element.12.own, f32[64,128,128]{2,1,0:T(8,128)S(1)} %bitcast.11, f32[136,128]{1,0:T(8,128)S(1)} %collective-permute-done.1.refs_0_.top, f32[136,128]{1,0:T(8,128)S(1)} %collective-permute-done.2.refs_1_.bottom), custom_call_target="tpu_custom_call" | custom-call | flops 5000000000 | bytes 100000 | tf_op jit(solution)/shard_map/pallas_call | solution.py:401
  21.3 2.1 %collective-permute-done.3.west = f32[136,128]{1,0:T(8,128)S(1)} collective-permute-done((f32[136,128]{1,0:T(8,128)S(1)}, f32[136,128]{1,0:T(8,128)S(1)}, u32[]{:S(2)}, u32[]{:S(2)}) %collective-permute-start.3) | collective-permute-done | bytes 69664 | tf_op jit(solution)/shard_map/ppermute | solution.py:505
  23.4 1.2 %collective-permute-done.4.east = f32[136,128]{1,0:T(8,128)S(1)} collective-permute-done((f32[136,128]{1,0:T(8,128)S(1)}, f32[136,128]{1,0:T(8,128)S(1)}, u32[]{:S(2)}, u32[]{:S(2)}) %collective-permute-start.4) | collective-permute-done | bytes 69664 | tf_op jit(solution)/shard_map/ppermute | solution.py:506
  24.6 0.7 %shard_map.89.refs_0_ = f32[384,128]{1,0:T(8,128)S(1)} custom-call(f32[528,128]{1,0:T(8,128)S(1)} %get-tuple-element.12.own, f32[136,128]{1,0:T(8,128)S(1)} %collective-permute-done.1.refs_0_.top, f32[136,128]{1,0:T(8,128)S(1)} %collective-permute-done.2.refs_1_.bottom, f32[136,128]{1,0:T(8,128)S(1)} %collective-permute-done.3.west, ...), custom_call_target="tpu_custom_call" | custom-call | flops 1000000 | bytes 100000 | tf_op jit(solution)/shard_map/pallas_call | solution.py:295
  25.3 5.1 %shard_map.90 = (f32[64,128,128]{2,1,0:T(8,128)}, f32[128,128]{1,0:T(8,128)S(1)}) custom-call(f32[528,128]{1,0:T(8,128)S(1)} %get-tuple-element.12.own, f32[64,128,128]{2,1,0:T(8,128)S(1)} %shard_map.87.x, f32[384,128]{1,0:T(8,128)S(1)} %shard_map.89.refs_0_), custom_call_target="tpu_custom_call" | custom-call | flops 1000000 | bytes 100000 | tf_op jit(solution)/shard_map/pallas_call | solution.py:401
  30.4 0.6 %all-to-all-done = f32[16,65,1,128]{3,2,1,0:T(1,128)S(1)} async-done(((f32[16,65,1,128]{3,2,1,0:T(1,128)}), f32[16,65,1,128]{3,2,1,0:T(1,128)S(1)}, u32[]{:S(2)}, u32[]{:S(2)}) %all-to-all-start) | async-done | bytes 532512 | tf_op jit(solution)/shard_map/all_to_all | solution.py:502
  30.9 1.1 %shard_map.91 = (f32[64,128,128]{2,1,0:T(8,128)}, f32[8,128,128]{2,1,0:T(8,128)}) custom-call(f32[528,128]{1,0:T(8,128)S(1)} %get-tuple-element.12.own, f32[1040,128]{1,0:T(8,128)S(1)} %bitcast.12, f32[128,128]{1,0:T(8,128)S(1)} %get-tuple-element.18.surface, f32[64,128,128]{2,1,0:T(8,128)} %get-tuple-element.19.second), custom_call_target="tpu_custom_call", output_to_operand_aliasing={{0}: (3, {})} | custom-call | flops 100000000 | bytes 2000000 | tf_op jit(solution)/shard_map/pallas_call | solution.py:458
Async XLA Ops:
  4.9 5.3 %collective-permute-start = (f32[1040,128]{1,0:T(8,128)S(1)}, f32[1040,128]{1,0:T(8,128)}, u32[]{:S(2)}, u32[]{:S(2)}) collective-permute-start(f32[1040,128]{1,0:T(8,128)S(1)} %get-tuple-element.13), channel_id=1, source_target_pairs={{0,16},{16,0},{1,17},{17,1},{2,18},{18,2},{3,19},{19,3},{4,20},{20... | collective-permute-start | bytes 1597448 | tf_op jit(solution)/shard_map/ppermute | solution.py:499
  5.5 10.0 %collective-permute-start.1 = (f32[136,128]{1,0:T(8,128)S(1)}, f32[136,128]{1,0:T(8,128)S(1)}, u32[]{:S(2)}, u32[]{:S(2)}) collective-permute-start(f32[136,128]{1,0:T(8,128)S(1)} %get-tuple-element.14), channel_id=1, source_target_pairs={{0,4},{4,8},{8,12},{12,0},{1,5},{5,9},{9,13},{13,1},{2,6},{6,10},{... | collective-permute-start | bytes 208904 | tf_op jit(solution)/shard_map/ppermute | solution.py:497
  8.1 7.3 %collective-permute-start.2 = (f32[136,128]{1,0:T(8,128)S(1)}, f32[136,128]{1,0:T(8,128)S(1)}, u32[]{:S(2)}, u32[]{:S(2)}) collective-permute-start(f32[136,128]{1,0:T(8,128)S(1)} %get-tuple-element.15), channel_id=1, source_target_pairs={{4,0},{8,4},{12,8},{0,12},{5,1},{9,5},{13,9},{1,13},{6,2},{10,6},{... | collective-permute-start | bytes 208904 | tf_op jit(solution)/shard_map/ppermute | solution.py:498
  10.2 20.7 %all-to-all-start = ((f32[16,65,1,128]{3,2,1,0:T(1,128)}), f32[16,65,1,128]{3,2,1,0:T(1,128)S(1)}, u32[]{:S(2)}, u32[]{:S(2)}) async-start(f32[16,65,1,128]{3,2,1,0:T(1,128)} %bitcast.6), calls=%async_computation | async-start | bytes 1064960 | tf_op jit(solution)/shard_map/all_to_all | solution.py:502
  15.5 3.1 %copy-start = (f32[1,64,128,128]{3,2,1,0:T(8,128)S(1)}, f32[1,64,128,128]{3,2,1,0:T(8,128)}, u32[]{:S(2)}) copy-start(f32[1,64,128,128]{3,2,1,0:T(8,128)} %param.7) | copy-start | bytes 12582916
  15.6 7.8 %collective-permute-start.3 = (f32[136,128]{1,0:T(8,128)S(1)}, f32[136,128]{1,0:T(8,128)S(1)}, u32[]{:S(2)}, u32[]{:S(2)}) collective-permute-start(f32[136,128]{1,0:T(8,128)S(1)} %get-tuple-element.16), channel_id=1, source_target_pairs={{0,1},{1,2},{2,3},{3,0},{4,5},{5,6},{6,7},{7,4},{8,9},{9,10},{10,1... | collective-permute-start | bytes 208904 | tf_op jit(solution)/shard_map/ppermute | solution.py:505
  17.6 7.0 %collective-permute-start.4 = (f32[136,128]{1,0:T(8,128)S(1)}, f32[136,128]{1,0:T(8,128)S(1)}, u32[]{:S(2)}, u32[]{:S(2)}) collective-permute-start(f32[136,128]{1,0:T(8,128)S(1)} %get-tuple-element.17), channel_id=1, source_target_pairs={{1,0},{2,1},{3,2},{0,3},{5,4},{6,5},{7,6},{4,7},{9,8},{10,9},{11,1... | collective-permute-start | bytes 208904 | tf_op jit(solution)/shard_map/ppermute | solution.py:506

commit v7 on v6

--- a/solution.py
+++ b/solution.py
@@ -190,15 +190,18 @@
 PAD = 8
 
 
-def relay_kernel(own, top, bottom, to_west, to_east):
-    cx = to_west.shape[0] - 8
-    cy = to_west.shape[1]
+def relay_kernel(own, top, bottom, first, second):
+    cx = first.shape[0] - 8
+    cy = first.shape[1]
     lev = top.shape[0] // 2 - 4
     eye = lanes((lev, cy)) == lax.broadcasted_iota(jnp.int32, (lev, cy), 0)
-    for out, part, c in ((to_west, parts(lev, cx)[3], 0), (to_east, parts(lev, cx)[4], cy - 1)):
-        out[...] = own[part, :]
+    even = lax.rem(lax.axis_index("gy"), 2) == 0
+    west, east = (own[part, :] for part in parts(lev, cx)[3:])
+    first[...] = jnp.where(even, east, west)
+    second[...] = jnp.where(even, west, east)
+    for out, turn in ((first, even), (second, jnp.logical_not(even))):
         for i, msg in enumerate((top, bottom)):
-            column = msg[0:lev, c : c + 1]
+            column = jnp.where(turn, msg[0:lev, cy - 1 : cy], msg[0:lev, 0:1])
             row = jnp.sum(jnp.where(eye, column, 0.0), axis=0, keepdims=True)
             out[cx + 1 + i : cx + 2 + i, :] = row
 
@@ -216,8 +219,11 @@
     )(own, top, bottom)
 
 
-def ring_kernel(ngx, ngy, own, top, bottom, west, east, ring):
-    cx, cy = west.shape[0] - 8, west.shape[1]
+def ring_kernel(ngx, ngy, own, top, bottom, got_a, got_b, ring):
+    cx, cy = got_a.shape[0] - 8, got_a.shape[1]
+    even = lax.rem(lax.axis_index("gy"), 2) == 0
+    a, b = got_a[...], got_b[...]
+    west, east = jnp.where(even, b, a), jnp.where(even, a, b)
     lev = top.shape[0] // 2 - 4
     wet, up, down, left, right = (own.at[part] for part in parts(lev, cx))
     ocean = lax.axis_index("mp") == 1
@@ -501,9 +507,13 @@
     buckets = buckets.reshape(ndev, whole[0] // ndev, 1, whole[1])
     got = lax.all_to_all(buckets, ("gx", "gy"), split_axis=0, concat_axis=0, tiled=True)
     got = got.reshape(whole)
-    to_west, to_east = relay(own, top, bottom, cx)
-    west = lax.ppermute(to_east, "gy", ahead(ngy))
-    east = lax.ppermute(to_west, "gy", behind(ngy))
+    first, second = relay(own, top, bottom, cx)
+
+    def exchange(x, start):
+        other = lambda i: i + 1 if i % 2 == start else i - 1
+        return lax.ppermute(x, "gy", [(i, other(i) if 0 <= other(i) < ngy else i) for i in range(ngy)])
+
+    west, east = exchange(first, 0), exchange(second, 1)
     first = one_step(own, state, (top, bottom), ngx, False)
     ring = outer_ring(own, top, bottom, west, east, ngx, ngy)
     second, level = one_step(own, first, (ring,), ngx, True)

time: 32.2 us -> 32.2 us (level)
    all_to_all x1, waiting for transfers between devices: 0.55 us -> 3.89 us  [local(): lax.all_to_all(buckets, ('gx', 'gy'), split_axis=0, concat_axis=0, tiled=...]
    ppermute x2, waiting for transfers between devices: 3.27 us -> 0.19 us  [exchange(): lax.ppermute(x, 'gy', [(i, other(i) if 0 <= other(i) < ngy else i) for i...]
    ppermute x2, starting transfers between devices: 2.98 us -> 2.64 us  [exchange(): lax.ppermute(x, 'gy', [(i, other(i) if 0 <= other(i) < ngy else i) for i...]
  transfers between devices with their start and end apart: 6 -> 6, of which waited for: 3 -> 2; matrix products, arithmetic and copies ran while one was open for 0% -> 0% of each run, Pallas kernels for 27% -> 27%
where the time goes in v7:
time: 32.2 us; the launch traced here: 32 us
  Pallas kernels  14.1 us (44%)
  starting transfers between devices  13.1 us (41%)
  waiting for transfers between devices  4.09 us (13%)
  between operations  0.71 us (2%)
    pallas_call x2, Pallas kernels, one_step(): pl.pallas_call(functools.partial(step_kernel, ngx, group, second), out_sh...  7.85 us
    all_to_all x1, starting transfers between devices, local(): lax.all_to_all(buckets, ('gx', 'gy'), split_axis=0, concat_axis=0, tiled=...  5.19 us
    pallas_call x1, Pallas kernels, outgoing(): pl.pallas_call(functools.partial(send_kernel, ndev, ngy, chunk, group), o...  4.3 us
    all_to_all x1, waiting for transfers between devices, local(): lax.all_to_all(buckets, ('gx', 'gy'), split_axis=0, concat_axis=0, tiled=...  3.89 us
    ppermute x1, starting transfers between devices, local(): top = lax.ppermute(down, 'gx', ahead(ngx))  2.65 us
    ppermute x2, starting transfers between devices, exchange(): lax.ppermute(x, 'gy', [(i, other(i) if 0 <= other(i) < ngy else i) for i...  2.64 us
    ppermute x1, starting transfers between devices, local(): bottom = lax.ppermute(up, 'gx', behind(ngx))  2.11 us
    pallas_call x1, Pallas kernels, collect(): pl.pallas_call(functools.partial(collect_kernel, ndev), out_shape=(jax.Sh...  1.07 us
  transfers between devices with their start and end apart: 6, of which 2 were waited for; matrix products, arithmetic and copies ran while one was open for 0% of the time, Pallas kernels for 27%

profile of v7, /device:TPU:0, one launch (start us, length us, event | category | flops | bytes accessed | tf_op | source)
XLA Modules:
  0.0 32.0 jit_solution(14302674390872387348)
XLA Ops:
  0.6 4.3 %shard_map.86 = (f32[1040,128]{1,0:T(8,128)S(1)}, f32[136,128]{1,0:T(8,128)S(1)}, f32[136,128]{1,0:T(8,128)S(1)}, f32[528,128]{1,0:T(8,128)S(1)}) custom-call(s32[64]{0:T(128)} %bitcast.16, s32[64]{0:T(128)} %bitcast.17, s32[64]{0:T(128)} %bitcast.18, s32[128,128]{1,0:T(8,128)} %mask.1, f32[1024,128]{1,0:T(8,128)} %bitcast.15, ...), custom_call_target="tpu_custom_call" | custom-call | flops 100000000 | bytes 8000000 | tf_op jit(solution)/shard_map/pallas_call | solution.py:149
  4.9 0.5 %collective-permute-start = (f32[1040,128]{1,0:T(8,128)S(1)}, f32[1040,128]{1,0:T(8,128)}, u32[]{:S(2)}, u32[]{:S(2)}) collective-permute-start(f32[1040,128]{1,0:T(8,128)S(1)} %get-tuple-element.13), channel_id=1, source_target_pairs={{0,16},{16,0},{1,17},{17,1},{2,18},{18,2},{3,19},{19,3},{4,20},{20... | collective-permute-start | bytes 1597448 | tf_op jit(solution)/shard_map/ppermute | solution.py:505
  5.5 2.6 %collective-permute-start.1 = (f32[136,128]{1,0:T(8,128)S(1)}, f32[136,128]{1,0:T(8,128)S(1)}, u32[]{:S(2)}, u32[]{:S(2)}) collective-permute-start(f32[136,128]{1,0:T(8,128)S(1)} %get-tuple-element.14), channel_id=1, source_target_pairs={{0,4},{4,8},{8,12},{12,0},{1,5},{5,9},{9,13},{13,1},{2,6},{6,10},{... | collective-permute-start | bytes 208904 | tf_op jit(solution)/shard_map/ppermute | solution.py:503
  8.1 2.1 %collective-permute-start.2 = (f32[136,128]{1,0:T(8,128)S(1)}, f32[136,128]{1,0:T(8,128)S(1)}, u32[]{:S(2)}, u32[]{:S(2)}) collective-permute-start(f32[136,128]{1,0:T(8,128)S(1)} %get-tuple-element.15), channel_id=1, source_target_pairs={{4,0},{8,4},{12,8},{0,12},{5,1},{9,5},{13,9},{1,13},{6,2},{10,6},{... | collective-permute-start | bytes 208904 | tf_op jit(solution)/shard_map/ppermute | solution.py:504
  10.2 0.0 collective-permute-done
  10.2 5.2 %all-to-all-start = ((f32[16,65,1,128]{3,2,1,0:T(1,128)}), f32[16,65,1,128]{3,2,1,0:T(1,128)S(1)}, u32[]{:S(2)}, u32[]{:S(2)}) async-start(f32[16,65,1,128]{3,2,1,0:T(1,128)} %bitcast.6), calls=%async_computation | async-start | bytes 1064960 | tf_op jit(solution)/shard_map/all_to_all | solution.py:508
  15.4 0.0 collective-permute-done.1.refs_0_.top
  15.4 0.0 collective-permute-done.2.refs_1_.bottom
  15.4 0.0 copy-start
  15.5 0.2 shard_map.88
  15.6 2.0 %collective-permute-start.3 = (f32[136,128]{1,0:T(8,128)S(1)}, f32[136,128]{1,0:T(8,128)S(1)}, u32[]{:S(2)}, u32[]{:S(2)}) collective-permute-start(f32[136,128]{1,0:T(8,128)S(1)} %get-tuple-element.16), channel_id=1, source_target_pairs={{0,1},{1,0},{2,3},{3,2},{4,5},{5,4},{6,7},{7,6},{8,9},{9,8},{10,11... | collective-permute-start | bytes 208904 | tf_op jit(solution)/shard_map/ppermute | solution.py:514
  17.6 0.7 %collective-permute-start.4 = (f32[136,128]{1,0:T(8,128)S(1)}, f32[136,128]{1,0:T(8,128)S(1)}, u32[]{:S(2)}, u32[]{:S(2)}) collective-permute-start(f32[136,128]{1,0:T(8,128)S(1)} %get-tuple-element.17), channel_id=1, source_target_pairs={{0,0},{1,2},{2,1},{3,3},{4,4},{5,6},{6,5},{7,7},{8,8},{9,10},{10,9... | collective-permute-start | bytes 208904 | tf_op jit(solution)/shard_map/ppermute | solution.py:514
  18.3 0.0 copy-done
  18.3 2.8 %shard_map.87.x = f32[64,128,128]{2,1,0:T(8,128)S(1)} custom-call(f32[528,128]{1,0:T(8,128)S(1)} %get-tuple-element.12.own, f32[64,128,128]{2,1,0:T(8,128)S(1)} %bitcast.11, f32[136,128]{1,0:T(8,128)S(1)} %collective-permute-done.1.refs_0_.top, f32[136,128]{1,0:T(8,128)S(1)} %collective-permute-done.2.refs_1_.bottom), custom_call_target="tpu_custom_call" | custom-call | flops 5000000000 | bytes 100000 | tf_op jit(solution)/shard_map/pallas_call | solution.py:407
  21.1 0.2 collective-permute-done.3.got_a
  21.3 0.0 collective-permute-done.4.got_b
  21.3 0.7 %shard_map.89.refs_0_ = f32[384,128]{1,0:T(8,128)S(1)} custom-call(f32[528,128]{1,0:T(8,128)S(1)} %get-tuple-element.12.own, f32[136,128]{1,0:T(8,128)S(1)} %collective-permute-done.1.refs_0_.top, f32[136,128]{1,0:T(8,128)S(1)} %collective-permute-done.2.refs_1_.bottom, f32[136,128]{1,0:T(8,128)S(1)} %collective-permute-done.3.got_a, ...), custom_call_target="tpu_custom_call" | custom-call | flops 1000000 | bytes 100000 | tf_op jit(solution)/shard_map/pallas_call | solution.py:301
  21.9 5.1 %shard_map.90 = (f32[64,128,128]{2,1,0:T(8,128)}, f32[128,128]{1,0:T(8,128)S(1)}) custom-call(f32[528,128]{1,0:T(8,128)S(1)} %get-tuple-element.12.own, f32[64,128,128]{2,1,0:T(8,128)S(1)} %shard_map.87.x, f32[384,128]{1,0:T(8,128)S(1)} %shard_map.89.refs_0_), custom_call_target="tpu_custom_call" | custom-call | flops 1000000 | bytes 100000 | tf_op jit(solution)/shard_map/pallas_call | solution.py:407
  27.0 3.9 %all-to-all-done = f32[16,65,1,128]{3,2,1,0:T(1,128)S(1)} async-done(((f32[16,65,1,128]{3,2,1,0:T(1,128)}), f32[16,65,1,128]{3,2,1,0:T(1,128)S(1)}, u32[]{:S(2)}, u32[]{:S(2)}) %all-to-all-start) | async-done | bytes 532512 | tf_op jit(solution)/shard_map/all_to_all | solution.py:508
  30.9 1.1 %shard_map.91 = (f32[64,128,128]{2,1,0:T(8,128)}, f32[8,128,128]{2,1,0:T(8,128)}) custom-call(f32[528,128]{1,0:T(8,128)S(1)} %get-tuple-element.12.own, f32[1040,128]{1,0:T(8,128)S(1)} %bitcast.12, f32[128,128]{1,0:T(8,128)S(1)} %get-tuple-element.18.surface, f32[64,128,128]{2,1,0:T(8,128)} %get-tuple-element.19.second), custom_call_target="tpu_custom_call", output_to_operand_aliasing={{0}: (3, {})} | custom-call | flops 100000000 | bytes 2000000 | tf_op jit(solution)/shard_map/pallas_call | solution.py:464
Async XLA Ops:
  4.9 5.3 %collective-permute-start = (f32[1040,128]{1,0:T(8,128)S(1)}, f32[1040,128]{1,0:T(8,128)}, u32[]{:S(2)}, u32[]{:S(2)}) collective-permute-start(f32[1040,128]{1,0:T(8,128)S(1)} %get-tuple-element.13), channel_id=1, source_target_pairs={{0,16},{16,0},{1,17},{17,1},{2,18},{18,2},{3,19},{19,3},{4,20},{20... | collective-permute-start | bytes 1597448 | tf_op jit(solution)/shard_map/ppermute | solution.py:505
  5.5 10.0 %collective-permute-start.1 = (f32[136,128]{1,0:T(8,128)S(1)}, f32[136,128]{1,0:T(8,128)S(1)}, u32[]{:S(2)}, u32[]{:S(2)}) collective-permute-start(f32[136,128]{1,0:T(8,128)S(1)} %get-tuple-element.14), channel_id=1, source_target_pairs={{0,4},{4,8},{8,12},{12,0},{1,5},{5,9},{9,13},{13,1},{2,6},{6,10},{... | collective-permute-start | bytes 208904 | tf_op jit(solution)/shard_map/ppermute | solution.py:503
  8.1 7.3 %collective-permute-start.2 = (f32[136,128]{1,0:T(8,128)S(1)}, f32[136,128]{1,0:T(8,128)S(1)}, u32[]{:S(2)}, u32[]{:S(2)}) collective-permute-start(f32[136,128]{1,0:T(8,128)S(1)} %get-tuple-element.15), channel_id=1, source_target_pairs={{4,0},{8,4},{12,8},{0,12},{5,1},{9,5},{13,9},{1,13},{6,2},{10,6},{... | collective-permute-start | bytes 208904 | tf_op jit(solution)/shard_map/ppermute | solution.py:504
  10.2 20.7 %all-to-all-start = ((f32[16,65,1,128]{3,2,1,0:T(1,128)}), f32[16,65,1,128]{3,2,1,0:T(1,128)S(1)}, u32[]{:S(2)}, u32[]{:S(2)}) async-start(f32[16,65,1,128]{3,2,1,0:T(1,128)} %bitcast.6), calls=%async_computation | async-start | bytes 1064960 | tf_op jit(solution)/shard_map/all_to_all | solution.py:508
  15.4 2.9 %copy-start = (f32[1,64,128,128]{3,2,1,0:T(8,128)S(1)}, f32[1,64,128,128]{3,2,1,0:T(8,128)}, u32[]{:S(2)}) copy-start(f32[1,64,128,128]{3,2,1,0:T(8,128)} %param.7) | copy-start | bytes 12582916
  15.6 5.6 %collective-permute-start.3 = (f32[136,128]{1,0:T(8,128)S(1)}, f32[136,128]{1,0:T(8,128)S(1)}, u32[]{:S(2)}, u32[]{:S(2)}) collective-permute-start(f32[136,128]{1,0:T(8,128)S(1)} %get-tuple-element.16), channel_id=1, source_target_pairs={{0,1},{1,0},{2,3},{3,2},{4,5},{5,4},{6,7},{7,6},{8,9},{9,8},{10,11... | collective-permute-start | bytes 208904 | tf_op jit(solution)/shard_map/ppermute | solution.py:514
  17.6 3.6 %collective-permute-start.4 = (f32[136,128]{1,0:T(8,128)S(1)}, f32[136,128]{1,0:T(8,128)S(1)}, u32[]{:S(2)}, u32[]{:S(2)}) collective-permute-start(f32[136,128]{1,0:T(8,128)S(1)} %get-tuple-element.17), channel_id=1, source_target_pairs={{0,0},{1,2},{2,1},{3,3},{4,4},{5,6},{6,5},{7,7},{8,8},{9,10},{10,9... | collective-permute-start | bytes 208904 | tf_op jit(solution)/shard_map/ppermute | solution.py:514

commit v8 on v7

--- a/solution.py
+++ b/solution.py
@@ -429,7 +429,7 @@
     store = pltpu.make_async_copy(level, out.at[0], sems.at[0])
 
     def leave(i):
-        part = pl.ds(i * fields // 2, fields // 2)
+        part = pl.ds(i * (fields - 2), (fields - 2, 2)[i])
         return pltpu.make_async_copy(sums.at[part], received.at[part], rsems.at[i])
 
     labels = got[block - extra : block, :]
@@ -448,7 +448,7 @@
         sums[k] = jnp.dot(
             onehot[...], jnp.concatenate([high, low], axis=0), preferred_element_type=jnp.float32
         )
-        if k == fields // 2 - 1:
+        if k == fields - 3:
             leave(0).start()
         if k == 0:
             level[...] = surface[...] + FORCE * own[0:cx, :] * sums[0]
@@ -513,7 +513,8 @@
         other = lambda i: i + 1 if i % 2 == start else i - 1
         return lax.ppermute(x, "gy", [(i, other(i) if 0 <= other(i) < ngy else i) for i in range(ngy)])
 
-    west, east = exchange(first, 0), exchange(second, 1)
+    east = exchange(second, 1)
+    west = exchange(first, 0)
     first = one_step(own, state, (top, bottom), ngx, False)
     ring = outer_ring(own, top, bottom, west, east, ngx, ngy)
     second, level = one_step(own, first, (ring,), ngx, True)

time: 32.2 us -> 32.3 us (level)
  no operation moved by 1% of the time
where the time goes in v8:
time: 32.3 us; the launch traced here: 32 us
  Pallas kernels  14.1 us (44%)
  starting transfers between devices  13.1 us (41%)
  waiting for transfers between devices  4.08 us (13%)
  between operations  0.71 us (2%)
    pallas_call x2, Pallas kernels, one_step(): pl.pallas_call(functools.partial(step_kernel, ngx, group, second), out_sh...  7.86 us
    all_to_all x1, starting transfers between devices, local(): lax.all_to_all(buckets, ('gx', 'gy'), split_axis=0, concat_axis=0, tiled=...  5.2 us
    pallas_call x1, Pallas kernels, outgoing(): pl.pallas_call(functools.partial(send_kernel, ndev, ngy, chunk, group), o...  4.31 us
    all_to_all x1, waiting for transfers between devices, local(): lax.all_to_all(buckets, ('gx', 'gy'), split_axis=0, concat_axis=0, tiled=...  3.89 us
    ppermute x2, starting transfers between devices, exchange(): lax.ppermute(x, 'gy', [(i, other(i) if 0 <= other(i) < ngy else i) for i...  2.64 us
    ppermute x1, starting transfers between devices, local(): top = lax.ppermute(down, 'gx', ahead(ngx))  2.63 us
    ppermute x1, starting transfers between devices, local(): bottom = lax.ppermute(up, 'gx', behind(ngx))  2.11 us
    pallas_call x1, Pallas kernels, collect(): pl.pallas_call(functools.partial(collect_kernel, ndev), out_shape=(jax.Sh...  1.1 us
  transfers between devices with their start and end apart: 6, of which 2 were waited for; matrix products, arithmetic and copies ran while one was open for 0% of the time, Pallas kernels for 27%

profile of v8, /device:TPU:0, one launch (start us, length us, event | category | flops | bytes accessed | tf_op | source)
XLA Modules:
  0.0 32.0 jit_solution(12802598364118780153)
XLA Ops:
  0.6 4.3 %shard_map.86 = (f32[1040,128]{1,0:T(8,128)S(1)}, f32[136,128]{1,0:T(8,128)S(1)}, f32[136,128]{1,0:T(8,128)S(1)}, f32[528,128]{1,0:T(8,128)S(1)}) custom-call(s32[64]{0:T(128)} %bitcast.16, s32[64]{0:T(128)} %bitcast.17, s32[64]{0:T(128)} %bitcast.18, s32[128,128]{1,0:T(8,128)} %mask.1, f32[1024,128]{1,0:T(8,128)} %bitcast.15, ...), custom_call_target="tpu_custom_call" | custom-call | flops 100000000 | bytes 8000000 | tf_op jit(solution)/shard_map/pallas_call | solution.py:149
  5.0 0.5 %collective-permute-start = (f32[1040,128]{1,0:T(8,128)S(1)}, f32[1040,128]{1,0:T(8,128)}, u32[]{:S(2)}, u32[]{:S(2)}) collective-permute-start(f32[1040,128]{1,0:T(8,128)S(1)} %get-tuple-element.13), channel_id=1, source_target_pairs={{0,16},{16,0},{1,17},{17,1},{2,18},{18,2},{3,19},{19,3},{4,20},{20... | collective-permute-start | bytes 1597448 | tf_op jit(solution)/shard_map/ppermute | solution.py:505
  5.5 2.6 %collective-permute-start.1 = (f32[136,128]{1,0:T(8,128)S(1)}, f32[136,128]{1,0:T(8,128)S(1)}, u32[]{:S(2)}, u32[]{:S(2)}) collective-permute-start(f32[136,128]{1,0:T(8,128)S(1)} %get-tuple-element.14), channel_id=1, source_target_pairs={{0,4},{4,8},{8,12},{12,0},{1,5},{5,9},{9,13},{13,1},{2,6},{6,10},{... | collective-permute-start | bytes 208904 | tf_op jit(solution)/shard_map/ppermute | solution.py:503
  8.1 2.1 %collective-permute-start.2 = (f32[136,128]{1,0:T(8,128)S(1)}, f32[136,128]{1,0:T(8,128)S(1)}, u32[]{:S(2)}, u32[]{:S(2)}) collective-permute-start(f32[136,128]{1,0:T(8,128)S(1)} %get-tuple-element.15), channel_id=1, source_target_pairs={{4,0},{8,4},{12,8},{0,12},{5,1},{9,5},{13,9},{1,13},{6,2},{10,6},{... | collective-permute-start | bytes 208904 | tf_op jit(solution)/shard_map/ppermute | solution.py:504
  10.2 0.0 collective-permute-done
  10.2 5.2 %all-to-all-start = ((f32[16,65,1,128]{3,2,1,0:T(1,128)}), f32[16,65,1,128]{3,2,1,0:T(1,128)S(1)}, u32[]{:S(2)}, u32[]{:S(2)}) async-start(f32[16,65,1,128]{3,2,1,0:T(1,128)} %bitcast.6), calls=%async_computation | async-start | bytes 1064960 | tf_op jit(solution)/shard_map/all_to_all | solution.py:508
  15.4 0.0 collective-permute-done.1.refs_0_.top
  15.4 0.0 collective-permute-done.2.refs_1_.bottom
  15.4 0.0 copy-start
  15.5 0.2 shard_map.88
  15.6 2.0 %collective-permute-start.3 = (f32[136,128]{1,0:T(8,128)S(1)}, f32[136,128]{1,0:T(8,128)S(1)}, u32[]{:S(2)}, u32[]{:S(2)}) collective-permute-start(f32[136,128]{1,0:T(8,128)S(1)} %get-tuple-element.16), channel_id=1, source_target_pairs={{0,1},{1,0},{2,3},{3,2},{4,5},{5,4},{6,7},{7,6},{8,9},{9,8},{10,11... | collective-permute-start | bytes 208904 | tf_op jit(solution)/shard_map/ppermute | solution.py:514
  17.6 0.7 %collective-permute-start.4 = (f32[136,128]{1,0:T(8,128)S(1)}, f32[136,128]{1,0:T(8,128)S(1)}, u32[]{:S(2)}, u32[]{:S(2)}) collective-permute-start(f32[136,128]{1,0:T(8,128)S(1)} %get-tuple-element.17), channel_id=1, source_target_pairs={{0,0},{1,2},{2,1},{3,3},{4,4},{5,6},{6,5},{7,7},{8,8},{9,10},{10,9... | collective-permute-start | bytes 208904 | tf_op jit(solution)/shard_map/ppermute | solution.py:514
  18.3 0.0 copy-done
  18.3 2.8 %shard_map.87.x = f32[64,128,128]{2,1,0:T(8,128)S(1)} custom-call(f32[528,128]{1,0:T(8,128)S(1)} %get-tuple-element.12.own, f32[64,128,128]{2,1,0:T(8,128)S(1)} %bitcast.11, f32[136,128]{1,0:T(8,128)S(1)} %collective-permute-done.1.refs_0_.top, f32[136,128]{1,0:T(8,128)S(1)} %collective-permute-done.2.refs_1_.bottom), custom_call_target="tpu_custom_call" | custom-call | flops 5000000000 | bytes 100000 | tf_op jit(solution)/shard_map/pallas_call | solution.py:407
  21.1 0.2 collective-permute-done.3.got_a
  21.3 0.0 collective-permute-done.4.got_b
  21.3 0.7 %shard_map.89.refs_0_ = f32[384,128]{1,0:T(8,128)S(1)} custom-call(f32[528,128]{1,0:T(8,128)S(1)} %get-tuple-element.12.own, f32[136,128]{1,0:T(8,128)S(1)} %collective-permute-done.1.refs_0_.top, f32[136,128]{1,0:T(8,128)S(1)} %collective-permute-done.2.refs_1_.bottom, f32[136,128]{1,0:T(8,128)S(1)} %collective-permute-done.3.got_a, ...), custom_call_target="tpu_custom_call" | custom-call | flops 1000000 | bytes 100000 | tf_op jit(solution)/shard_map/pallas_call | solution.py:301
  21.9 5.1 %shard_map.90 = (f32[64,128,128]{2,1,0:T(8,128)}, f32[128,128]{1,0:T(8,128)S(1)}) custom-call(f32[528,128]{1,0:T(8,128)S(1)} %get-tuple-element.12.own, f32[64,128,128]{2,1,0:T(8,128)S(1)} %shard_map.87.x, f32[384,128]{1,0:T(8,128)S(1)} %shard_map.89.refs_0_), custom_call_target="tpu_custom_call" | custom-call | flops 1000000 | bytes 100000 | tf_op jit(solution)/shard_map/pallas_call | solution.py:407
  27.0 3.9 %all-to-all-done = f32[16,65,1,128]{3,2,1,0:T(1,128)S(1)} async-done(((f32[16,65,1,128]{3,2,1,0:T(1,128)}), f32[16,65,1,128]{3,2,1,0:T(1,128)S(1)}, u32[]{:S(2)}, u32[]{:S(2)}) %all-to-all-start) | async-done | bytes 532512 | tf_op jit(solution)/shard_map/all_to_all | solution.py:508
  30.9 1.1 %shard_map.91 = (f32[64,128,128]{2,1,0:T(8,128)}, f32[8,128,128]{2,1,0:T(8,128)}) custom-call(f32[528,128]{1,0:T(8,128)S(1)} %get-tuple-element.12.own, f32[1040,128]{1,0:T(8,128)S(1)} %bitcast.12, f32[128,128]{1,0:T(8,128)S(1)} %get-tuple-element.18.surface, f32[64,128,128]{2,1,0:T(8,128)} %get-tuple-element.19.second), custom_call_target="tpu_custom_call", output_to_operand_aliasing={{0}: (3, {})} | custom-call | flops 100000000 | bytes 2000000 | tf_op jit(solution)/shard_map/pallas_call | solution.py:464
Async XLA Ops:
  5.0 5.3 %collective-permute-start = (f32[1040,128]{1,0:T(8,128)S(1)}, f32[1040,128]{1,0:T(8,128)}, u32[]{:S(2)}, u32[]{:S(2)}) collective-permute-start(f32[1040,128]{1,0:T(8,128)S(1)} %get-tuple-element.13), channel_id=1, source_target_pairs={{0,16},{16,0},{1,17},{17,1},{2,18},{18,2},{3,19},{19,3},{4,20},{20... | collective-permute-start | bytes 1597448 | tf_op jit(solution)/shard_map/ppermute | solution.py:505
  5.5 10.0 %collective-permute-start.1 = (f32[136,128]{1,0:T(8,128)S(1)}, f32[136,128]{1,0:T(8,128)S(1)}, u32[]{:S(2)}, u32[]{:S(2)}) collective-permute-start(f32[136,128]{1,0:T(8,128)S(1)} %get-tuple-element.14), channel_id=1, source_target_pairs={{0,4},{4,8},{8,12},{12,0},{1,5},{5,9},{9,13},{13,1},{2,6},{6,10},{... | collective-permute-start | bytes 208904 | tf_op jit(solution)/shard_map/ppermute | solution.py:503
  8.1 7.3 %collective-permute-start.2 = (f32[136,128]{1,0:T(8,128)S(1)}, f32[136,128]{1,0:T(8,128)S(1)}, u32[]{:S(2)}, u32[]{:S(2)}) collective-permute-start(f32[136,128]{1,0:T(8,128)S(1)} %get-tuple-element.15), channel_id=1, source_target_pairs={{4,0},{8,4},{12,8},{0,12},{5,1},{9,5},{13,9},{1,13},{6,2},{10,6},{... | collective-permute-start | bytes 208904 | tf_op jit(solution)/shard_map/ppermute | solution.py:504
  10.2 20.7 %all-to-all-start = ((f32[16,65,1,128]{3,2,1,0:T(1,128)}), f32[16,65,1,128]{3,2,1,0:T(1,128)S(1)}, u32[]{:S(2)}, u32[]{:S(2)}) async-start(f32[16,65,1,128]{3,2,1,0:T(1,128)} %bitcast.6), calls=%async_computation | async-start | bytes 1064960 | tf_op jit(solution)/shard_map/all_to_all | solution.py:508
  15.4 2.9 %copy-start = (f32[1,64,128,128]{3,2,1,0:T(8,128)S(1)}, f32[1,64,128,128]{3,2,1,0:T(8,128)}, u32[]{:S(2)}) copy-start(f32[1,64,128,128]{3,2,1,0:T(8,128)} %param.7) | copy-start | bytes 12582916
  15.6 5.6 %collective-permute-start.3 = (f32[136,128]{1,0:T(8,128)S(1)}, f32[136,128]{1,0:T(8,128)S(1)}, u32[]{:S(2)}, u32[]{:S(2)}) collective-permute-start(f32[136,128]{1,0:T(8,128)S(1)} %get-tuple-element.16), channel_id=1, source_target_pairs={{0,1},{1,0},{2,3},{3,2},{4,5},{5,4},{6,7},{7,6},{8,9},{9,8},{10,11... | collective-permute-start | bytes 208904 | tf_op jit(solution)/shard_map/ppermute | solution.py:514
  17.6 3.6 %collective-permute-start.4 = (f32[136,128]{1,0:T(8,128)S(1)}, f32[136,128]{1,0:T(8,128)S(1)}, u32[]{:S(2)}, u32[]{:S(2)}) collective-permute-start(f32[136,128]{1,0:T(8,128)S(1)} %get-tuple-element.17), channel_id=1, source_target_pairs={{0,0},{1,2},{2,1},{3,3},{4,4},{5,6},{6,5},{7,7},{8,8},{9,10},{10,9... | collective-permute-start | bytes 208904 | tf_op jit(solution)/shard_map/ppermute | solution.py:514
